TPU v7x, 32 devices: a whole 2x2x4 slice. The times are simulated.
32 devices in a mesh: seq: 8 (over y, x, core), fsdp: 4 (over z).
Axes of the slice: x: 2, y: 2, z: 4, core: 2. Of those that a mesh axis runs over, the one named last changes fastest.
Arguments:
- tokens: bfloat16 [4, 4096, 1536], P('fsdp', 'seq'), may hold values from -6 to 6
- cotangent: bfloat16 [4, 4096, 1536], P('fsdp', 'seq'), may hold values from -6 to 6
- arrival_order: int32 [4, 4096], P('fsdp', 'seq'), may hold values from 0 to 4095, as said below
- lengths: int32 [4, 4], P('fsdp'), may hold values from 1 to 3840, 4096 in all within a row
- norm_gain: bfloat16 [1536], P('fsdp'), may hold values from 0.5 to 1.5
- w_query: bfloat16 [1536, 1536], P('fsdp'), may hold values from -0.15625 to 0.15625
- w_kv: bfloat16 [1536, 384], P('fsdp'), may hold values from -0.15625 to 0.15625
- w_out: bfloat16 [1536, 1536], P('fsdp'), may hold values from -1.25 to 1.25
- ffn_gain: bfloat16 [1536], P('fsdp'), may hold values from 0.5 to 1.5
- w_gate_up: bfloat16 [1536, 9216], P('fsdp'), may hold values from -0.15625 to 0.15625
- w_down: bfloat16 [4608, 1536], P('fsdp'), may hold values from -0.09375 to 0.09375
Outputs:
- block_out: bfloat16 [4, 4096, 1536], P('fsdp', 'seq')
- grad_tokens: bfloat16 [4, 4096, 1536], P('fsdp', 'seq')
- grad_norm_gain: float32 [1536], P('fsdp')
- grad_w_query: float32 [1536, 1536], P('fsdp')
- grad_w_kv: float32 [1536, 384], P('fsdp')
- grad_w_out: float32 [1536, 1536], P('fsdp')
- grad_ffn_gain: float32 [1536], P('fsdp')
- grad_w_gate_up: float32 [1536, 9216], P('fsdp')
- grad_w_down: float32 [4608, 1536], P('fsdp')
Inputs may be any that keep to these rules, and one draw needn't show every extreme that they name: `arrival_order`: in each group the entries are a permutation of the packed places. Of the 512 rows that one index of seq holds, exactly 128 have packed places on each of half the indices of seq (places s * 512 to (s + 1) * 512 - 1 belong to index s) and none on the others. Each group's 4 lengths sum to 4096, and one of them is 3840.
All inputs are finite; a program needn't handle non-finite values.
Results may differ from a plain program's by a relative error of at most 0.02.
Values may be sent and summed in bfloat16 or wider, within the bound.
No kernel may reach another device: no remote copies, remote signals or barrier semaphores. Data moves between devices by JAX's collectives and lax.ppermute only.
A program may use at most 320 MiB of HBM per device.

v0:
```python
import jax
import jax.numpy as jnp
from jax import lax
from jax.sharding import PartitionSpec as P

HD = 192
FF = 4608
WINDOW = 1024


EPSILON = 1e-06
ROPE_BASE = 10000.0
MASKED = -1e30


def passed_along(x, axis, by):
    length = lax.axis_size(axis)
    pairs = [(i, i + by) for i in range(length) if 0 <= i + by < length]
    return lax.ppermute(x, axis, pairs)


def rms_scale(values, gain):
    return values * lax.rsqrt(jnp.mean(values * values, axis=-1, keepdims=True) + EPSILON) * gain


def rotate(heads, cosine, sine):
    half = heads.shape[-1] // 2
    first_half = heads[..., :half]
    second_half = heads[..., half:]
    return jnp.concatenate(
        [first_half * cosine - second_half * sine, second_half * cosine + first_half * sine],
        axis=-1,
    )


def unrotate(heads, cosine, sine):
    half = heads.shape[-1] // 2
    first_half = heads[..., :half]
    second_half = heads[..., half:]
    return jnp.concatenate(
        [first_half * cosine + second_half * sine, second_half * cosine - first_half * sine],
        axis=-1,
    )


def angles(places, head_width):
    steps_half = jnp.arange(head_width // 2, dtype=jnp.float32)
    inverse = ROPE_BASE ** (-2.0 * steps_half / head_width)
    theta = places[:, None] * inverse[None, :]
    return (jnp.cos(theta), jnp.sin(theta))


def layout(lengths, places):
    ends = jnp.cumsum(lengths)
    starts = ends - lengths
    inside = (places[:, None] >= starts[None, :]) & (places[:, None] < ends[None, :])
    numbers = jnp.arange(1, lengths.shape[0] + 1, dtype=jnp.int32)
    document = jnp.sum(jnp.where(inside, numbers[None, :], 0), axis=1) - 1
    offset = places - jnp.sum(jnp.where(inside, starts[None, :], 0), axis=1)
    return (document, offset)


def gelu_product(gate_up):
    return jax.nn.gelu(gate_up[:, :FF], approximate=True) * gate_up[:, FF:]


def body(
    tokens,
    cotangent,
    arrival_order,
    lengths,
    norm_gain,
    w_query,
    w_kv,
    w_out,
    ffn_gain,
    w_gate_up,
    w_down,
):
    row_count = tokens.shape[1]
    model_width = tokens.shape[2]
    head_count = model_width // HD
    ranks = lax.axis_size("seq")
    capacity = 2 * row_count // ranks
    reach = WINDOW // row_count
    position = lax.axis_index("seq")
    arrived_at = arrival_order[0]
    owner = arrived_at // row_count
    owner_hits = (owner[:, None] == jnp.arange(ranks, dtype=jnp.int32)[None, :]).astype(jnp.int32)
    within = jnp.sum(jnp.cumsum(owner_hits, axis=0) * owner_hits, axis=1) - 1
    send_slot = owner * capacity + within

    def to_slots(source_rows):
        return (
            jnp.zeros((ranks * capacity, model_width), source_rows.dtype)
            .at[send_slot]
            .set(source_rows)
            .reshape(ranks, capacity, model_width)
        )

    slot_place = (
        jnp.full((ranks * capacity,), -1, jnp.int32)
        .at[send_slot]
        .set(arrived_at % row_count)
        .reshape(ranks, capacity)
    )
    got_tokens, got_cotangent, got_place = (
        lax.all_to_all(to_slots(tokens[0]), "seq", split_axis=0, concat_axis=0, tiled=True),
        lax.all_to_all(to_slots(cotangent[0]), "seq", split_axis=0, concat_axis=0, tiled=True),
        lax.all_to_all(slot_place, "seq", split_axis=0, concat_axis=0, tiled=True),
    )
    recv_place = got_place.reshape(ranks * capacity)
    is_live = recv_place >= 0
    landing = jnp.where(is_live, recv_place, row_count)
    safe_place = jnp.where(is_live, recv_place, 0)

    def from_slots(slot_rows):
        return (
            jnp.zeros((row_count, model_width), slot_rows.dtype)
            .at[landing]
            .set(slot_rows.reshape(ranks * capacity, model_width), mode="drop")
        )

    def to_owner(local_rows):
        return jnp.where(
            is_live[:, None], local_rows[safe_place], jnp.zeros((), local_rows.dtype)
        ).reshape(ranks, capacity, model_width)

    packed = from_slots(got_tokens)
    packed_grad = from_slots(got_cotangent)
    gain_attn, query_w, kv_w, out_w, gain_ffn, gate_up_w, down_w = (
        lax.all_gather(norm_gain, "fsdp", axis=0, tiled=True),
        lax.all_gather(w_query, "fsdp", axis=0, tiled=True),
        lax.all_gather(w_kv, "fsdp", axis=0, tiled=True),
        lax.all_gather(w_out, "fsdp", axis=0, tiled=True),
        lax.all_gather(ffn_gain, "fsdp", axis=0, tiled=True),
        lax.all_gather(w_gate_up, "fsdp", axis=0, tiled=True),
        lax.all_gather(w_down, "fsdp", axis=0, tiled=True),
    )
    places = position * row_count + jnp.arange(row_count, dtype=jnp.int32)
    doc_query, offset_query = layout(lengths[0], places)
    key_places = (
        position * row_count
        - reach * row_count
        + jnp.arange((reach + 1) * row_count, dtype=jnp.int32)
    )
    doc_key, unused_offset = layout(lengths[0], key_places)
    gap = places[:, None] - key_places[None, :]
    allowed = (
        (doc_query[:, None] == doc_key[None, :])
        & (doc_key[None, :] >= 0)
        & (gap >= 0)
        & (gap < WINDOW)
    )
    cosine, sine = angles(offset_query.astype(jnp.float32), HD)
    packed_f = packed.astype(jnp.float32)
    normed = rms_scale(packed_f, gain_attn.astype(jnp.float32)).astype(jnp.bfloat16)
    query_lin = jnp.dot(normed, query_w, preferred_element_type=jnp.float32)
    kv_lin = jnp.dot(normed, kv_w, preferred_element_type=jnp.float32)
    queries = (
        rotate(query_lin.reshape(row_count, head_count, HD), cosine[:, None, :], sine[:, None, :])
        * HD ** (-0.5)
    ).astype(jnp.bfloat16)
    own_keys = rotate(kv_lin[:, :HD], cosine, sine).astype(jnp.bfloat16)
    own_values = kv_lin[:, HD:].astype(jnp.bfloat16)
    own_pair = jnp.concatenate([own_keys, own_values], axis=1)
    earlier = []
    for distance in range(reach, 0, -1):
        earlier.append(passed_along(own_pair, "seq", distance))
    pair_rows = jnp.concatenate(earlier + [own_pair], axis=0)
    keys_all = pair_rows[:, :HD]
    values_all = pair_rows[:, HD:]

    def masked_scores():
        raw = jnp.einsum("qhd,kd->hqk", queries, keys_all, preferred_element_type=jnp.float32)
        return jnp.where(allowed[None], raw, MASKED)

    scores = masked_scores()
    top_score = jnp.max(scores, axis=-1, keepdims=True)
    log_total = top_score + jnp.log(jnp.sum(jnp.exp(scores - top_score), axis=-1, keepdims=True))
    probs_low = jnp.exp(scores - log_total).astype(jnp.bfloat16)
    mixed = (
        jnp.einsum("hqk,kd->qhd", probs_low, values_all, preferred_element_type=jnp.float32)
        .reshape(row_count, model_width)
        .astype(jnp.bfloat16)
    )
    hidden_state = packed_f + jnp.dot(mixed, out_w, preferred_element_type=jnp.float32)
    ffn_in = rms_scale(hidden_state, gain_ffn.astype(jnp.float32)).astype(jnp.bfloat16)
    gate_up = jnp.dot(ffn_in, gate_up_w, preferred_element_type=jnp.float32)
    activated = gelu_product(gate_up).astype(jnp.bfloat16)
    block_rows = (
        hidden_state + jnp.dot(activated, down_w, preferred_element_type=jnp.float32)
    ).astype(jnp.bfloat16)
    gain_attn, query_w, kv_w, out_w, gain_ffn, gate_up_w, down_w = (
        lax.all_gather(norm_gain, "fsdp", axis=0, tiled=True),
        lax.all_gather(w_query, "fsdp", axis=0, tiled=True),
        lax.all_gather(w_kv, "fsdp", axis=0, tiled=True),
        lax.all_gather(w_out, "fsdp", axis=0, tiled=True),
        lax.all_gather(ffn_gain, "fsdp", axis=0, tiled=True),
        lax.all_gather(w_gate_up, "fsdp", axis=0, tiled=True),
        lax.all_gather(w_down, "fsdp", axis=0, tiled=True),
    )
    grad_down = jnp.einsum("tf,td->fd", activated, packed_grad, preferred_element_type=jnp.float32)
    d_activated = jnp.einsum("td,fd->tf", packed_grad, down_w, preferred_element_type=jnp.float32)
    unused_product, glu_pull = jax.vjp(gelu_product, gate_up)
    d_gate_up = glu_pull(d_activated)[0].astype(jnp.bfloat16)
    grad_gate_up = jnp.einsum("td,tf->df", ffn_in, d_gate_up, preferred_element_type=jnp.float32)
    d_ffn_in = jnp.einsum("tf,df->td", d_gate_up, gate_up_w, preferred_element_type=jnp.float32)
    unused_scaled, ffn_norm_pull = jax.vjp(rms_scale, hidden_state, gain_ffn.astype(jnp.float32))
    d_hidden_norm, grad_gain_ffn = ffn_norm_pull(d_ffn_in)
    d_hidden = packed_grad.astype(jnp.float32) + d_hidden_norm
    d_branch = d_hidden.astype(jnp.bfloat16)
    grad_out = jnp.einsum("te,td->ed", mixed, d_branch, preferred_element_type=jnp.float32)
    d_mixed = (
        jnp.einsum("td,ed->te", d_branch, out_w, preferred_element_type=jnp.float32)
        .astype(jnp.bfloat16)
        .reshape(row_count, head_count, HD)
    )
    probs = jnp.exp(masked_scores() - log_total)
    d_probs = jnp.einsum("qhd,kd->hqk", d_mixed, values_all, preferred_element_type=jnp.float32)
    weighted = jnp.sum(probs * d_probs, axis=-1, keepdims=True)
    d_scores = (probs * (d_probs - weighted)).astype(jnp.bfloat16)
    d_queries = jnp.einsum("hqk,kd->qhd", d_scores, keys_all, preferred_element_type=jnp.float32)
    d_keys = jnp.einsum("hqk,qhd->kd", d_scores, queries, preferred_element_type=jnp.float32)
    d_values = jnp.einsum(
        "hqk,qhd->kd", probs.astype(jnp.bfloat16), d_mixed, preferred_element_type=jnp.float32
    )
    d_pairs = jnp.concatenate([d_keys, d_values], axis=1)
    d_own = d_pairs[reach * row_count :]
    for distance in range(reach, 0, -1):
        start_row = (reach - distance) * row_count
        d_own = d_own + passed_along(
            d_pairs[start_row : start_row + row_count].astype(jnp.bfloat16), "seq", -distance
        ).astype(jnp.float32)
    d_kv_lin = jnp.concatenate(
        [unrotate(d_own[:, :HD], cosine, sine), d_own[:, HD:]], axis=1
    ).astype(jnp.bfloat16)
    d_query_lin = (
        (unrotate(d_queries, cosine[:, None, :], sine[:, None, :]) * HD ** (-0.5))
        .reshape(row_count, model_width)
        .astype(jnp.bfloat16)
    )
    grad_query = jnp.einsum("te,tf->ef", normed, d_query_lin, preferred_element_type=jnp.float32)
    grad_kv = jnp.einsum("te,tf->ef", normed, d_kv_lin, preferred_element_type=jnp.float32)
    d_normed = jnp.einsum(
        "tf,ef->te", d_query_lin, query_w, preferred_element_type=jnp.float32
    ) + jnp.einsum("tf,ef->te", d_kv_lin, kv_w, preferred_element_type=jnp.float32)
    unused_normed, attn_norm_pull = jax.vjp(rms_scale, packed_f, gain_attn.astype(jnp.float32))
    d_packed_norm, grad_gain_attn = attn_norm_pull(d_normed)
    grad_rows = (d_hidden + d_packed_norm).astype(jnp.bfloat16)
    home_out, home_grad = (
        lax.all_to_all(to_owner(block_rows), "seq", split_axis=0, concat_axis=0, tiled=True),
        lax.all_to_all(to_owner(grad_rows), "seq", split_axis=0, concat_axis=0, tiled=True),
    )
    block_arrived = home_out.reshape(ranks * capacity, model_width)[send_slot]
    grad_arrived = home_grad.reshape(ranks * capacity, model_width)[send_slot]
    share_gain_attn, share_query, share_kv, share_out, share_gain_ffn, share_gate_up, share_down = (
        lax.psum_scatter(
            grad_gain_attn.astype(jnp.bfloat16), "fsdp", scatter_dimension=0, tiled=True
        ).astype(jnp.float32),
        lax.psum_scatter(
            grad_query.astype(jnp.bfloat16), "fsdp", scatter_dimension=0, tiled=True
        ).astype(jnp.float32),
        lax.psum_scatter(
            grad_kv.astype(jnp.bfloat16), "fsdp", scatter_dimension=0, tiled=True
        ).astype(jnp.float32),
        lax.psum_scatter(
            grad_out.astype(jnp.bfloat16), "fsdp", scatter_dimension=0, tiled=True
        ).astype(jnp.float32),
        lax.psum_scatter(
            grad_gain_ffn.astype(jnp.bfloat16), "fsdp", scatter_dimension=0, tiled=True
        ).astype(jnp.float32),
        lax.psum_scatter(
            grad_gate_up.astype(jnp.bfloat16), "fsdp", scatter_dimension=0, tiled=True
        ).astype(jnp.float32),
        lax.psum_scatter(
            grad_down.astype(jnp.bfloat16), "fsdp", scatter_dimension=0, tiled=True
        ).astype(jnp.float32),
    )
    total_gain_attn, total_query, total_kv, total_out, total_gain_ffn, total_gate_up, total_down = (
        lax.psum(share_gain_attn.astype(jnp.bfloat16), "seq").astype(jnp.float32),
        lax.psum(share_query.astype(jnp.bfloat16), "seq").astype(jnp.float32),
        lax.psum(share_kv.astype(jnp.bfloat16), "seq").astype(jnp.float32),
        lax.psum(share_out.astype(jnp.bfloat16), "seq").astype(jnp.float32),
        lax.psum(share_gain_ffn.astype(jnp.bfloat16), "seq").astype(jnp.float32),
        lax.psum(share_gate_up.astype(jnp.bfloat16), "seq").astype(jnp.float32),
        lax.psum(share_down.astype(jnp.bfloat16), "seq").astype(jnp.float32),
    )
    return (
        block_arrived[None],
        grad_arrived[None],
        total_gain_attn,
        total_query,
        total_kv,
        total_out,
        total_gain_ffn,
        total_gate_up,
        total_down,
    )


def solution(mesh):
    placed = (
        P("fsdp", "seq", None),
        P("fsdp", "seq", None),
        P("fsdp", "seq"),
        P("fsdp", None),
        P("fsdp"),
        P("fsdp", None),
        P("fsdp", None),
        P("fsdp", None),
        P("fsdp"),
        P("fsdp", None),
        P("fsdp", None),
    )
    return jax.shard_map(
        body,
        mesh=mesh,
        in_specs=placed,
        out_specs=(
            P("fsdp", "seq", None),
            P("fsdp", "seq", None),
            P("fsdp"),
            P("fsdp", None),
            P("fsdp", None),
            P("fsdp", None),
            P("fsdp"),
            P("fsdp", None),
            P("fsdp", None),
        ),
        check_vma=False,
    )
```

profile of v0, /device:TPU:0, one launch (start us, length us, event | category | flops | bytes accessed | tf_op | source)
XLA Modules:
  0.0 2260.2 jit_solution(13109601046858253837)
XLA Ops:
  35.5 12.1 all-gather.1
  95.4 15.0 all-to-all-done.3
  120.4 12.5 all-gather.10.cloned.1.call-done
  160.3 12.2 convolution_convert_fusion.6
  172.5 50.0 %all-gather.12.cloned.1.call-done = bf16[1536,1536]{1,0:T(8,128)(2,1)} async-done(((bf16[384,1536]{1,0:T(8,128)(2,1)}), bf16[1536,1536]{1,0:T(8,128)(2,1)}) %all-gather.12.cloned.1.call-update) | async-done | bytes 4718608 | tf_op jit(solution)/shard_map/all_gather | solution.py:135
  229.8 468.7 %all-gather.14.cloned.1.call-done = bf16[1536,9216]{1,0:T(8,128)(2,1)} async-done(((bf16[384,9216]{1,0:T(8,128)(2,1)}), bf16[1536,9216]{1,0:T(8,128)(2,1)}) %all-gather.14.cloned.1.call-update) | async-done | bytes 28311568 | tf_op jit(solution)/shard_map/all_gather | solution.py:137
  698.5 25.5 %fusion.85 = f32[512,9216]{1,0:T(8,128)} fusion(bf16[1536,9216]{1,0:T(8,128)(2,1)} %all-gather.14.cloned.1.call-done, f32[512,1536]{1,0:T(8,128)} %get-tuple-element.50, f32[1536]{0:T(1024)S(1)} %copy-done.29, f32[512]{0:T(512)S(1)} %fusion.73), kind=kOutput, calls=%fused_computation.195 | convolution fusion | flops 14497873920 | bytes 50339840 | tf_op jit(solution)/shard_map/dot_general | solution.py:189
  724.0 218.1 %all-gather.16.cloned.1.call-done = bf16[4608,1536]{1,0:T(8,128)(2,1)} async-done(((bf16[1152,1536]{1,0:T(8,128)(2,1)}), bf16[4608,1536]{1,0:T(8,128)(2,1)}) %all-gather.16.cloned.1.call-update) | async-done | bytes 14155792 | tf_op jit(solution)/shard_map/all_gather | solution.py:138
  942.1 25.3 %fusion.13 = (f32[512,4608]{1,0:T(8,128)}, f32[512,4608]{1,0:T(8,128)}, bf16[512,4608]{1,0:T(8,128)(2,1)}) fusion(f32[512,9216]{1,0:T(8,128)} %fusion.85, bf16[512,1536]{1,0:T(8,128)(2,1)S(1)} %copy-done.6, bf16[4608,1536]{1,0:T(8,128)(2,1)} %all-gather.16.cloned.1.call-done), kind=kOutput, calls=%fused_computation.46 | convolution fusion | flops 7304380416 | bytes 58195968 | tf_op jit(solution)/shard_map/td,fd->tf/dot_general | solution.py:204
  967.4 24.9 %multiply_reduce_fusion = (bf16[1536]{0:T(1024)(128)(2,1)}, f32[512]{0:T(512)S(1)}, f32[512,1536]{1,0:T(8,128)}) fusion(f32[512,1536]{1,0:T(8,128)} %get-tuple-element.50, f32[512]{0:T(512)S(1)} %fusion.73, f32[1536]{0:T(1024)S(1)} %copy-done.29, bf16[1536,9216]{1,0:T(8,128)(2,1)} %all-gather.14.cloned.1.call-done, f32[512,4608]{1,0:T(8,128)} %get-tuple-element.25, ...), kind=kOutput, calls=%fused_computation.59 | convolution fusion | flops 14509668352 | bytes 53490688 | tf_op jit(solution)/shard_map/tf,df->td/dot_general | solution.py:208
  1005.4 12.6 convolution_bitcast_fusion
  1018.0 16.2 fusion
  1034.2 17.8 fusion.2
  1095.7 12.5 convolution_convert_fusion.1
  1108.9 24.2 %convolution_convert_fusion = bf16[1536,9216]{1,0:T(8,128)(2,1)} fusion(f32[512,4608]{1,0:T(8,128)} %get-tuple-element.25, f32[512,4608]{1,0:T(8,128)} %get-tuple-element.24, f32[512,1536]{1,0:T(8,128)} %get-tuple-element.50, f32[1536]{0:T(1024)S(1)} %copy-done.29, f32[512]{0:T(512)S(1)} %copy-done.46), kind=kOutput, calls=%fused_computation.9 | convolution fusion | flops 14521466880 | bytes 50339840 | tf_op jit(solution)/shard_map/td,tf->df/dot_general | solution.py:207
  1134.4 13.0 fusion.25
  1162.0 29.1 %reduce-scatter.10.cloned.1.call-done = bf16[384,1536]{1,0:T(8,128)(2,1)} async-done(((bf16[1536,1536]{1,0:T(8,128)(2,1)}), bf16[384,1536]{1,0:T(8,128)(2,1)}) %reduce-scatter.10.cloned.1.call-update) | async-done | bytes 1179664 | tf_op jit(solution)/shard_map/reduce_scatter | solution.py:267
  1191.1 88.1 %reduce-scatter.6.cloned.1.call-done = bf16[384,1536]{1,0:T(8,128)(2,1)} async-done(((bf16[1536,1536]{1,0:T(8,128)(2,1)}), bf16[384,1536]{1,0:T(8,128)(2,1)}) %reduce-scatter.6.cloned.1.call-update) | async-done | bytes 1179664 | tf_op jit(solution)/shard_map/reduce_scatter | solution.py:261
  1279.2 240.7 %reduce-scatter.14.cloned.1.call-done = bf16[1152,1536]{1,0:T(8,128)(2,1)} async-done(((bf16[4608,1536]{1,0:T(8,128)(2,1)}), bf16[1152,1536]{1,0:T(8,128)(2,1)}) %reduce-scatter.14.cloned.1.call-update) | async-done | bytes 3538960 | tf_op jit(solution)/shard_map/reduce_scatter | solution.py:276
  1519.9 468.0 %reduce-scatter.12.cloned.1.call-done = bf16[384,9216]{1,0:T(8,128)(2,1)} async-done(((bf16[1536,9216]{1,0:T(8,128)(2,1)}), bf16[384,9216]{1,0:T(8,128)(2,1)}) %reduce-scatter.12.cloned.1.call-update) | async-done | bytes 7077904 | tf_op jit(solution)/shard_map/reduce_scatter | solution.py:273
  2001.5 75.2 %all_to_all.29 = bf16[8,128,1536]{2,1,0:T(8,128)(2,1)} all-to-all(bf16[8,128,1536]{2,1,0:T(8,128)(2,1)S(1)} %get-tuple-element.45), channel_id=1, replica_groups=mesh['seq'=8,'fsdp'=4] {'seq'}, dimensions={0} | all-to-all | bytes 6291456 | tf_op jit(solution)/shard_map/all_to_all | solution.py:253
  2082.6 13.1 all-reduce.6
  2095.8 46.8 %all-reduce.4 = (bf16[384]{0:T(512)(128)(2,1)S(1)}, bf16[384]{0:T(512)(128)(2,1)S(1)}) all-reduce(bf16[384]{0:T(512)(128)(2,1)S(1)} %dynamic-slice.1, bf16[384]{0:T(512)(128)(2,1)S(1)} %dynamic-slice.3), channel_id=1, replica_groups=mesh['seq'=8,'fsdp'=4] {'seq'}, use_global_device_ids=true, to_apply=%region_21.22 | all-reduce | flops 768 | bytes 3072 | tf_op jit(solution)/shard_map/psum | solution.py:281
  2157.8 77.9 %all-reduce.9.cloned.1.call-done = (bf16[384,1536]{1,0:T(8,128)(2,1)}, bf16[384,384]{1,0:T(8,128)(2,1)}, bf16[384,1536]{1,0:T(8,128)(2,1)}, bf16[384,9216]{1,0:T(8,128)(2,1)}, bf16[1152,1536]{1,0:T(8,128)(2,1)}) async-done(((bf16[384,1536]{1,0:T(8,128)(2,1)}, bf16[384,384]{1,0:T(8,128)(2,1)}, bf16[384,1536]{1,0:T(8,128)(2,1)}, bf16[384,9216]{1,0:T(8,128)(2,1)}, bf16[1152,1536]{1,0:T(8,128)(2,1)}), ...) | async-done | bytes 13271056 | tf_op jit(solution)/shard_map/psum | solution.py:282
  (252 shorter events, 245.1 us)
Async XLA Ops:
  7.2 75.8 %all-gather.8.cloned.1.call-start = ((), (), s32[]{:S(2)}) async-start(), calls=%async_computation.10 | async-start | bytes 1474560 | tf_op jit(solution)/shard_map/all_gather | solution.py:134
  7.9 125.0 %all-gather.10.cloned.1.call-start = ((), (), s32[]{:S(2)}) async-start(), calls=%async_computation.11 | async-start | bytes 5898240 | tf_op jit(solution)/shard_map/all_gather | solution.py:133
  8.7 213.8 %all-gather.12.cloned.1.call-start = ((), (), s32[]{:S(2)}) async-start(), calls=%async_computation.12 | async-start | bytes 5898240 | tf_op jit(solution)/shard_map/all_gather | solution.py:135
  9.4 689.1 %all-gather.14.cloned.1.call-start = ((), (), s32[]{:S(2)}) async-start(), calls=%async_computation.13 | async-start | bytes 35389440 | tf_op jit(solution)/shard_map/all_gather | solution.py:137
  10.0 932.1 %all-gather.16.cloned.1.call-start = ((), (), s32[]{:S(2)}) async-start(), calls=%async_computation.14 | async-start | bytes 17694720 | tf_op jit(solution)/shard_map/all_gather | solution.py:138
  15.2 10.3 all-to-all-start
  25.6 42.5 %all-to-all-start.1 = ((bf16[8,128,1536]{2,1,0:T(8,128)(2,1)}), bf16[8,128,1536]{2,1,0:T(8,128)(2,1)}, u32[]{:S(2)}, u32[]{:S(2)}) async-start(bf16[8,128,1536]{2,1,0:T(8,128)(2,1)} %bitcast.132), calls=%async_computation.1 | async-start | bytes 6291456 | tf_op jit(solution)/shard_map/all_to_all | solution.py:108
  68.1 42.3 %all-to-all-start.3 = ((bf16[8,128,1536]{2,1,0:T(8,128)(2,1)}), bf16[8,128,1536]{2,1,0:T(8,128)(2,1)}, u32[]{:S(2)}, u32[]{:S(2)}) async-start(bf16[8,128,1536]{2,1,0:T(8,128)(2,1)} %bitcast.131), calls=%async_computation.3 | async-start | bytes 6291456 | tf_op jit(solution)/shard_map/all_to_all | solution.py:109
  72.5 1089.5 %reduce-scatter.8.cloned.1.call-start = ((), (), s32[]{:S(2)}) async-start(), calls=%async_computation.16 | async-start | bytes 1474560 | tf_op jit(solution)/shard_map/reduce_scatter | solution.py:264
  73.4 59.5 %copy-start.24 = (f32[1536]{0:T(1024)}, f32[1536]{0:T(1024)S(1)}, u32[]{:S(2)}) copy-start(f32[1536]{0:T(1024)S(1)} %reshape.556) | copy-start | bytes 18436
  82.5 139.9 %copy-start.2 = (bf16[512,1536]{1,0:T(8,128)(2,1)}, bf16[512,1536]{1,0:T(8,128)(2,1)S(1)}, u32[]{:S(2)}) copy-start(bf16[512,1536]{1,0:T(8,128)(2,1)S(1)} %scatter_custom_fusion.2) | copy-start | bytes 4718596
  87.1 31.2 %collective-permute-start.1 = (bf16[512,384]{0,1:T(8,128)(2,1)}, bf16[512,384]{0,1:T(8,128)(2,1)S(1)}, u32[]{:S(2)}, u32[]{:S(2)}) collective-permute-start(bf16[512,384]{0,1:T(8,128)(2,1)} %pad_maximum_fusion.1), channel_id=1, source_target_pairs={{0,4},{4,8},{8,12},{12,16},{16,20},{20,24},{24,28},{1,5},{5,9},{9,... | collective-permute-start | bytes 1179656 | tf_op jit(solution)/shard_map/ppermute | solution.py:19
  89.4 28.9 %collective-permute-start = (bf16[512,384]{0,1:T(8,128)(2,1)}, bf16[512,384]{0,1:T(8,128)(2,1)}, u32[]{:S(2)}, u32[]{:S(2)}) collective-permute-start(bf16[512,384]{0,1:T(8,128)(2,1)} %pad_maximum_fusion.1), channel_id=1, source_target_pairs={{0,8},{4,12},{8,16},{12,20},{16,24},{20,28},{1,9},{5,13},{9,17},{1... | collective-permute-start | bytes 1179656 | tf_op jit(solution)/shard_map/ppermute | solution.py:19
  222.4 476.1 %copy-start.29 = (f32[1536]{0:T(1024)S(1)}, f32[1536]{0:T(1024)}, u32[]{:S(2)}) copy-start(f32[1536]{0:T(1024)} %reshape.557) | copy-start | bytes 18436
  229.8 762.5 %copy-start.45 = (f32[512]{0:T(512)}, f32[512]{0:T(512)S(1)}, u32[]{:S(2)}) copy-start(f32[512]{0:T(512)S(1)} %fusion.73) | copy-start | bytes 6148
  698.5 243.6 %copy-start.6 = (bf16[512,1536]{1,0:T(8,128)(2,1)S(1)}, bf16[512,1536]{1,0:T(8,128)(2,1)}, u32[]{:S(2)}) copy-start(bf16[512,1536]{1,0:T(8,128)(2,1)} %scatter_custom_fusion.4) | copy-start | bytes 4718596
  1057.2 13.1 collective-permute-start.2
  1058.6 11.7 collective-permute-start.3
  1073.6 117.5 %reduce-scatter.10.cloned.1.call-start = ((), (), s32[]{:S(2)}) async-start(), calls=%async_computation.17 | async-start | bytes 5898240 | tf_op jit(solution)/shard_map/reduce_scatter | solution.py:267
  1080.2 199.0 %reduce-scatter.6.cloned.1.call-start = ((), (), s32[]{:S(2)}) async-start(), calls=%async_computation.15 | async-start | bytes 5898240 | tf_op jit(solution)/shard_map/reduce_scatter | solution.py:261
  1094.3 425.6 %reduce-scatter.14.cloned.1.call-start = ((), (), s32[]{:S(2)}) async-start(), calls=%async_computation.19 | async-start | bytes 17694720 | tf_op jit(solution)/shard_map/reduce_scatter | solution.py:276
  1108.3 879.7 %reduce-scatter.12.cloned.1.call-start = ((), (), s32[]{:S(2)}) async-start(), calls=%async_computation.18 | async-start | bytes 35389440 | tf_op jit(solution)/shard_map/reduce_scatter | solution.py:273
  1133.1 1102.6 %all-reduce.9.cloned.1.call-start = ((), (), s32[]{:S(2)}) async-start(), calls=%async_computation.20 | async-start | bytes 26542080 | tf_op jit(solution)/shard_map/psum | solution.py:282
  2076.7 73.8 %all-to-all-start.2 = ((bf16[8,128,1536]{2,1,0:T(8,128)(2,1)}), bf16[8,128,1536]{2,1,0:T(8,128)(2,1)}, u32[]{:S(2)}, u32[]{:S(2)}) async-start(bf16[8,128,1536]{2,1,0:T(8,128)(2,1)} %get-tuple-element.46), calls=%async_computation.2 | async-start | bytes 6291456 | tf_op jit(solution)/shard_map/all_to_all | solution.py:252
  (57 other events, 563.7 us)
Sparse Core Ops, SparseCore 0:
  9.6 33.1 all-gather.7
  44.4 88.5 all-gather.9
  134.5 87.8 all-gather.11
  223.9 474.5 all-gather.13
  699.9 242.0 all-gather.15
  1073.7 31.0 reduce-scatter.7
  1107.1 83.9 reduce-scatter.9
  1193.4 85.7 reduce-scatter.5
  1282.1 237.7 reduce-scatter.13
  1522.1 465.7 reduce-scatter.11
  1993.1 242.6 all-reduce.8
where the time goes:
time: 2270 us; the launch traced here: 2260 us
  waiting for transfers between devices  1690 us (74%)
  matrix products  230 us (10%)
  blocking collectives  159 us (7%)
  other arithmetic  72.2 us (3%)
  local copies, waits for them, and re-layouts  64.7 us (3%)
  starting transfers between devices  28.7 us (1%)
    all_gather x1, waiting for transfers between devices, body(): lax.all_gather(w_gate_up, 'fsdp', axis=0, tiled=True)  469 us
    reduce_scatter x1, waiting for transfers between devices, body(): lax.psum_scatter(grad_gate_up.astype(jnp.bfloat16), 'fsdp', scatter_dimen...  468 us
    reduce_scatter x1, waiting for transfers between devices, body(): lax.psum_scatter(grad_down.astype(jnp.bfloat16), 'fsdp', scatter_dimensio...  241 us
    all_gather x1, waiting for transfers between devices, body(): lax.all_gather(w_down, 'fsdp', axis=0, tiled=True)  218 us
    reduce_scatter x1, waiting for transfers between devices, body(): lax.psum_scatter(grad_query.astype(jnp.bfloat16), 'fsdp', scatter_dimensi...  88.1 us
    psum x1, waiting for transfers between devices, body(): lax.psum(share_query.astype(jnp.bfloat16), 'seq').astype(jnp.float32)  77.9 us
    all_to_all x1, blocking collectives, body(): lax.all_to_all(to_owner(grad_rows), 'seq', split_axis=0, concat_axis=0, t...  75.2 us
    all_gather x1, waiting for transfers between devices, body(): lax.all_gather(w_out, 'fsdp', axis=0, tiled=True)  50 us
  transfers between devices with their start and end apart: 19, of which 12 were waited for; matrix products, arithmetic and copies ran while one was open for 10% of the time, Pallas kernels for 0%

commit v1 on v0

--- a/solution.py
+++ b/solution.py
@@ -128,14 +128,27 @@
 
     packed = from_slots(got_tokens)
     packed_grad = from_slots(got_cotangent)
-    gain_attn, query_w, kv_w, out_w, gain_ffn, gate_up_w, down_w = (
+    def whole(shard):
+        part = shard.shape[0] // ranks
+        mine = lax.dynamic_slice_in_dim(shard, position * part, part, axis=0)
+        return lax.all_gather(mine, ("fsdp", "seq"), axis=0, tiled=True)
+
+    def shared(grad):
+        mine = lax.psum_scatter(
+            grad.astype(jnp.bfloat16), ("fsdp", "seq"), scatter_dimension=0, tiled=True
+        )
+        return lax.all_gather(mine, "seq", axis=0, tiled=True).astype(jnp.float32)
+
+    query_w, kv_w, out_w, gate_up_w, down_w = (
+        whole(w_query),
+        whole(w_kv),
+        whole(w_out),
+        whole(w_gate_up),
+        whole(w_down),
+    )
+    gain_attn, gain_ffn = (
         lax.all_gather(norm_gain, "fsdp", axis=0, tiled=True),
-        lax.all_gather(w_query, "fsdp", axis=0, tiled=True),
-        lax.all_gather(w_kv, "fsdp", axis=0, tiled=True),
-        lax.all_gather(w_out, "fsdp", axis=0, tiled=True),
         lax.all_gather(ffn_gain, "fsdp", axis=0, tiled=True),
-        lax.all_gather(w_gate_up, "fsdp", axis=0, tiled=True),
-        lax.all_gather(w_down, "fsdp", axis=0, tiled=True),
     )
     places = position * row_count + jnp.arange(row_count, dtype=jnp.int32)
     doc_query, offset_query = layout(lengths[0], places)
@@ -191,15 +204,6 @@
     block_rows = (
         hidden_state + jnp.dot(activated, down_w, preferred_element_type=jnp.float32)
     ).astype(jnp.bfloat16)
-    gain_attn, query_w, kv_w, out_w, gain_ffn, gate_up_w, down_w = (
-        lax.all_gather(norm_gain, "fsdp", axis=0, tiled=True),
-        lax.all_gather(w_query, "fsdp", axis=0, tiled=True),
-        lax.all_gather(w_kv, "fsdp", axis=0, tiled=True),
-        lax.all_gather(w_out, "fsdp", axis=0, tiled=True),
-        lax.all_gather(ffn_gain, "fsdp", axis=0, tiled=True),
-        lax.all_gather(w_gate_up, "fsdp", axis=0, tiled=True),
-        lax.all_gather(w_down, "fsdp", axis=0, tiled=True),
-    )
     grad_down = jnp.einsum("tf,td->fd", activated, packed_grad, preferred_element_type=jnp.float32)
     d_activated = jnp.einsum("td,fd->tf", packed_grad, down_w, preferred_element_type=jnp.float32)
     unused_product, glu_pull = jax.vjp(gelu_product, gate_up)
@@ -254,37 +258,18 @@
     )
     block_arrived = home_out.reshape(ranks * capacity, model_width)[send_slot]
     grad_arrived = home_grad.reshape(ranks * capacity, model_width)[send_slot]
-    share_gain_attn, share_query, share_kv, share_out, share_gain_ffn, share_gate_up, share_down = (
-        lax.psum_scatter(
-            grad_gain_attn.astype(jnp.bfloat16), "fsdp", scatter_dimension=0, tiled=True
-        ).astype(jnp.float32),
-        lax.psum_scatter(
-            grad_query.astype(jnp.bfloat16), "fsdp", scatter_dimension=0, tiled=True
-        ).astype(jnp.float32),
-        lax.psum_scatter(
-            grad_kv.astype(jnp.bfloat16), "fsdp", scatter_dimension=0, tiled=True
-        ).astype(jnp.float32),
-        lax.psum_scatter(
-            grad_out.astype(jnp.bfloat16), "fsdp", scatter_dimension=0, tiled=True
-        ).astype(jnp.float32),
-        lax.psum_scatter(
-            grad_gain_ffn.astype(jnp.bfloat16), "fsdp", scatter_dimension=0, tiled=True
-        ).astype(jnp.float32),
-        lax.psum_scatter(
-            grad_gate_up.astype(jnp.bfloat16), "fsdp", scatter_dimension=0, tiled=True
-        ).astype(jnp.float32),
-        lax.psum_scatter(
-            grad_down.astype(jnp.bfloat16), "fsdp", scatter_dimension=0, tiled=True
-        ).astype(jnp.float32),
-    )
-    total_gain_attn, total_query, total_kv, total_out, total_gain_ffn, total_gate_up, total_down = (
-        lax.psum(share_gain_attn.astype(jnp.bfloat16), "seq").astype(jnp.float32),
-        lax.psum(share_query.astype(jnp.bfloat16), "seq").astype(jnp.float32),
-        lax.psum(share_kv.astype(jnp.bfloat16), "seq").astype(jnp.float32),
-        lax.psum(share_out.astype(jnp.bfloat16), "seq").astype(jnp.float32),
-        lax.psum(share_gain_ffn.astype(jnp.bfloat16), "seq").astype(jnp.float32),
-        lax.psum(share_gate_up.astype(jnp.bfloat16), "seq").astype(jnp.float32),
-        lax.psum(share_down.astype(jnp.bfloat16), "seq").astype(jnp.float32),
+    total_query, total_kv, total_out, total_gate_up, total_down = (
+        shared(grad_query),
+        shared(grad_kv),
+        shared(grad_out),
+        shared(grad_gate_up),
+        shared(grad_down),
+    )
+    total_gain_attn, total_gain_ffn = (
+        lax.psum(
+            lax.psum_scatter(gain, "fsdp", scatter_dimension=0, tiled=True), "seq"
+        )
+        for gain in (grad_gain_attn, grad_gain_ffn)
     )
     return (
         block_arrived[None],

time: 2270 us -> 1490 us (0.66)
  waiting for transfers between devices: 1690 us -> 943 us
  blocking collectives: 159 us -> 123 us
    all_gather x5 -> x9, waiting for transfers between devices: 749 us -> 371 us  [the longest x5 290 us: whole(): return lax.all_gather(mine, ('fsdp', 'seq'), axis=0, tiled=True)]
    reduce_scatter x5, waiting for transfers between devices: 826 us -> 528 us  [shared(): lax.psum_scatter(grad.astype(jnp.bfloat16), ('fsdp', 'seq'), scatter_dime...]
    psum x1 -> x0, waiting for transfers between devices: 77.9 us -> none  [body(): lax.psum(share_query.astype(jnp.bfloat16), 'seq').astype(jnp.float32)]
    all_to_all x1, blocking collectives: 75.2 us -> 44 us  [body(): lax.all_to_all(to_owner(grad_rows), 'seq', split_axis=0, concat_axis=0, t...]
  transfers between devices with their start and end apart: 19 -> 22, of which waited for: 12 -> 13; matrix products, arithmetic and copies ran while one was open for 10% -> 19% of each run, Pallas kernels for 0% -> 0%
where the time goes in v1:
time: 1490 us; the launch traced here: 1480 us
  waiting for transfers between devices  943 us (63%)
  matrix products  230 us (15%)
  blocking collectives  123 us (8%)
  other arithmetic  72.4 us (5%)
  local copies, waits for them, and re-layouts  71.1 us (5%)
  starting transfers between devices  28 us (2%)
  between operations  15.7 us (1%)
    reduce_scatter x5, waiting for transfers between devices, shared(): lax.psum_scatter(grad.astype(jnp.bfloat16), ('fsdp', 'seq'), scatter_dime...  528 us
    all_gather x5, waiting for transfers between devices, whole(): return lax.all_gather(mine, ('fsdp', 'seq'), axis=0, tiled=True)  290 us
    all_gather x4, waiting for transfers between devices, shared(): return lax.all_gather(mine, 'seq', axis=0, tiled=True).astype(jnp.float32)  81 us
    all_to_all x1, blocking collectives, body(): lax.all_to_all(to_owner(grad_rows), 'seq', split_axis=0, concat_axis=0, t...  44 us
  transfers between devices with their start and end apart: 22, of which 13 were waited for; matrix products, arithmetic and copies ran while one was open for 19% of the time, Pallas kernels for 0%

profile of v1, /device:TPU:0, one launch (start us, length us, event | category | flops | bytes accessed | tf_op | source)
XLA Modules:
  0.0 1483.2 jit_solution(12017635830104237169)
XLA Ops:
  41.5 12.1 all-gather.1
  53.6 11.9 all-gather
  103.6 22.1 %all-to-all-done.3 = bf16[8,128,1536]{2,1,0:T(8,128)(2,1)} async-done(((bf16[8,128,1536]{2,1,0:T(8,128)(2,1)}), bf16[8,128,1536]{2,1,0:T(8,128)(2,1)}, u32[]{:S(2)}, u32[]{:S(2)}) %all-to-all-start.3) | async-done | bytes 3145760 | tf_op jit(solution)/shard_map/all_to_all | solution.py:109
  135.8 19.3 %all-gather.14.cloned.1.call-done = bf16[1536,1536]{1,0:T(8,128)(2,1)} async-done(((bf16[48,1536]{1,0:T(8,128)(2,1)}), bf16[1536,1536]{1,0:T(8,128)(2,1)}) %all-gather.14.cloned.1.call-update) | async-done | bytes 4718608 | tf_op jit(solution)/shard_map/all_gather | solution.py:134
  181.6 12.2 convolution_convert_fusion.6
  193.8 26.9 %all-gather.16.cloned.1.call-done = bf16[1536,1536]{1,0:T(8,128)(2,1)} async-done(((bf16[48,1536]{1,0:T(8,128)(2,1)}), bf16[1536,1536]{1,0:T(8,128)(2,1)}) %all-gather.16.cloned.1.call-update) | async-done | bytes 4718608 | tf_op jit(solution)/shard_map/all_gather | solution.py:134
  229.0 163.0 %all-gather.18.cloned.1.call-done = bf16[1536,9216]{1,0:T(8,128)(2,1)} async-done(((bf16[48,9216]{1,0:T(8,128)(2,1)}), bf16[1536,9216]{1,0:T(8,128)(2,1)}) %all-gather.18.cloned.1.call-update) | async-done | bytes 28311568 | tf_op jit(solution)/shard_map/all_gather | solution.py:134
  392.0 23.8 %fusion.85 = f32[512,9216]{1,0:T(8,128)} fusion(bf16[1536,9216]{1,0:T(8,128)(2,1)} %all-gather.18.cloned.1.call-done, f32[512,1536]{1,0:T(8,128)} %get-tuple-element.45, f32[1536]{0:T(1024)} %reshape.557, f32[512]{0:T(512)} %fusion.73), kind=kOutput, calls=%fused_computation.200 | convolution fusion | flops 14497873920 | bytes 50339840 | tf_op jit(solution)/shard_map/dot_general | solution.py:202
  415.8 80.9 %all-gather.20.cloned.1.call-done = bf16[4608,1536]{1,0:T(8,128)(2,1)} async-done(((bf16[144,1536]{1,0:T(8,128)(2,1)}), bf16[4608,1536]{1,0:T(8,128)(2,1)}) %all-gather.20.cloned.1.call-update) | async-done | bytes 14155792 | tf_op jit(solution)/shard_map/all_gather | solution.py:134
  496.7 25.3 %fusion.13 = (f32[512,4608]{1,0:T(8,128)}, f32[512,4608]{1,0:T(8,128)}, bf16[512,4608]{1,0:T(8,128)(2,1)}) fusion(f32[512,9216]{1,0:T(8,128)} %fusion.85, bf16[512,1536]{1,0:T(8,128)(2,1)S(1)} %copy-done.11, bf16[4608,1536]{1,0:T(8,128)(2,1)} %all-gather.20.cloned.1.call-done), kind=kOutput, calls=%fused_computation.46 | convolution fusion | flops 7304380416 | bytes 58195968 | tf_op jit(solution)/shard_map/td,fd->tf/dot_general | solution.py:208
  522.0 25.0 %multiply_reduce_fusion = (f32[1536]{0:T(1024)}, f32[512]{0:T(512)}, f32[512,1536]{1,0:T(8,128)}) fusion(f32[512,1536]{1,0:T(8,128)} %get-tuple-element.45, f32[512]{0:T(512)} %fusion.73, f32[1536]{0:T(1024)} %reshape.557, bf16[1536,9216]{1,0:T(8,128)(2,1)} %all-gather.18.cloned.1.call-done, f32[512,4608]{1,0:T(8,128)} %get-tuple-element.20, ...), kind=kOutput, calls=%fused_computation.59 | convolution fusion | flops 14509668352 | bytes 53493760 | tf_op jit(solution)/shard_map/tf,df->td/dot_general | solution.py:212
  566.5 22.1 %fusion = (f32[8,512]{1,0:T(8,128)}, f32[1536,512,8]{1,0,2:T(8,128)}) fusion(f32[1536,512,8]{1,0,2:T(8,128)} %get-tuple-element.43, f32[8,512]{1,0:T(8,128)S(1)} %log_add_fusion, pred[512,1536]{0,1:T(8,128)(4,1)S(1)} %fusion.24, bf16[512,8,192]{0,2,1:T(8,128)(2,1)S(1)} %bitcast.134, bf16[1536,384]{0,1:T(8,128)(2,1)S(1)} %maximum_maximum_fusion), kind=kOutput, calls=%fused_computation.12 | convolution fusion | flops 2441080832 | bytes 53313536 | tf_op jit(solution)/shard_map/qhd,kd->hqk/dot_general | solution.py:224
  588.6 18.1 %fusion.2 = bf16[8,512,1536]{1,2,0:T(8,128)(2,1)S(1)} fusion(f32[1536,512,8]{1,0,2:T(8,128)} %get-tuple-element.48, f32[1536,512,8]{1,0,2:T(8,128)} %get-tuple-element.43, f32[8,512]{1,0:T(8,128)} %get-tuple-element.47, f32[8,512]{1,0:T(8,128)S(1)} %log_add_fusion, pred[512,1536]{0,1:T(8,128)(4,1)S(1)} %fusion.24), kind=kLoop, calls=%fused_computation.14 | loop fusion | flops 31457280 | bytes 63733760 | tf_op jit(solution)/shard_map/convert_element_type | solution.py:226
  619.3 12.9 convolution_convert_fusion.1
  632.9 23.7 %convolution_convert_fusion = bf16[1536,9216]{1,0:T(8,128)(2,1)} fusion(f32[512,4608]{1,0:T(8,128)} %get-tuple-element.20, f32[512,4608]{1,0:T(8,128)} %get-tuple-element.19, f32[512,1536]{1,0:T(8,128)} %get-tuple-element.45, f32[1536]{0:T(1024)S(1)} %copy-done.31, f32[512]{0:T(512)S(1)} %copy-done.42), kind=kOutput, calls=%fused_computation.9 | convolution fusion | flops 14521466880 | bytes 50339840 | tf_op jit(solution)/shard_map/td,tf->df/dot_general | solution.py:211
  693.9 90.3 %reduce-scatter.6.cloned.1.call-done = bf16[48,1536]{1,0:T(8,128)(2,1)} async-done(((bf16[1536,1536]{1,0:T(8,128)(2,1)}), bf16[48,1536]{1,0:T(8,128)(2,1)}) %reduce-scatter.6.cloned.1.call-update) | async-done | bytes 147472 | tf_op jit(solution)/shard_map/reduce_scatter | solution.py:137
  784.2 168.5 %reduce-scatter.14.cloned.1.call-done = bf16[144,1536]{1,0:T(8,128)(2,1)} async-done(((bf16[4608,1536]{1,0:T(8,128)(2,1)}), bf16[144,1536]{1,0:T(8,128)(2,1)}) %reduce-scatter.14.cloned.1.call-update) | async-done | bytes 442384 | tf_op jit(solution)/shard_map/reduce_scatter | solution.py:137
  952.8 268.8 %reduce-scatter.12.cloned.1.call-done = bf16[48,9216]{1,0:T(8,128)(2,1)} async-done(((bf16[1536,9216]{1,0:T(8,128)(2,1)}), bf16[48,9216]{1,0:T(8,128)(2,1)}) %reduce-scatter.12.cloned.1.call-update) | async-done | bytes 884752 | tf_op jit(solution)/shard_map/reduce_scatter | solution.py:137
  1222.2 12.5 fusion.25
  1258.4 44.0 %all_to_all.29 = bf16[8,128,1536]{2,1,0:T(8,128)(2,1)} all-to-all(bf16[8,128,1536]{2,1,0:T(8,128)(2,1)S(1)} %get-tuple-element.40), channel_id=1, replica_groups=mesh['seq'=8,'fsdp'=4] {'seq'}, dimensions={0} | all-to-all | bytes 6291456 | tf_op jit(solution)/shard_map/all_to_all | solution.py:257
  1307.5 17.4 %all-reduce.5 = (f32[1536]{0:T(1024)S(1)}, f32[1536]{0:T(1024)S(1)}) all-reduce(f32[1536]{0:T(1024)S(1)} %copy-done.32, f32[1536]{0:T(1024)S(1)} %copy-done.46), channel_id=2, replica_groups=mesh['seq'=8,'fsdp'=4] {'fsdp'}, use_global_device_ids=true, to_apply=%region_20.21.clone | all-reduce | flops 3072 | bytes 24576
  1325.1 27.9 %all-reduce.4 = (f32[384]{0:T(512)}, f32[384]{0:T(512)}) all-reduce(f32[384]{0:T(512)S(1)} %dynamic-slice.1, f32[384]{0:T(512)S(1)} %dynamic-slice.3), channel_id=1, replica_groups=mesh['seq'=8,'fsdp'=4] {'seq'}, use_global_device_ids=true, to_apply=%region_21.22 | all-reduce | flops 768 | bytes 6144 | tf_op jit(solution)/shard_map/psum | solution.py:269
  1382.7 32.9 %all-gather.28.cloned.1.call-done = bf16[1152,1536]{1,0:T(8,128)(2,1)} async-done(((bf16[144,1536]{1,0:T(8,128)(2,1)}), bf16[1152,1536]{1,0:T(8,128)(2,1)}) %all-gather.28.cloned.1.call-update) | async-done | bytes 3538960 | tf_op jit(solution)/shard_map/all_gather | solution.py:140
  1421.5 44.7 %all-gather.26.cloned.1.call-done = bf16[384,9216]{1,0:T(8,128)(2,1)} async-done(((bf16[48,9216]{1,0:T(8,128)(2,1)}), bf16[384,9216]{1,0:T(8,128)(2,1)}) %all-gather.26.cloned.1.call-update) | async-done | bytes 7077904 | tf_op jit(solution)/shard_map/all_gather | solution.py:140
  (250 shorter events, 261.3 us)
Async XLA Ops:
  7.2 84.1 %all-gather.12.cloned.1.call-start = ((), (), s32[]{:S(2)}) async-start(), calls=%async_computation.10 | async-start | bytes 1216512 | tf_op jit(solution)/shard_map/all_gather | solution.py:134
  8.8 146.3 %all-gather.14.cloned.1.call-start = ((), (), s32[]{:S(2)}) async-start(), calls=%async_computation.11 | async-start | bytes 4866048 | tf_op jit(solution)/shard_map/all_gather | solution.py:134
  10.5 210.2 %all-gather.16.cloned.1.call-start = ((), (), s32[]{:S(2)}) async-start(), calls=%async_computation.12 | async-start | bytes 4866048 | tf_op jit(solution)/shard_map/all_gather | solution.py:134
  12.1 379.9 %all-gather.18.cloned.1.call-start = ((), (), s32[]{:S(2)}) async-start(), calls=%async_computation.13 | async-start | bytes 29196288 | tf_op jit(solution)/shard_map/all_gather | solution.py:134
  14.3 482.4 %all-gather.20.cloned.1.call-start = ((), (), s32[]{:S(2)}) async-start(), calls=%async_computation.14 | async-start | bytes 14598144 | tf_op jit(solution)/shard_map/all_gather | solution.py:134
  19.8 11.1 all-to-all-start
  31.0 45.4 %all-to-all-start.1 = ((bf16[8,128,1536]{2,1,0:T(8,128)(2,1)}), bf16[8,128,1536]{2,1,0:T(8,128)(2,1)S(1)}, u32[]{:S(2)}, u32[]{:S(2)}) async-start(bf16[8,128,1536]{2,1,0:T(8,128)(2,1)} %bitcast.13), calls=%async_computation.1 | async-start | bytes 6291456 | tf_op jit(solution)/shard_map/all_to_all | solution.py:108
  78.0 47.6 %all-to-all-start.3 = ((bf16[8,128,1536]{2,1,0:T(8,128)(2,1)}), bf16[8,128,1536]{2,1,0:T(8,128)(2,1)}, u32[]{:S(2)}, u32[]{:S(2)}) async-start(bf16[8,128,1536]{2,1,0:T(8,128)(2,1)} %bitcast.30), calls=%async_computation.3 | async-start | bytes 6291456 | tf_op jit(solution)/shard_map/all_to_all | solution.py:109
  82.5 610.7 %reduce-scatter.10.cloned.1.call-start = ((), (), s32[]{:S(2)}) async-start(), calls=%async_computation.18 | async-start | bytes 4866048 | tf_op jit(solution)/shard_map/reduce_scatter | solution.py:137
  95.3 38.4 %collective-permute-start.1 = (bf16[512,384]{0,1:T(8,128)(2,1)S(1)}, bf16[512,384]{0,1:T(8,128)(2,1)S(1)}, u32[]{:S(2)}, u32[]{:S(2)}) collective-permute-start(bf16[512,384]{0,1:T(8,128)(2,1)S(1)} %pad_maximum_fusion.1), channel_id=1, source_target_pairs={{0,4},{4,8},{8,12},{12,16},{16,20},{20,24},{24,28},{1,5},{5,9},{9,... | collective-permute-start | bytes 1179656 | tf_op jit(solution)/shard_map/ppermute | solution.py:19
  97.6 36.9 %collective-permute-start = (bf16[512,384]{0,1:T(8,128)(2,1)S(1)}, bf16[512,384]{0,1:T(8,128)(2,1)}, u32[]{:S(2)}, u32[]{:S(2)}) collective-permute-start(bf16[512,384]{0,1:T(8,128)(2,1)S(1)} %pad_maximum_fusion.1), channel_id=1, source_target_pairs={{0,8},{4,12},{8,16},{12,20},{16,24},{20,28},{1,9},{5,13},{9,17},{1... | collective-permute-start | bytes 1179656 | tf_op jit(solution)/shard_map/ppermute | solution.py:19
  566.4 217.7 %reduce-scatter.6.cloned.1.call-start = ((), (), s32[]{:S(2)}) async-start(), calls=%async_computation.15 | async-start | bytes 4866048 | tf_op jit(solution)/shard_map/reduce_scatter | solution.py:137
  618.0 334.8 %reduce-scatter.14.cloned.1.call-start = ((), (), s32[]{:S(2)}) async-start(), calls=%async_computation.22 | async-start | bytes 14598144 | tf_op jit(solution)/shard_map/reduce_scatter | solution.py:137
  632.3 589.3 %reduce-scatter.12.cloned.1.call-start = ((), (), s32[]{:S(2)}) async-start(), calls=%async_computation.20 | async-start | bytes 29196288 | tf_op jit(solution)/shard_map/reduce_scatter | solution.py:137
  656.7 696.4 %reduce-scatter.8.cloned.1.call-start = ((), (), s32[]{:S(2)}) async-start(), calls=%async_computation.17 | async-start | bytes 1216512 | tf_op jit(solution)/shard_map/reduce_scatter | solution.py:137
  676.7 13.1 collective-permute-start.2
  678.0 11.8 collective-permute-start.3
  690.9 530.7 %copy-start.30 = (s32[8,1,128]{2,1,0:T(1,128)S(1)}, s32[8,1,128]{2,1,0:T(1,128)}, u32[]{:S(2)}) copy-start(s32[8,1,128]{2,1,0:T(1,128)} %copy-done.29) | copy-start | bytes 12292
  690.9 531.3 %copy-start.41 = (s32[1024,1]{0,1:T(1,128)S(1)}, s32[1024,1]{0,1:T(1,128)}, u32[]{:S(2)}) copy-start(s32[1024,1]{0,1:T(1,128)} %get-tuple-element.32) | copy-start | bytes 12292
  693.1 680.2 %all-gather.24.cloned.1.call-start = ((), (), s32[]{:S(2)}) async-start(), calls=%async_computation.19 | async-start | bytes 1327104 | tf_op jit(solution)/shard_map/all_gather | solution.py:140
  693.8 685.9 %all-gather.22.cloned.1.call-start = ((), (), s32[]{:S(2)}) async-start(), calls=%async_computation.16 | async-start | bytes 1327104 | tf_op jit(solution)/shard_map/all_gather | solution.py:140
  784.2 631.4 %all-gather.28.cloned.1.call-start = ((), (), s32[]{:S(2)}) async-start(), calls=%async_computation.23 | async-start | bytes 3981312 | tf_op jit(solution)/shard_map/all_gather | solution.py:140
  952.7 513.5 %all-gather.26.cloned.1.call-start = ((), (), s32[]{:S(2)}) async-start(), calls=%async_computation.21 | async-start | bytes 7962624 | tf_op jit(solution)/shard_map/all_gather | solution.py:140
  1302.4 67.9 %all-to-all-start.2 = ((bf16[8,128,1536]{2,1,0:T(8,128)(2,1)}), bf16[8,128,1536]{2,1,0:T(8,128)(2,1)S(1)}, u32[]{:S(2)}, u32[]{:S(2)}) async-start(bf16[8,128,1536]{2,1,0:T(8,128)(2,1)} %get-tuple-element.41), calls=%async_computation.2 | async-start | bytes 6291456 | tf_op jit(solution)/shard_map/all_to_all | solution.py:256
  (53 other events, 1190.4 us)
Sparse Core Ops, SparseCore 0:
  11.5 59.8 all-gather.11
  74.3 80.7 all-gather.13
  158.0 62.6 all-gather.15
  223.5 168.4 all-gather.17
  395.3 101.3 all-gather.19
  566.5 105.1 reduce-scatter.9
  678.1 106.0 reduce-scatter.5
  790.8 161.9 reduce-scatter.13
  959.2 262.3 reduce-scatter.11
  1227.1 100.0 reduce-scatter.7
  1329.0 24.8 all-gather.23
  1355.7 23.9 all-gather.21
  1381.6 33.9 all-gather.27
  1417.3 48.8 all-gather.25

commit v2 on v1

v2 whole, which is shorter than its diff:
```python
import jax
import jax.numpy as jnp
from jax import lax
from jax.experimental import pallas as pl
from jax.experimental.pallas import tpu as pltpu
from jax.sharding import PartitionSpec as P

HD = 192
FF = 4608
WINDOW = 1024


EPSILON = 1e-06
ROPE_BASE = 10000.0
MASKED = -1e30


def passed_along(x, axis, by):
    length = lax.axis_size(axis)
    pairs = [(i, i + by) for i in range(length) if 0 <= i + by < length]
    return lax.ppermute(x, axis, pairs)


def rms_scale(values, gain):
    return values * lax.rsqrt(jnp.mean(values * values, axis=-1, keepdims=True) + EPSILON) * gain


def rotate(heads, cosine, sine):
    half = heads.shape[-1] // 2
    first_half = heads[..., :half]
    second_half = heads[..., half:]
    return jnp.concatenate(
        [first_half * cosine - second_half * sine, second_half * cosine + first_half * sine],
        axis=-1,
    )


def unrotate(heads, cosine, sine):
    half = heads.shape[-1] // 2
    first_half = heads[..., :half]
    second_half = heads[..., half:]
    return jnp.concatenate(
        [first_half * cosine + second_half * sine, second_half * cosine - first_half * sine],
        axis=-1,
    )


def angles(places, head_width):
    steps_half = jnp.arange(head_width // 2, dtype=jnp.float32)
    inverse = ROPE_BASE ** (-2.0 * steps_half / head_width)
    theta = places[:, None] * inverse[None, :]
    return (jnp.cos(theta), jnp.sin(theta))


def layout(lengths, places):
    ends = jnp.cumsum(lengths)
    starts = ends - lengths
    inside = (places[:, None] >= starts[None, :]) & (places[:, None] < ends[None, :])
    numbers = jnp.arange(1, lengths.shape[0] + 1, dtype=jnp.int32)
    document = jnp.sum(jnp.where(inside, numbers[None, :], 0), axis=1) - 1
    offset = places - jnp.sum(jnp.where(inside, starts[None, :], 0), axis=1)
    return (document, offset)


def after(x, *done):
    return lax.optimization_barrier((x, *done))[0]


def after_all(xs, *done):
    return lax.optimization_barrier((*xs, *done))[: len(xs)]


def rounded(x):
    return x.astype(jnp.bfloat16)


def widened(x):
    return x.astype(jnp.float32)


def added(*terms):
    return rounded(sum(widened(term) for term in terms))


def dot(a, b):
    return jnp.dot(a, b, preferred_element_type=jnp.float32)


def dot_rows(a, b):
    return jnp.einsum("td,tf->df", a, b, preferred_element_type=jnp.float32)


def dot_across(a, b):
    return jnp.einsum("tf,df->td", a, b, preferred_element_type=jnp.float32)


def turn(x, tables, back):
    width = x.shape[-1]
    half = HD // 2
    later = pltpu.roll(x, width - half, axis=1)
    sooner = pltpu.roll(x, half, axis=1)
    turned = later * tables[1] + sooner * tables[2]
    return x * tables[0] - turned if back else x * tables[0] + turned


def tables_of(cosine, sine, heads, still):
    none = jnp.zeros_like(sine)
    ones = jnp.ones_like(sine)
    return (
        jnp.concatenate([cosine, cosine] * heads + [ones, ones] * still, axis=1),
        jnp.concatenate([-sine, none] * heads + [none, none] * still, axis=1),
        jnp.concatenate([none, sine] * heads + [none, none] * still, axis=1),
    )


def no_entry(doc_query, doc_key, rows, keys):
    key = lax.broadcasted_iota(jnp.int32, (keys, rows), 0)
    row = lax.broadcasted_iota(jnp.int32, (keys, rows), 1)
    gap = WINDOW + row - key
    seen = (doc_key == doc_query) & (doc_key >= 0) & (gap >= 0) & (gap < WINDOW)
    return jnp.where(seen, 0.0, MASKED)


def dot_last(a, b):
    return lax.dot_general(a, b, (((1,), (1,)), ((), ())), preferred_element_type=jnp.float32)


def attend(query_lin, tables, pairs, pairs_across, doc_query, doc_key):
    rows, width = query_lin.shape
    block = 256
    keys = WINDOW + block
    couples = width // (2 * HD)

    def kernel(q_ref, t0, t1, t2, pairs_ref, across_ref, dq_ref, dk_ref, turned_ref, mixed_ref, total_ref, bias):
        start = pl.multiple_of(pl.program_id(0) * block, block)
        window = pl.ds(start, keys)

        @pl.when(pl.program_id(1) == 0)
        def fill():
            bias[...] = no_entry(dq_ref[...], dk_ref[window, :], block, keys)

        queries = turn(q_ref[...], (t0[...], t1[...], t2[...]), False) * HD ** (-0.5)
        queries = queries.astype(jnp.bfloat16)
        turned_ref[...] = queries
        own_keys = pairs_ref[window, :][:, :HD]
        values = across_ref[pl.ds(HD, HD), window]
        mixed, totals = [], []
        for head in range(2):
            scores = dot_last(own_keys, queries[:, head * HD : (head + 1) * HD]) + bias[...]
            top = jnp.max(scores, axis=0, keepdims=True)
            weights = jnp.exp(scores - top)
            total = jnp.sum(weights, axis=0, keepdims=True)
            totals.append(top + jnp.log(total))
            mixed.append(dot(values, weights.astype(jnp.bfloat16)) * (1.0 / total))
        mixed_ref[...] = jnp.concatenate(mixed, axis=0).T.astype(jnp.bfloat16)
        total_ref[0] = jnp.concatenate(totals, axis=0)

    tile = pl.BlockSpec((block, 2 * HD), lambda i, j: (i, j))
    table = pl.BlockSpec((block, 2 * HD), lambda i, j: (i, 0))
    return pl.pallas_call(
        kernel,
        grid=(rows // block, couples),
        in_specs=[
            tile,
            table,
            table,
            table,
            pl.BlockSpec(pairs.shape, lambda i, j: (0, 0)),
            pl.BlockSpec(pairs_across.shape, lambda i, j: (0, 0)),
            pl.BlockSpec((1, block), lambda i, j: (0, i)),
            pl.BlockSpec(doc_key.shape, lambda i, j: (0, 0)),
        ],
        out_specs=[tile, tile, pl.BlockSpec((1, 2, block), lambda i, j: (j, 0, i))],
        out_shape=[
            jax.ShapeDtypeStruct((rows, width), jnp.bfloat16),
            jax.ShapeDtypeStruct((rows, width), jnp.bfloat16),
            jax.ShapeDtypeStruct((couples, 2, rows), jnp.float32),
        ],
        scratch_shapes=[pltpu.VMEM((keys, block), jnp.float32)],
        compiler_params=pltpu.CompilerParams(vmem_limit_bytes=48 * 2**20),
        cost_estimate=pl.CostEstimate(
            flops=2 * 2 * rows * couples * 2 * keys * HD, bytes_accessed=12 * 2**20, transcendentals=rows * couples * 2 * keys
        ),
    )(query_lin, *tables, pairs, pairs_across, doc_query, doc_key)


def attend_back(queries, d_mixed, totals, tables, pairs, pairs_across, doc_query, doc_key):
    rows, width = queries.shape
    block = 256
    keys = WINDOW + block
    couples = width // (2 * HD)
    last = (rows // block - 1, couples - 1)

    def kernel(q_ref, do_ref, total_ref, t0, t1, t2, pairs_ref, across_ref, dq_ref, dk_ref, d_lin_ref, d_pairs_ref, bias, d_keys, d_values, values):
        start = pl.multiple_of(pl.program_id(0) * block, block)
        window = pl.ds(start, keys)

        @pl.when((pl.program_id(0) == 0) & (pl.program_id(1) == 0))
        def clear():
            d_keys[...] = jnp.zeros_like(d_keys)
            d_values[...] = jnp.zeros_like(d_values)
            values[...] = pairs_ref[...][:, HD:]

        @pl.when(pl.program_id(1) == 0)
        def fill():
            bias[...] = no_entry(dq_ref[...], dk_ref[window, :], block, keys)

        own_keys = pairs_ref[window, :][:, :HD]
        own_values = values[window, :]
        keys_across = across_ref[pl.ds(0, HD), window]
        d_turned = []
        for head in range(2):
            part = slice(head * HD, (head + 1) * HD)
            q, do = q_ref[...][:, part], do_ref[...][:, part]
            scores = dot_last(own_keys, q) + bias[...]
            probs = jnp.exp(scores - total_ref[0][head : head + 1, :])
            d_probs = dot_last(own_values, do)
            product = probs * d_probs
            weighted = jnp.sum(product, axis=0, keepdims=True)
            d_scores = (product - probs * weighted).astype(jnp.bfloat16)
            d_turned.append(dot(keys_across, d_scores))
            d_keys[window, :] += dot(d_scores, q)
            d_values[window, :] += dot(probs.astype(jnp.bfloat16), do)
        d_turned = jnp.concatenate(d_turned, axis=0).T
        d_lin = turn(d_turned, (t0[...], t1[...], t2[...]), True) * HD ** (-0.5)
        d_lin_ref[...] = d_lin.astype(jnp.bfloat16)

        @pl.when((pl.program_id(0) == last[0]) & (pl.program_id(1) == last[1]))
        def finish():
            d_pairs_ref[...] = jnp.concatenate([d_keys[...], d_values[...]], axis=1)

    tile = pl.BlockSpec((block, 2 * HD), lambda i, j: (i, j))
    table = pl.BlockSpec((block, 2 * HD), lambda i, j: (i, 0))
    return pl.pallas_call(
        kernel,
        grid=(rows // block, couples),
        in_specs=[
            tile,
            tile,
            pl.BlockSpec((1, 2, block), lambda i, j: (j, 0, i)),
            table,
            table,
            table,
            pl.BlockSpec(pairs.shape, lambda i, j: (0, 0)),
            pl.BlockSpec(pairs_across.shape, lambda i, j: (0, 0)),
            pl.BlockSpec((1, block), lambda i, j: (0, i)),
            pl.BlockSpec(doc_key.shape, lambda i, j: (0, 0)),
        ],
        out_specs=[tile, pl.BlockSpec(pairs.shape, lambda i, j: (0, 0))],
        out_shape=[
            jax.ShapeDtypeStruct((rows, width), jnp.bfloat16),
            jax.ShapeDtypeStruct(pairs.shape, jnp.float32),
        ],
        scratch_shapes=[
            pltpu.VMEM((keys, block), jnp.float32),
            pltpu.VMEM((pairs.shape[0], HD), jnp.float32),
            pltpu.VMEM((pairs.shape[0], HD), jnp.float32),
            pltpu.VMEM((pairs.shape[0], HD), jnp.bfloat16),
        ],
        compiler_params=pltpu.CompilerParams(vmem_limit_bytes=48 * 2**20),
        cost_estimate=pl.CostEstimate(
            flops=5 * 2 * rows * couples * 2 * keys * HD, bytes_accessed=12 * 2**20, transcendentals=rows * couples * 2 * keys
        ),
    )(queries, d_mixed, totals, *tables, pairs, pairs_across, doc_query, doc_key)


def put_pieces(pieces, positions, shards):
    count = len(pieces)
    others, rows, unused_width = pieces[0].shape
    depth = others + 1
    widths = [shard.shape[2] for shard in shards]

    def kernel(positions_ref, *refs):
        i, j = pl.program_id(0), pl.program_id(1)
        sources, locals_, targets = (
            refs[:count],
            refs[count : count + len(shards)],
            refs[count + len(shards) :],
        )
        for at in range(count):

            @pl.when((i == at) & (j < others))
            def take():
                start = 0
                for target, width in zip(targets, widths):
                    target[0, 0] = sources[at][j, :, pl.ds(start, width)]
                    start += width

        @pl.when(j == others)
        def keep():
            for target, source in zip(targets, locals_):
                target[0, 0] = source[0]

    return pl.pallas_call(
        kernel,
        out_shape=[
            jax.ShapeDtypeStruct((depth, count, rows, width), pieces[0].dtype) for width in widths
        ],
        grid_spec=pltpu.PrefetchScalarGridSpec(
            num_scalar_prefetch=1,
            grid=(count, depth),
            in_specs=[pl.BlockSpec(p.shape, lambda i, j, at: (0, 0, 0)) for p in pieces]
            + [pl.BlockSpec((1, rows, width), lambda i, j, at: (at[i], 0, 0)) for width in widths],
            out_specs=[
                pl.BlockSpec(
                    (1, 1, rows, width),
                    lambda i, j, at: (at[count + j], at[i], 0, 0),
                )
                for width in widths
            ],
        ),
        compiler_params=pltpu.CompilerParams(vmem_limit_bytes=40 * 2**20),
    )(positions, *pieces, *shards)


def rest(x, level):
    depth = x.shape[0]
    block = (1,) + x.shape[1:]
    zeros = (0,) * (x.ndim - 1)

    def kernel(level_ref, source, target):
        target[...] = source[...]

    return pl.pallas_call(
        kernel,
        out_shape=jax.ShapeDtypeStruct((depth - 1,) + x.shape[1:], x.dtype),
        grid_spec=pltpu.PrefetchScalarGridSpec(
            num_scalar_prefetch=1,
            grid=(depth - 1,),
            in_specs=[
                pl.BlockSpec(block, lambda i, at: (lax.rem(at[0] + i + 1, depth), *zeros))
            ],
            out_specs=pl.BlockSpec(block, lambda i, at: (i, *zeros)),
        ),
    )(level[None], x)


def spread(pieces, positions, shape, place):
    count = len(pieces)
    rows, width = pieces[0].shape

    def kernel(positions_ref, *refs):
        for at in range(count):

            @pl.when(pl.program_id(0) == at)
            def take():
                refs[-1][...] = refs[at][...].astype(jnp.float32)

    return pl.pallas_call(
        kernel,
        out_shape=jax.ShapeDtypeStruct(shape, jnp.float32),
        grid_spec=pltpu.PrefetchScalarGridSpec(
            num_scalar_prefetch=1,
            grid=(count,),
            in_specs=[pl.BlockSpec((rows, width), lambda i, at: (0, 0))] * count,
            out_specs=pl.BlockSpec((rows, width), lambda i, at: place(at[i])),
        ),
        compiler_params=pltpu.CompilerParams(vmem_limit_bytes=40 * 2**20),
    )(positions, *pieces)


GELU_SCALE = 0.7978845608028654
GELU_CUBE = 0.044715


def dot_first(a, b):
    return lax.dot_general(a, b, (((0,), (0,)), ((), ())), preferred_element_type=jnp.float32)


def feed(facts, x, grad, first_w, second_w, shard, down_pieces, down_shard, block_sum, back_sum, terms):
    rows, width = x.shape
    hidden = first_w.shape[1]
    half = hidden // 2
    column = width // 4
    depth = down_pieces[0].shape[0] + 1
    level_rows = width // depth
    full = depth * hidden
    started = back_sum is not None
    pieces = 8
    f32, bf16 = jnp.float32, jnp.bfloat16

    def kernel(facts_ref, x_ref, g_ref, *refs):
        wa_in, wb_in, shard_in, down_in, block_in = refs[:5]
        down_pieces_in = refs[5 : 5 + pieces]
        refs = refs[5 + pieces :]
        if started:
            back_in = refs[0]
            refs = refs[1 + pieces :]
        block_out, back_out, ga_out, gb_out = refs[:4]
        term_out = refs[4 : 4 + pieces]
        wa, wb, wd, a, b, d, act, da, db, block, back, ga, gb, gd, sems = refs[4 + pieces :]
        chip = facts_ref[1]
        core, level = facts_ref[2], facts_ref[7]

        def rows_of(source, target, side, sem):
            copies = []
            for i in range(1, depth):
                place = pl.multiple_of(lax.rem(level + i, depth) * level_rows, 16)
                copies.append(
                    pltpu.make_async_copy(
                        source.at[pl.ds((i - 1) * level_rows, level_rows)],
                        target.at[pl.ds(place, level_rows)],
                        sem,
                    )
                )
            place = pl.multiple_of(level * level_rows, 16)
            start = pl.multiple_of(side * full + chip * hidden, 128)
            copies.append(
                pltpu.make_async_copy(
                    shard_in.at[:, pl.ds(start, hidden)],
                    target.at[pl.ds(place, level_rows)],
                    sem,
                )
            )
            return copies

        for copy in rows_of(wa_in, wa, core, sems.at[0]):
            copy.start()
        for copy in rows_of(wb_in, wb, 1 - core, sems.at[1]):
            copy.start()

        @pl.when(chip == level)
        def here():
            pltpu.make_async_copy(down_in, wd, sems.at[2]).start()

        @pl.when(chip != level)
        def elsewhere():
            step = lax.rem(chip - level + depth - 1, depth)
            for i in range(pieces):
                side = jnp.where(i < 4, core, 1 - core)
                pltpu.make_async_copy(
                    down_pieces_in[i].at[step],
                    wd.at[
                        pl.ds(pl.multiple_of(side * half, 16), half),
                        pl.ds(pl.multiple_of(facts_ref[3 + i % 4] * column, 128), column),
                    ],
                    sems.at[2],
                ).start()

        load_block = pltpu.make_async_copy(block_in, block, sems.at[3])
        load_block.start()
        if started:
            load_back = pltpu.make_async_copy(back_in, back, sems.at[4])
            load_back.start()
        pltpu.make_async_copy(wa, wa, sems.at[0]).wait()
        a[...] = dot(x_ref[...], wa[...])
        pltpu.make_async_copy(wb, wb, sems.at[1]).wait()
        b[...] = dot(x_ref[...], wb[...])
        pltpu.make_async_copy(wd, wd, sems.at[2]).wait()
        d[...] = dot_last(g_ref[...], wd[...])
        swapped = facts_ref[0] == 1

        @pl.loop(0, rows // 16)
        def glu(i):
            part = pl.ds(pl.multiple_of(i * 16, 16), 16)
            for j in range(hidden // 384):
                lanes = slice(j * 384, (j + 1) * 384)
                one, two, slope = a[part, lanes], b[part, lanes], d[part, lanes]
                gate = jnp.where(swapped, two, one)
                up = jnp.where(swapped, one, two)
                square = gate * gate
                inner = gate * (square * (GELU_SCALE * GELU_CUBE) + GELU_SCALE)
                share = 0.5 * jnp.tanh(inner) + 0.5
                gelu = gate * share
                bend = square * (6.0 * GELU_SCALE * GELU_CUBE) + 2.0 * GELU_SCALE
                rise = share + gelu * (1.0 - share) * bend
                d_gate = (slope * up) * rise
                d_up = slope * gelu
                act[part, lanes] = (gelu * up).astype(bf16)
                da[part, lanes] = jnp.where(swapped, d_up, d_gate).astype(bf16)
                db[part, lanes] = jnp.where(swapped, d_gate, d_up).astype(bf16)

        for i in range(width // 384):
            part = pl.ds(i * 384, 384)
            gb[part, :] = dot_first(x_ref[:, i * 384 : (i + 1) * 384], db[...]).astype(bf16)
            pltpu.make_async_copy(gb.at[part], gb_out.at[part], sems.at[5]).start()
        for i in range(width // 384):
            part = pl.ds(i * 384, 384)
            ga[part, :] = dot_first(x_ref[:, i * 384 : (i + 1) * 384], da[...]).astype(bf16)
            pltpu.make_async_copy(ga.at[part], ga_out.at[part], sems.at[6]).start()
        for i in range(hidden // 384):
            part = pl.ds(i * 384, 384)
            gd[part, :] = dot_first(act[:, i * 384 : (i + 1) * 384], g_ref[...]).astype(bf16)
        stores = []
        for i in range(pieces):
            side = jnp.where(i < 4, core, 1 - core)
            stores.append(
                pltpu.make_async_copy(
                    gd.at[
                        pl.ds(pl.multiple_of(side * half, 16), half),
                        pl.ds(pl.multiple_of(facts_ref[3 + i % 4] * column, 128), column),
                    ],
                    term_out[i].at[chip],
                    sems.at[7 + i],
                )
            )
        for store in stores:
            store.start()
        if started:
            load_back.wait()

            back[...] += dot_last(da[...], wa[...])
            back[...] += dot_last(db[...], wb[...])
        else:
            back[...] = dot_last(da[...], wa[...])
            back[...] += dot_last(db[...], wb[...])
        store_back = pltpu.make_async_copy(back, back_out, sems.at[15])
        store_back.start()
        load_block.wait()
        for i in range(2):
            part = pl.ds(i * (rows // 2), rows // 2)
            block[part, :] += dot(act[part, :], wd[...])
            pltpu.make_async_copy(block.at[part], block_out.at[part], sems.at[16]).start()
        for store in stores:
            store.wait()
        pltpu.make_async_copy(gb, gb_out, sems.at[5]).wait()
        pltpu.make_async_copy(ga, ga_out, sems.at[6]).wait()
        store_back.wait()
        pltpu.make_async_copy(block, block_out, sems.at[16]).wait()

    anywhere = pl.BlockSpec(memory_space=pl.ANY)
    inside = pl.BlockSpec(memory_space=pltpu.VMEM)
    operands = [facts, x, grad, first_w, second_w, shard, down_shard, block_sum, *down_pieces]
    aliases = {7: 0}
    if started:
        aliases[len(operands)] = 1
        operands.append(back_sum)
        for i, term in enumerate(terms):
            aliases[len(operands)] = 4 + i
            operands.append(term)
    sums = jax.ShapeDtypeStruct((rows, width), f32)
    grads = jax.ShapeDtypeStruct((width, hidden), bf16)
    results = pl.pallas_call(
        kernel,
        in_specs=[pl.BlockSpec(memory_space=pltpu.SMEM), inside, inside]
        + [anywhere] * (len(operands) - 3),
        out_specs=[anywhere] * (4 + pieces),
        out_shape=[sums, sums, grads, grads]
        + [jax.ShapeDtypeStruct((depth, half, column), bf16)] * pieces,
        input_output_aliases=aliases,
        scratch_shapes=[
            pltpu.VMEM((width, hidden), bf16),
            pltpu.VMEM((width, hidden), bf16),
            pltpu.VMEM((hidden, width), bf16),
            pltpu.VMEM((rows, hidden), f32),
            pltpu.VMEM((rows, hidden), f32),
            pltpu.VMEM((rows, hidden), f32),
            pltpu.VMEM((rows, hidden), bf16),
            pltpu.VMEM((rows, hidden), bf16),
            pltpu.VMEM((rows, hidden), bf16),
            pltpu.VMEM((rows, width), f32),
            pltpu.VMEM((rows, width), f32),
            pltpu.VMEM((width, hidden), bf16),
            pltpu.VMEM((width, hidden), bf16),
            pltpu.VMEM((hidden, width), bf16),
            pltpu.SemaphoreType.DMA((17,)),
        ],
        compiler_params=pltpu.CompilerParams(vmem_limit_bytes=56 * 2**20),
        cost_estimate=pl.CostEstimate(
            flops=9 * 2 * rows * width * hidden,
            bytes_accessed=40 * 2**20,
            transcendentals=rows * hidden,
        ),
    )(*operands)
    return results[0], results[1], results[2], results[3], results[4:]


class Plane:
    def __init__(self):
        self.me = lax.axis_index("seq")
        self.core = self.me % 2
        self.chip = self.me // 2
        first = jnp.where(self.core == 0, 1, 2)
        self.chips = [self.chip, self.chip ^ first, self.chip ^ (3 - first), self.chip ^ 3]
        self.first_pairs = [(i, i ^ (2 if i % 2 == 0 else 4)) for i in range(8)]
        self.second_pairs = [(i, i ^ (4 if i % 2 == 0 else 2)) for i in range(8)]
        self.core_pairs = [(i, i ^ 1) for i in range(8)]
        self.sources = jnp.stack(
            [chip * 2 + self.core for chip in self.chips]
            + [chip * 2 + 1 - self.core for chip in self.chips]
        )

    def first(self, x):
        return lax.ppermute(x, "seq", self.first_pairs)

    def second(self, x):
        return lax.ppermute(x, "seq", self.second_pairs)

    def along(self, x):
        depth = lax.axis_size("fsdp")
        return [
            lax.ppermute(x, "fsdp", [((i + k) % depth, i) for i in range(depth)])
            for k in range(1, depth)
        ]

    def swap(self, x):
        return lax.ppermute(x, "seq", self.core_pairs)

    def gather(self, piece):
        u = self.first(piece)
        v = self.second(piece)
        d = self.second(u)
        return [piece, u, v, d], [self.swap(piece), self.swap(v), self.swap(u), self.swap(d)]

    def merge(self, own, other):
        swaps = [self.swap(term) for term in other]
        from_d = self.second(added(own[3], swaps[3]))
        from_v = self.second(added(own[2], swaps[1]))
        from_u = self.first(added(own[1], swaps[2], from_d))
        return added(own[0], swaps[0], from_v, from_u)

    def down_columns(self, x):
        return lax.psum_scatter(x, "fsdp", scatter_dimension=0, tiled=True)


def places_of(arrival_order, ranks):
    row_count = arrival_order.shape[1]
    capacity = 2 * row_count // ranks
    arrived_at = arrival_order[0]
    owner = arrived_at // row_count
    owner_hits = (owner[:, None] == jnp.arange(ranks, dtype=jnp.int32)[None, :]).astype(jnp.int32)
    within = jnp.sum(jnp.cumsum(owner_hits, axis=0) * owner_hits, axis=1) - 1
    return owner * capacity + within, arrived_at % row_count


def to_slots(rows, slots, ranks, empty=0):
    capacity = 2 * rows.shape[0] // ranks
    out = jnp.full((ranks * capacity,) + rows.shape[1:], empty, rows.dtype)
    return out.at[slots].set(rows).reshape((ranks, capacity) + rows.shape[1:])


def from_slots(slots, landing):
    flat = slots.reshape((-1, slots.shape[-1]))
    out = jnp.zeros((flat.shape[0] // 2, flat.shape[1]), flat.dtype)
    return out.at[landing].set(flat, mode="drop")


def back_to_slots(rows, is_live, safe_place, ranks):
    chosen = jnp.where(is_live[:, None], rows[safe_place], jnp.zeros((), rows.dtype))
    return chosen.reshape(ranks, -1, rows.shape[1])


def exchange(x):
    return lax.all_to_all(x, "seq", split_axis=0, concat_axis=0, tiled=True)


def positions_of(lengths, row_count):
    position = lax.axis_index("seq")
    places = position * row_count + jnp.arange(row_count, dtype=jnp.int32)
    doc_query, offset_query = layout(lengths[0], places)
    key_places = (
        position * row_count - WINDOW + jnp.arange(WINDOW + row_count, dtype=jnp.int32)
    )
    doc_key, unused_offset = layout(lengths[0], key_places)
    cosine, sine = angles(offset_query.astype(jnp.float32), HD)
    return (doc_query[None, :], doc_key[:, None]), cosine, sine


def pair_of(kv_lin, cosine, sine):
    own_keys = rounded(rotate(kv_lin[:, :HD], cosine, sine))
    return jnp.concatenate([own_keys, rounded(kv_lin[:, HD:])], axis=1)


def with_earlier(pair, reach):
    return jnp.concatenate(
        [passed_along(pair, "seq", distance) for distance in range(reach, 0, -1)] + [pair], axis=0
    )


def owners_sum(d_pairs, row_count, reach):
    parts = [
        passed_along(
            rounded(d_pairs[(reach - distance) * row_count :][:row_count]), "seq", -distance
        )
        for distance in range(reach, 0, -1)
    ]
    own = d_pairs[reach * row_count :]
    for part in parts:
        own = own + widened(part)
    return own


def body(*operands):
    return square_body(*operands) if lax.axis_size("seq") == 8 else plain_body(*operands)


def plain_body(
    tokens,
    cotangent,
    arrival_order,
    lengths,
    norm_gain,
    w_query,
    w_kv,
    w_out,
    ffn_gain,
    w_gate_up,
    w_down,
):
    row_count = tokens.shape[1]
    ranks = lax.axis_size("seq")
    reach = WINDOW // row_count
    position = lax.axis_index("seq")

    def whole(shard):
        part = shard.shape[0] // ranks
        mine = lax.dynamic_slice_in_dim(shard, position * part, part, axis=0)
        return lax.all_gather(mine, ("fsdp", "seq"), axis=0, tiled=True)

    def summed(grad):
        mine = lax.psum_scatter(rounded(grad), ("fsdp", "seq"), scatter_dimension=0, tiled=True)
        return widened(lax.all_gather(mine, "seq", axis=0, tiled=True))

    send_slot, send_place = places_of(arrival_order, ranks)
    got_tokens = exchange(to_slots(tokens[0], send_slot, ranks))
    got_cotangent = exchange(to_slots(cotangent[0], send_slot, ranks))
    recv_place = exchange(to_slots(send_place, send_slot, ranks, -1)).reshape(-1)
    is_live = recv_place >= 0
    landing = jnp.where(is_live, recv_place, row_count)
    safe_place = jnp.where(is_live, recv_place, 0)
    packed_f = widened(from_slots(got_tokens, landing))
    packed_grad = from_slots(got_cotangent, landing)
    query_w, kv_w, out_w, down_w, gate_up_w = (
        whole(w_query),
        whole(w_kv),
        whole(w_out),
        whole(w_down),
        whole(w_gate_up),
    )
    gain_attn, gain_ffn = (
        widened(lax.all_gather(gain, "fsdp", axis=0, tiled=True)) for gain in (norm_gain, ffn_gain)
    )
    docs, cosine, sine = positions_of(lengths, row_count)
    tables = tables_of(cosine, sine, 2, 0)

    normed = rounded(rms_scale(packed_f, gain_attn))
    pair_rows = with_earlier(pair_of(dot(normed, kv_w), cosine, sine), reach)
    queries, mixed, totals = attend(dot(normed, query_w), tables, pair_rows, pair_rows.T, *docs)
    hidden_state = packed_f + dot(mixed, out_w)
    ffn_in = rounded(rms_scale(hidden_state, gain_ffn))
    gate, up = dot(ffn_in, gate_up_w[:, :FF]), dot(ffn_in, gate_up_w[:, FF:])
    activated, pull = jax.vjp(lambda g, u: jax.nn.gelu(g, approximate=True) * u, gate, up)
    activated = rounded(activated)
    block_rows = rounded(hidden_state + dot(activated, down_w))

    d_gate, d_up = pull(dot_across(packed_grad, down_w))
    d_gate_up = jnp.concatenate([rounded(d_gate), rounded(d_up)], axis=1)
    unused_scaled, ffn_norm_pull = jax.vjp(rms_scale, hidden_state, gain_ffn)
    d_hidden_norm, grad_gain_ffn = ffn_norm_pull(dot_across(d_gate_up, gate_up_w))
    d_hidden = widened(packed_grad) + d_hidden_norm
    d_branch = rounded(d_hidden)
    d_mixed = rounded(dot_across(d_branch, out_w))
    d_query_lin, d_pairs = attend_back(
        queries, d_mixed, totals, tables, pair_rows, pair_rows.T, *docs
    )
    d_own = owners_sum(d_pairs, row_count, reach)
    d_kv_lin = rounded(
        jnp.concatenate([unrotate(d_own[:, :HD], cosine, sine), d_own[:, HD:]], axis=1)
    )
    d_normed = dot_across(d_query_lin, query_w) + dot_across(d_kv_lin, kv_w)
    unused_normed, attn_norm_pull = jax.vjp(rms_scale, packed_f, gain_attn)
    d_packed_norm, grad_gain_attn = attn_norm_pull(d_normed)
    grad_rows = rounded(d_hidden + d_packed_norm)
    block_arrived, grad_arrived = (
        exchange(back_to_slots(rows, is_live, safe_place, ranks)).reshape(-1, rows.shape[1])[
            send_slot
        ]
        for rows in (block_rows, grad_rows)
    )
    total_gain_attn, total_gain_ffn = (
        lax.psum(lax.psum_scatter(gain, "fsdp", scatter_dimension=0, tiled=True), "seq")
        for gain in (grad_gain_attn, grad_gain_ffn)
    )
    return (
        block_arrived[None],
        grad_arrived[None],
        total_gain_attn,
        summed(dot_rows(normed, d_query_lin)),
        summed(dot_rows(normed, d_kv_lin)),
        summed(dot_rows(mixed, d_branch)),
        total_gain_ffn,
        summed(dot_rows(ffn_in, d_gate_up)),
        summed(dot_rows(activated, packed_grad)),
    )


def square_body(
    tokens,
    cotangent,
    arrival_order,
    lengths,
    norm_gain,
    w_query,
    w_kv,
    w_out,
    ffn_gain,
    w_gate_up,
    w_down,
):
    row_count = tokens.shape[1]
    model_width = tokens.shape[2]
    ranks = lax.axis_size("seq")
    depth = lax.axis_size("fsdp")
    reach = WINDOW // row_count
    shard_rows = w_query.shape[0]
    part_rows = shard_rows // ranks
    quarter = FF // 4
    column = model_width // 4
    half_rows = w_down.shape[0] // 2
    split = model_width + 2 * HD
    plane = Plane()
    level = lax.axis_index("fsdp").astype(jnp.int32)
    levels = (level + 1 + jnp.arange(depth, dtype=jnp.int32)) % depth
    at = jnp.concatenate([plane.sources, levels]).astype(jnp.int32)

    def my_rows(shard):
        return lax.dynamic_slice_in_dim(shard, plane.me * part_rows, part_rows, axis=0)

    def by_parts(shard):
        return shard.reshape(ranks, part_rows, shard.shape[1])

    gains = jnp.pad(jnp.stack([norm_gain, ffn_gain]), ((0, 14), (0, 0)))
    early = plane.along(jnp.concatenate([my_rows(w_query), my_rows(w_kv)], axis=1))
    other_gains = plane.along(gains)
    send_slot, send_place = places_of(arrival_order, ranks)
    place_slots = to_slots(send_place, send_slot, ranks, -1)
    token_slots = to_slots(tokens[0], send_slot, ranks)
    cotangent_slots = to_slots(after(cotangent[0], token_slots), send_slot, ranks)
    got_place = exchange(place_slots)
    got_tokens = exchange(token_slots)
    early = jnp.stack(after_all(early, cotangent_slots))
    own, other = plane.gather(early)
    got_cotangent = exchange(after(cotangent_slots, early))
    down_piece = lax.dynamic_slice(
        after(w_down, early), (plane.core * half_rows, plane.chip * column), (half_rows, column)
    )
    down_piece = lax.all_gather(down_piece, "fsdp", axis=0, tiled=False)
    gate_up_piece = lax.dynamic_slice(
        after(w_gate_up, early),
        (0, plane.core * FF + plane.chip * quarter),
        (shard_rows, quarter),
    )
    gate_up_piece = lax.all_gather(gate_up_piece, "fsdp", axis=0, tiled=False)
    out_piece = plane.along(after(my_rows(w_out), early))

    recv_place = got_place.reshape(-1)
    is_live = recv_place >= 0
    landing = jnp.where(is_live, recv_place, row_count)
    safe_place = jnp.where(is_live, recv_place, 0)
    packed_f = widened(from_slots(got_tokens, landing))
    gain_rows = jnp.concatenate([jnp.stack(other_gains), gains[None]], axis=0)[:, :2]
    gain_rows = gain_rows[(jnp.arange(depth, dtype=jnp.int32) + depth - 1 - level) % depth]
    gain_attn = widened(gain_rows[:, 0].reshape(model_width))
    gain_ffn = widened(gain_rows[:, 1].reshape(model_width))
    docs, cosine, sine = positions_of(lengths, row_count)
    tables = tables_of(cosine, sine, 2, 0)
    normed = rounded(rms_scale(packed_f, gain_attn))

    query_w, kv_w = put_pieces(own + other, at, [by_parts(w_query), by_parts(w_kv)])
    query_w = query_w.reshape(model_width, model_width)
    kv_w = kv_w.reshape(model_width, 2 * HD)
    pair = pair_of(dot(normed, kv_w), cosine, sine)
    query_lin = dot(after(normed, pair), query_w)
    out_own, out_other = plane.gather(jnp.stack(after_all(out_piece, own[3])))
    packed_grad = from_slots(after(got_cotangent, pair), landing)
    down_piece = rest(after(down_piece, pair), level)
    down_own, down_other = plane.gather(down_piece)
    down_pieces = down_own + down_other
    pair_rows = with_earlier(pair, reach)
    pairs_across = pair_rows.T
    queries, mixed, totals = attend(
        after(query_lin, packed_grad, down_piece), tables, pair_rows, pairs_across, *docs
    )
    (out_w,) = put_pieces(out_own + out_other, after(at, mixed), [by_parts(w_out)])
    out_w = out_w.reshape(model_width, model_width)
    hidden_state = packed_f + dot(mixed, out_w)
    ffn_in = rounded(rms_scale(hidden_state, gain_ffn))

    gate_up_piece = rest(after(gate_up_piece, ffn_in), level)
    first_ws, second_ws = plane.gather(gate_up_piece.reshape((depth - 1) * shard_rows, quarter))
    block_sum, d_ffn_in, terms = hidden_state, None, None
    firsts, swaps = [], []
    chunk_in = ffn_in
    for slot in range(4):
        if slot >= 2:
            chunk_in = after(chunk_in, swaps[slot - 2])
        facts = [plane.core, plane.chips[slot], plane.core, *plane.chips, level]
        block_sum, d_ffn_in, first_grad, second_grad, terms = feed(
            jnp.stack(facts).astype(jnp.int32),
            chunk_in,
            packed_grad,
            first_ws[slot],
            second_ws[slot],
            w_gate_up,
            down_pieces,
            w_down,
            block_sum,
            d_ffn_in,
            terms,
        )
        firsts.append(first_grad)
        swaps.append(plane.swap(second_grad))
        if slot == 2:
            sum_v = added(firsts[2], swaps[1])
            from_v = plane.second(sum_v)
            chunk_in = after(chunk_in, sum_v)

    terms = [term.reshape(depth * half_rows, column) for term in terms]
    down_swaps = [plane.swap(term) for term in terms[4:]]
    unused_scaled, ffn_norm_pull = jax.vjp(rms_scale, hidden_state, gain_ffn)
    d_hidden_norm, grad_gain_ffn = ffn_norm_pull(d_ffn_in)
    d_hidden = widened(packed_grad) + d_hidden_norm
    d_branch = rounded(d_hidden)
    d_mixed = rounded(dot_across(d_branch, out_w))
    sum_d = added(after(firsts[3], d_mixed), swaps[3])
    from_d = plane.second(sum_d)
    down_sums = [
        added(after(term, sum_d), down_swaps[match])
        for term, match in zip(terms[:4], (0, 2, 1, 3))
    ]
    from_down_d, from_down_v = plane.second(down_sums[3]), plane.second(down_sums[2])
    d_query_lin, d_pairs = attend_back(
        queries, after(d_mixed, *down_sums), totals, tables, pair_rows, pairs_across, *docs
    )
    d_own = owners_sum(d_pairs, row_count, reach)
    sum_u = added(after(firsts[1], d_pairs), swaps[2], from_d)
    from_u = plane.first(sum_u)
    grad_out = dot_rows(mixed, after(d_branch, sum_u))
    grad_query = dot_rows(normed, after(d_query_lin, sum_u))
    block_rows = rounded(after(block_sum, sum_u))
    home_out = exchange(back_to_slots(block_rows, is_live, safe_place, ranks))
    down_u = added(after(down_sums[1], grad_query), from_down_d)
    from_down_u = plane.first(down_u)
    d_kv_lin = rounded(
        jnp.concatenate([unrotate(d_own[:, :HD], cosine, sine), d_own[:, HD:]], axis=1)
    )
    d_kv_lin = after(d_kv_lin, down_u)
    grad_kv = dot_rows(normed, d_kv_lin)
    d_normed = dot_across(d_query_lin, query_w) + dot_across(d_kv_lin, kv_w)
    unused_normed, attn_norm_pull = jax.vjp(rms_scale, packed_f, gain_attn)
    d_packed_norm, grad_gain_attn = attn_norm_pull(d_normed)
    grad_rows = rounded(d_hidden + d_packed_norm)
    home_grad = exchange(back_to_slots(grad_rows, is_live, safe_place, ranks))

    total = added(after(firsts[0], grad_rows), swaps[0], from_v, from_u)
    mine_gate_up = plane.down_columns(total)

    def by_rows(grad):
        pieces = rounded(grad).reshape(depth, ranks, part_rows, grad.shape[1])
        return [
            lax.dynamic_index_in_dim(pieces, plane.sources[i], axis=1, keepdims=False)
            for i in range(8)
        ]

    gain_rows = jnp.concatenate(
        [
            rounded(grad_gain_attn).reshape(depth, 1, shard_rows),
            rounded(grad_gain_ffn).reshape(depth, 1, shard_rows),
        ],
        axis=2,
    )
    gain_rows = jnp.pad(gain_rows, ((0, 0), (0, 15), (0, split - 2 * shard_rows)))
    pieces = [
        jnp.concatenate([jnp.concatenate([q, k], axis=2), gain_rows], axis=1).reshape(
            depth * (part_rows + 16), split
        )
        for q, k in zip(by_rows(grad_query), by_rows(grad_kv))
    ]
    mine_early = plane.down_columns(plane.merge(pieces[:4], pieces[4:]))
    total = added(down_sums[0], from_down_v, from_down_u)
    mine_down = plane.down_columns(total)
    pieces = [p.reshape(depth * part_rows, model_width) for p in by_rows(grad_out)]
    mine_out = plane.down_columns(plane.merge(pieces[:4], pieces[4:]))

    def everywhere(mine, rows, width, place):
        own, other = plane.gather(mine)
        return spread(own + other, plane.sources, (rows, width), place)

    total_gate_up = everywhere(
        mine_gate_up, shard_rows, 2 * FF, lambda p: (0, (p % 2) * 4 + p // 2)
    )
    total_down = everywhere(
        mine_down, 2 * half_rows, model_width, lambda p: (p % 2, p // 2)
    )
    total_out = everywhere(mine_out, shard_rows, model_width, lambda p: (p, 0))
    total_early = everywhere(mine_early[:part_rows], shard_rows, split, lambda p: (p, 0))
    block_arrived = home_out.reshape(-1, model_width)[send_slot]
    grad_arrived = home_grad.reshape(-1, model_width)[send_slot]
    return (
        block_arrived[None],
        grad_arrived[None],
        widened(mine_early[part_rows, :shard_rows]),
        total_early[:, :model_width],
        total_early[:, model_width:],
        total_out,
        widened(mine_early[part_rows, shard_rows : 2 * shard_rows]),
        total_gate_up,
        total_down,
    )


def solution(mesh):
    placed = (
        P("fsdp", "seq", None),
        P("fsdp", "seq", None),
        P("fsdp", "seq"),
        P("fsdp", None),
        P("fsdp"),
        P("fsdp", None),
        P("fsdp", None),
        P("fsdp", None),
        P("fsdp"),
        P("fsdp", None),
        P("fsdp", None),
    )
    return jax.shard_map(
        body,
        mesh=mesh,
        in_specs=placed,
        out_specs=(
            P("fsdp", "seq", None),
            P("fsdp", "seq", None),
            P("fsdp"),
            P("fsdp", None),
            P("fsdp", None),
            P("fsdp", None),
            P("fsdp"),
            P("fsdp", None),
            P("fsdp", None),
        ),
        check_vma=False,
    )
```

time: 1490 us -> 924 us (0.62)
  waiting for transfers between devices: 943 us -> 343 us
  Pallas kernels: 0 us -> 201 us
  matrix products: 230 us -> 32.5 us
  blocking collectives: 123 us -> 0 us
  starting transfers between devices: 28 us -> 119 us
  local copies, waits for them, and re-layouts: 71.1 us -> 121 us
    reduce_scatter x5 -> x4, waiting for transfers between devices: 528 us -> 0.03 us  [down_columns(): return lax.psum_scatter(x, 'fsdp', scatter_dimension=0, tiled=True)]
    all_gather x9 -> x2, waiting for transfers between devices: 371 us -> 0.01 us  [the longest x1 0.01 us: square_body(): down_piece = lax.all_gather(down_piece, 'fsdp', axis=0, tiled=False)]
    ppermute x0 -> x93, waiting for transfers between devices: none -> 309 us  [the longest x24 178 us: second(): return lax.ppermute(x, 'seq', self.second_pairs)]
    pallas_call x0 -> x14, Pallas kernels: none -> 201 us  [the longest x4 115 us: feed(): pl.pallas_call(kernel, in_specs=[pl.BlockSpec(memory_space=pltpu.SMEM), i...]
    dot_general x21 -> x9, matrix products: 230 us -> 32.5 us  [the longest x3 11.6 us: dot_rows(): return jnp.einsum('td,tf->df', a, b, preferred_element_type=jnp.float32)]
    ppermute x0 -> x93, starting transfers between devices: none -> 88.3 us  [the longest x24 28.4 us: second(): return lax.ppermute(x, 'seq', self.second_pairs)]
    all_to_all x1 -> x0, blocking collectives: 44 us -> none  [body(): lax.all_to_all(to_owner(grad_rows), 'seq', split_axis=0, concat_axis=0, t...]
    all_gather x3 -> x0, blocking collectives: 33.7 us -> none  [the longest x1 12.1 us: body(): lax.all_gather(ffn_gain, 'fsdp', axis=0, tiled=True)]
  transfers between devices with their start and end apart: 22 -> 108, of which waited for: 13 -> 30; matrix products, arithmetic and copies ran while one was open for 19% -> 21% of each run, Pallas kernels for 0% -> 18%
where the time goes in v2:
time: 924 us; the launch traced here: 913 us
  waiting for transfers between devices  343 us (37%)
  Pallas kernels  201 us (22%)
  local copies, waits for them, and re-layouts  121 us (13%)
  starting transfers between devices  119 us (13%)
  other arithmetic  80.4 us (9%)
  matrix products  32.5 us (4%)
  between operations  15.8 us (2%)
    ppermute x24, waiting for transfers between devices, second(): return lax.ppermute(x, 'seq', self.second_pairs)  178 us
    pallas_call x4, Pallas kernels, feed(): pl.pallas_call(kernel, in_specs=[pl.BlockSpec(memory_space=pltpu.SMEM), i...  115 us
    ppermute x12, waiting for transfers between devices, first(): return lax.ppermute(x, 'seq', self.first_pairs)  107 us
    convert_element_type x23, other arithmetic, rounded(): return x.astype(jnp.bfloat16)  55.1 us
    unnamed x222, local copies, waits for them, and re-layouts  38.2 us
    ppermute x24, starting transfers between devices, second(): return lax.ppermute(x, 'seq', self.second_pairs)  28.4 us
    all_to_all x5, waiting for transfers between devices, exchange(): return lax.all_to_all(x, 'seq', split_axis=0, concat_axis=0, tiled=True)  27.5 us
    pallas_call x1, Pallas kernels, attend_back(): pl.pallas_call(kernel, grid=(rows // block, couples), in_specs=[tile, til...  25.6 us
  transfers between devices with their start and end apart: 108, of which 30 were waited for; matrix products, arithmetic and copies ran while one was open for 21% of the time, Pallas kernels for 18%

profile of v2, /device:TPU:0, one launch (start us, length us, event | category | flops | bytes accessed | tf_op | source)
XLA Modules:
  0.0 913.1 jit_solution(9779410134231352738)
XLA Ops:
  51.4 45.0 %collective-permute-done.6.refs_1_ = bf16[3,48,1920]{2,1,0:T(8,128)(2,1)} collective-permute-done((bf16[3,48,1920]{2,1,0:T(8,128)(2,1)S(1)}, bf16[3,48,1920]{2,1,0:T(8,128)(2,1)}, u32[]{:S(2)}, u32[]{:S(2)}) %collective-permute-start.6) | collective-permute-done | bytes 552992 | tf_op jit(solution)/shard_map/ppermute | solution.py:584
  143.9 7.5 scatter_custom_fusion.2
  170.4 7.1 fusion.83.q_ref
  180.7 7.8 scatter_custom_fusion.4.g_ref
  202.4 20.9 %shard_map.180 = (bf16[512,1536]{1,0:T(8,128)(2,1)}, bf16[512,1536]{1,0:T(8,128)(2,1)}, f32[4,2,512]{2,1,0:T(2,128)S(1)}) custom-call(f32[512,1536]{1,0:T(8,128)} %fusion.83.q_ref, f32[512,384]{1,0:T(8,128)S(1)} %copy-done.15, f32[512,384]{1,0:T(8,128)S(1)} %copy-done.17, f32[512,384]{1,0:T(8,128)S(1)} %copy-done.19, bf16[1536,384]{1,0:T(8,128)(2,1)S(1)} %copy-done.5, ...), custom_call_target="tpu_custom_call" | custom-call | flops 4026531840 | bytes 12582912 | tf_op jit(solution)/shard_map/pallas_call | solution.py:160
  244.2 41.5 %collective-permute-done.28.refs_8_ = bf16[3,576,384]{2,1,0:T(8,128)(2,1)} collective-permute-done((bf16[3,576,384]{2,1,0:T(8,128)(2,1)}, bf16[3,576,384]{2,1,0:T(8,128)(2,1)}, u32[]{:S(2)}, u32[]{:S(2)}) %collective-permute-start.28) | collective-permute-done | bytes 1327136 | tf_op jit(solution)/shard_map/ppermute | solution.py:587
  292.6 28.7 %shard_map.183 = (f32[512,1536]{1,0:T(8,128)}, f32[512,1536]{1,0:T(8,128)}, bf16[1536,1152]{1,0:T(8,128)(2,1)}, bf16[1536,1152]{1,0:T(8,128)(2,1)}, bf16[4,576,3...) custom-call(s32[8]{0:T(128)} %stack.154.facts_ref, ...), custom_call_target="tpu_custom_call", output_to_operand_aliasing={{0}: (7, {})} | custom-call | flops 16307453952 | bytes 41943040 | tf_op jit(solution)/shard_map/pallas_call | solution.py:533
  322.4 28.6 %shard_map.184 = (f32[512,1536]{1,0:T(8,128)}, f32[512,1536]{1,0:T(8,128)}, bf16[1536,1152]{1,0:T(8,128)(2,1)}, bf16[1536,1152]{1,0:T(8,128)(2,1)}, bf16[4,576,3...) custom-call(s32[8]{0:T(128)} %stack.156.facts_ref, ...), custom_call_target="tpu_custom_call", output_to_operand_aliasing={{0}: (7, {}), {1}: (16, {}), {4}: (17, {}), {5}: (18, {}), ... | custom-call | flops 16307453952 | bytes 41943040 | tf_op jit(solution)/shard_map/pallas_call | solution.py:533
  354.2 28.9 %shard_map.185 = (f32[512,1536]{1,0:T(8,128)}, f32[512,1536]{1,0:T(8,128)}, bf16[1536,1152]{1,0:T(8,128)(2,1)}, bf16[1536,1152]{1,0:T(8,128)(2,1)}, bf16[4,576,3...) custom-call(s32[8]{0:T(128)} %stack.155.facts_ref, ...), custom_call_target="tpu_custom_call", output_to_operand_aliasing={{0}: (7, {}), {1}: (16, {}), {4}: (17, {}), {5}: (18, {}), ... | custom-call | flops 16307453952 | bytes 41943040 | tf_op jit(solution)/shard_map/pallas_call | solution.py:533
  390.4 29.0 %shard_map.186 = (f32[512,1536]{1,0:T(8,128)}, f32[512,1536]{1,0:T(8,128)}, bf16[1536,1152]{1,0:T(8,128)(2,1)}, bf16[1536,1152]{1,0:T(8,128)(2,1)}, bf16[4,576,3...) custom-call(s32[8]{0:T(128)} %stack.131.facts_ref, ...), custom_call_target="tpu_custom_call", output_to_operand_aliasing={{0}: (7, {}), {1}: (16, {}), {4}: (17, {}), {5}: (18, {}), ... | custom-call | flops 16307453952 | bytes 41943040 | tf_op jit(solution)/shard_map/pallas_call | solution.py:533
  447.1 25.6 %shard_map.187 = (bf16[512,1536]{1,0:T(8,128)(2,1)}, f32[1536,384]{1,0:T(8,128)}) custom-call(bf16[512,1536]{1,0:T(8,128)(2,1)} %get-tuple-element.155.q_ref, bf16[512,1536]{1,0:T(8,128)(2,1)} %convolution_convert_fusion.1.do_ref, f32[4,2,512]{2,1,0:T(2,128)S(1)} %get-tuple-element.173.total_ref, f32[512,384]{1,0:T(8,128)S(1)} %copy-done.16, ...), custom_call_target="tpu_custom_call" | custom-call | flops 10066329600 | bytes 12582912 | tf_op jit(solution)/shard_map/pallas_call | solution.py:234
  482.2 6.9 collective-permute-done.48
  507.5 67.7 %collective-permute-done.50 = bf16[2304,384]{1,0:T(8,128)(2,1)S(1)} collective-permute-done((bf16[2304,384]{1,0:T(8,128)(2,1)}, bf16[2304,384]{1,0:T(8,128)(2,1)S(1)}, u32[]{:S(2)}, u32[]{:S(2)}) %collective-permute-start.50) | collective-permute-done | bytes 1769504 | tf_op jit(solution)/shard_map/ppermute | solution.py:587
  587.3 6.7 add_convert_fusion
  602.0 12.0 %collective-permute-start.66 = (bf16[192,1536]{1,0:T(8,128)(2,1)}, bf16[192,1536]{1,0:T(8,128)(2,1)}, u32[]{:S(2)}, u32[]{:S(2)}) collective-permute-start(bf16[192,1536]{1,0:T(8,128)(2,1)} %bitcast.103), channel_id=1, source_target_pairs={{0,4},{4,0},{8,12},{12,8},{16,20},{20,16},{24,28},{28,24},{1,5},{5... | collective-permute-start | bytes 1769480 | tf_op jit(solution)/shard_map/ppermute | solution.py:597
  638.9 17.6 %collective-permute-done.56 = bf16[256,1920]{1,0:T(8,128)(2,1)S(1)} collective-permute-done((bf16[256,1920]{1,0:T(8,128)(2,1)S(1)}, bf16[256,1920]{1,0:T(8,128)(2,1)S(1)}, u32[]{:S(2)}, u32[]{:S(2)}) %collective-permute-start.56) | collective-permute-done | bytes 983072 | tf_op jit(solution)/shard_map/ppermute | solution.py:587
  665.2 14.0 %collective-permute-done.53 = bf16[256,1920]{1,0:T(8,128)(2,1)} collective-permute-done((bf16[256,1920]{1,0:T(8,128)(2,1)}, bf16[256,1920]{1,0:T(8,128)(2,1)}, u32[]{:S(2)}, u32[]{:S(2)}) %collective-permute-start.53) | collective-permute-done | bytes 983072 | tf_op jit(solution)/shard_map/ppermute | solution.py:587
  710.1 7.0 collective-permute-done.88
  726.5 26.1 %all-to-all-done.4 = bf16[8,128,1536]{2,1,0:T(8,128)(2,1)S(1)} async-done(((bf16[8,128,1536]{2,1,0:T(8,128)(2,1)}), bf16[8,128,1536]{2,1,0:T(8,128)(2,1)S(1)}, u32[]{:S(2)}, u32[]{:S(2)}) %all-to-all-start.4) | async-done | bytes 3145760 | tf_op jit(solution)/shard_map/all_to_all | solution.py:644
  763.0 46.2 %collective-permute-done.72.refs_1_ = bf16[48,1536]{1,0:T(8,128)(2,1)S(1)} collective-permute-done((bf16[48,1536]{1,0:T(8,128)(2,1)}, bf16[48,1536]{1,0:T(8,128)(2,1)S(1)}, u32[]{:S(2)}, u32[]{:S(2)}) %collective-permute-start.72) | collective-permute-done | bytes 147488 | tf_op jit(solution)/shard_map/ppermute | solution.py:584
  836.6 20.9 %collective-permute-done.92.refs_3_ = bf16[576,384]{1,0:T(8,128)(2,1)} collective-permute-done((bf16[576,384]{1,0:T(8,128)(2,1)S(1)}, bf16[576,384]{1,0:T(8,128)(2,1)}, u32[]{:S(2)}, u32[]{:S(2)}) %collective-permute-start.92) | collective-permute-done | bytes 442400 | tf_op jit(solution)/shard_map/ppermute | solution.py:587
  860.8 6.7 gather_fusion.4
  867.5 6.7 gather_fusion.2
  897.5 8.5 shard_map.190
  (565 shorter events, 379.6 us)
Async XLA Ops:
  7.2 170.3 %all-gather.5.cloned.1.call-start = ((), (), s32[]{:S(2)}) async-start(), calls=%async_computation.13 | async-start | bytes 2211840 | tf_op jit(solution)/shard_map/all_gather | solution.py:837
  38.6 80.5 %collective-permute-start = (bf16[16,384]{1,0:T(8,128)(2,1)S(1)}, bf16[16,384]{1,0:T(8,128)(2,1)S(1)}, u32[]{:S(2)}, u32[]{:S(2)}) collective-permute-start(bf16[16,384]{1,0:T(8,128)(2,1)S(1)} %get-tuple-element.237), channel_id=1, source_target_pairs={{1,0},{2,1},{3,2},{0,3},{5,4},{6,5},{7,6},{4,7},{9,8},{10,9},{11,1... | collective-permute-start | bytes 36872 | tf_op jit(solution)/shard_map/ppermute | solution.py:592
  43.2 82.3 %all-to-all-start.1 = ((bf16[8,128,1536]{2,1,0:T(8,128)(2,1)}), bf16[8,128,1536]{2,1,0:T(8,128)(2,1)}, u32[]{:S(2)}, u32[]{:S(2)}) async-start(bf16[8,128,1536]{2,1,0:T(8,128)(2,1)} %bitcast.216), calls=%async_computation.1 | async-start | bytes 6291456 | tf_op jit(solution)/shard_map/all_to_all | solution.py:644
  47.6 187.5 %all-gather.7.cloned.1.call-start = ((), (), s32[]{:S(2)}) async-start(), calls=%async_computation.14 | async-start | bytes 4423680 | tf_op jit(solution)/shard_map/all_gather | solution.py:843
  49.9 69.7 %collective-permute-start.7 = (bf16[3,48,1920]{2,1,0:T(8,128)(2,1)S(1)}, bf16[3,48,1920]{2,1,0:T(8,128)(2,1)}, u32[]{:S(2)}, u32[]{:S(2)}) collective-permute-start(bf16[3,48,1920]{2,1,0:T(8,128)(2,1)S(1)} %pad_maximum_fusion.3.refs_0_), channel_id=1, source_target_pairs={{0,16},{4,12},{8,24},{12,4},{16,0},{20,28},{24,8},{28,20},{1,17},{... | collective-permute-start | bytes 1658888 | tf_op jit(solution)/shard_map/ppermute | solution.py:587
  125.4 55.3 %all-to-all-start.2 = ((bf16[8,128,1536]{2,1,0:T(8,128)(2,1)}), bf16[8,128,1536]{2,1,0:T(8,128)(2,1)}, u32[]{:S(2)}, u32[]{:S(2)}) async-start(bf16[8,128,1536]{2,1,0:T(8,128)(2,1)} %bitcast.215), calls=%async_computation.2 | async-start | bytes 6291456 | tf_op jit(solution)/shard_map/all_to_all | solution.py:644
  130.0 628.8 %reduce-scatter.9.cloned.1.call-start = ((), (), s32[]{:S(2)}) async-start(), calls=%async_computation.11 | async-start | bytes 4423680 | tf_op jit(solution)/shard_map/reduce_scatter | solution.py:613
  130.8 57.7 %collective-permute-start.19 = (bf16[3,48,1536]{2,1,0:T(8,128)(2,1)S(1)}, bf16[3,48,1536]{2,1,0:T(8,128)(2,1)}, u32[]{:S(2)}, u32[]{:S(2)}) collective-permute-start(bf16[3,48,1536]{2,1,0:T(8,128)(2,1)S(1)} %pad_maximum_fusion.4.refs_0_), channel_id=1, source_target_pairs={{0,16},{4,12},{8,24},{12,4},{16,0},{20,28},{24,8},{28,20},{1,17},{... | collective-permute-start | bytes 1327112 | tf_op jit(solution)/shard_map/ppermute | solution.py:587
  132.7 90.7 %collective-permute-start.21 = (bf16[3,48,1536]{2,1,0:T(8,128)(2,1)S(1)}, bf16[3,48,1536]{2,1,0:T(8,128)(2,1)}, u32[]{:S(2)}, u32[]{:S(2)}) collective-permute-start(bf16[3,48,1536]{2,1,0:T(8,128)(2,1)S(1)} %pad_maximum_fusion.4.refs_0_), channel_id=1, source_target_pairs={{0,4},{4,0},{8,12},{12,8},{16,20},{20,16},{24,28},{28,24},{1,5},{5... | collective-permute-start | bytes 1327112 | tf_op jit(solution)/shard_map/ppermute | solution.py:597
  132.9 56.0 %collective-permute-start.20 = (bf16[3,48,1536]{2,1,0:T(8,128)(2,1)}, bf16[3,48,1536]{2,1,0:T(8,128)(2,1)}, u32[]{:S(2)}, u32[]{:S(2)}) collective-permute-start(bf16[3,48,1536]{2,1,0:T(8,128)(2,1)} %collective-permute-done.18.refs_1_), channel_id=1, source_target_pairs={{0,16},{4,12},{8,24},{12,4},{16,0},{20,28},{24,8},{28,20},{1,17},{... | collective-permute-start | bytes 1327112 | tf_op jit(solution)/shard_map/ppermute | solution.py:587
  189.4 51.4 %collective-permute-start.26 = (bf16[3,576,384]{2,1,0:T(8,128)(2,1)}, bf16[3,576,384]{2,1,0:T(8,128)(2,1)}, u32[]{:S(2)}, u32[]{:S(2)}) collective-permute-start(bf16[3,576,384]{2,1,0:T(8,128)(2,1)} %shard_map.179.refs_5_), channel_id=1, source_target_pairs={{0,8},{4,20},{8,0},{12,28},{16,24},{20,4},{24,16},{28,12},{1,9},{5... | collective-permute-start | bytes 3981320 | tf_op jit(solution)/shard_map/ppermute | solution.py:584
  241.3 51.3 %collective-permute-start.25 = (bf16[1152,1152]{1,0:T(8,128)(2,1)}, bf16[1152,1152]{1,0:T(8,128)(2,1)}, u32[]{:S(2)}, u32[]{:S(2)}) collective-permute-start(bf16[1152,1152]{1,0:T(8,128)(2,1)} %bitcast.223), channel_id=1, source_target_pairs={{0,4},{4,0},{8,12},{12,8},{16,20},{20,16},{24,28},{28,24},{1,5},{5... | collective-permute-start | bytes 7962632 | tf_op jit(solution)/shard_map/ppermute | solution.py:597
  419.9 71.8 %collective-permute-start.46 = (bf16[1536,1152]{1,0:T(8,128)(2,1)}, bf16[1536,1152]{1,0:T(8,128)(2,1)}, u32[]{:S(2)}, u32[]{:S(2)}) collective-permute-start(bf16[1536,1152]{1,0:T(8,128)(2,1)} %get-tuple-element.176), channel_id=1, source_target_pairs={{0,4},{4,0},{8,12},{12,8},{16,20},{20,16},{24,28},{28,24},{1,5},{5... | collective-permute-start | bytes 10616840 | tf_op jit(solution)/shard_map/ppermute | solution.py:597
  437.8 53.9 %collective-permute-start.47 = (bf16[1536,1152]{1,0:T(8,128)(2,1)}, bf16[1536,1152]{1,0:T(8,128)(2,1)}, u32[]{:S(2)}, u32[]{:S(2)}) collective-permute-start(bf16[1536,1152]{1,0:T(8,128)(2,1)} %add_convert_fusion.2), channel_id=1, source_target_pairs={{0,16},{4,12},{8,24},{12,4},{16,0},{20,28},{24,8},{28,20},{1,17},{... | collective-permute-start | bytes 10616840 | tf_op jit(solution)/shard_map/ppermute | solution.py:587
  477.9 109.4 %collective-permute-start.79 = (bf16[1536,1152]{1,0:T(8,128)(2,1)S(1)}, bf16[1536,1152]{1,0:T(8,128)(2,1)}, u32[]{:S(2)}, u32[]{:S(2)}) collective-permute-start(bf16[1536,1152]{1,0:T(8,128)(2,1)S(1)} %copy-done.66), channel_id=1, source_target_pairs={{0,16},{4,12},{8,24},{12,4},{16,0},{20,28},{24,8},{28,20},{1,17},{... | collective-permute-start | bytes 10616840 | tf_op jit(solution)/shard_map/ppermute | solution.py:587
  489.1 86.2 %collective-permute-start.50 = (bf16[2304,384]{1,0:T(8,128)(2,1)}, bf16[2304,384]{1,0:T(8,128)(2,1)S(1)}, u32[]{:S(2)}, u32[]{:S(2)}) collective-permute-start(bf16[2304,384]{1,0:T(8,128)(2,1)} %add_convert_fusion.6), channel_id=1, source_target_pairs={{0,16},{4,12},{8,24},{12,4},{16,0},{20,28},{24,8},{28,20},{1,17},{... | collective-permute-start | bytes 5308424 | tf_op jit(solution)/shard_map/ppermute | solution.py:587
  496.3 91.0 %collective-permute-start.80 = (bf16[1536,1152]{1,0:T(8,128)(2,1)S(1)}, bf16[1536,1152]{1,0:T(8,128)(2,1)S(1)}, u32[]{:S(2)}, u32[]{:S(2)}) collective-permute-start(bf16[1536,1152]{1,0:T(8,128)(2,1)S(1)} %add_convert_fusion.1), channel_id=1, source_target_pairs={{0,8},{4,20},{8,0},{12,28},{16,24},{20,4},{24,16},{28,12},{1,9},{5... | collective-permute-start | bytes 10616840 | tf_op jit(solution)/shard_map/ppermute | solution.py:584
  594.0 167.9 %reduce-scatter.7.cloned.1.call-start = ((), (), s32[]{:S(2)}) async-start(), calls=%async_computation.10 | async-start | bytes 737280 | tf_op jit(solution)/shard_map/reduce_scatter | solution.py:613
  663.0 146.9 %reduce-scatter.5.cloned.1.call-start = ((), (), s32[]{:S(2)}) async-start(), calls=%async_computation.9 | async-start | bytes 1228800 | tf_op jit(solution)/shard_map/reduce_scatter | solution.py:613
  663.1 54.0 %collective-permute-start.88 = (bf16[2304,384]{1,0:T(8,128)(2,1)}, bf16[2304,384]{1,0:T(8,128)(2,1)}, u32[]{:S(2)}, u32[]{:S(2)}) collective-permute-start(bf16[2304,384]{1,0:T(8,128)(2,1)} %add_convert_fusion.7), channel_id=1, source_target_pairs={{0,16},{4,12},{8,24},{12,4},{16,0},{20,28},{24,8},{28,20},{1,17},{... | collective-permute-start | bytes 5308424 | tf_op jit(solution)/shard_map/ppermute | solution.py:587
  665.1 56.9 %collective-permute-start.89 = (bf16[2304,384]{1,0:T(8,128)(2,1)}, bf16[2304,384]{1,0:T(8,128)(2,1)}, u32[]{:S(2)}, u32[]{:S(2)}) collective-permute-start(bf16[2304,384]{1,0:T(8,128)(2,1)} %add_convert_fusion.5), channel_id=1, source_target_pairs={{0,8},{4,20},{8,0},{12,28},{16,24},{20,4},{24,16},{28,12},{1,9},{5... | collective-permute-start | bytes 5308424 | tf_op jit(solution)/shard_map/ppermute | solution.py:584
  710.0 111.2 %reduce-scatter.11.cloned.1.call-start = ((), (), s32[]{:S(2)}) async-start(), calls=%async_computation.12 | async-start | bytes 2211840 | tf_op jit(solution)/shard_map/reduce_scatter | solution.py:613
  754.2 113.4 %all-to-all-start.3 = ((bf16[8,128,1536]{2,1,0:T(8,128)(2,1)}), bf16[8,128,1536]{2,1,0:T(8,128)(2,1)}, u32[]{:S(2)}, u32[]{:S(2)}) async-start(bf16[8,128,1536]{2,1,0:T(8,128)(2,1)} %get-tuple-element.247), calls=%async_computation.3 | async-start | bytes 6291456 | tf_op jit(solution)/shard_map/all_to_all | solution.py:644
  758.9 65.3 %collective-permute-start.81 = (bf16[384,1152]{1,0:T(8,128)(2,1)}, bf16[384,1152]{1,0:T(8,128)(2,1)S(1)}, u32[]{:S(2)}, u32[]{:S(2)}) collective-permute-start(bf16[384,1152]{1,0:T(8,128)(2,1)} %reduce-scatter.9.cloned.1.call-done.refs_0_), channel_id=1, source_target_pairs={{0,8},{4,20},{8,0},{12,28},{16,24},{20,4},{24,16},{28,12},{1,9},{5... | collective-permute-start | bytes 2654216 | tf_op jit(solution)/shard_map/ppermute | solution.py:584
  (194 other events, 3011.4 us)
Sparse Core Ops, SparseCore 0:
  32.0 40.9 all-gather.4
  114.2 69.5 all-gather.6
  594.2 76.5 reduce-scatter.8
  673.4 22.2 reduce-scatter.6
  698.5 24.4 reduce-scatter.4
  726.6 39.8 reduce-scatter.10

commit v3 on v2

--- a/solution.py
+++ b/solution.py
@@ -66,8 +66,8 @@
     return lax.optimization_barrier((x, *done))[0]
 
 
-def after_all(xs, *done):
-    return lax.optimization_barrier((*xs, *done))[: len(xs)]
+def fence(*xs):
+    return lax.optimization_barrier(xs)
 
 
 def rounded(x):
@@ -111,6 +111,16 @@
         jnp.concatenate([-sine, none] * heads + [none, none] * still, axis=1),
         jnp.concatenate([none, sine] * heads + [none, none] * still, axis=1),
     )
+
+
+def rows_first(arrays):
+    def kernel(*refs):
+        for source, target in zip(refs, refs[len(arrays) :]):
+            target[...] = source[...]
+
+    return pl.pallas_call(
+        kernel, out_shape=[jax.ShapeDtypeStruct(x.shape, x.dtype) for x in arrays]
+    )(*arrays)
 
 
 def no_entry(doc_query, doc_key, rows, keys):
@@ -178,9 +188,7 @@
         ],
         scratch_shapes=[pltpu.VMEM((keys, block), jnp.float32)],
         compiler_params=pltpu.CompilerParams(vmem_limit_bytes=48 * 2**20),
-        cost_estimate=pl.CostEstimate(
-            flops=2 * 2 * rows * couples * 2 * keys * HD, bytes_accessed=12 * 2**20, transcendentals=rows * couples * 2 * keys
-        ),
+        cost_estimate=pl.CostEstimate(flops=10**8, bytes_accessed=10**5, transcendentals=0),
     )(query_lin, *tables, pairs, pairs_across, doc_query, doc_key)
 
 
@@ -258,9 +266,7 @@
             pltpu.VMEM((pairs.shape[0], HD), jnp.bfloat16),
         ],
         compiler_params=pltpu.CompilerParams(vmem_limit_bytes=48 * 2**20),
-        cost_estimate=pl.CostEstimate(
-            flops=5 * 2 * rows * couples * 2 * keys * HD, bytes_accessed=12 * 2**20, transcendentals=rows * couples * 2 * keys
-        ),
+        cost_estimate=pl.CostEstimate(flops=10**8, bytes_accessed=10**5, transcendentals=0),
     )(queries, d_mixed, totals, *tables, pairs, pairs_across, doc_query, doc_key)
 
 
@@ -521,8 +527,9 @@
     anywhere = pl.BlockSpec(memory_space=pl.ANY)
     inside = pl.BlockSpec(memory_space=pltpu.VMEM)
     operands = [facts, x, grad, first_w, second_w, shard, down_shard, block_sum, *down_pieces]
-    aliases = {7: 0}
+    aliases = {}
     if started:
+        aliases[7] = 0
         aliases[len(operands)] = 1
         operands.append(back_sum)
         for i, term in enumerate(terms):
@@ -556,11 +563,7 @@
             pltpu.SemaphoreType.DMA((17,)),
         ],
         compiler_params=pltpu.CompilerParams(vmem_limit_bytes=56 * 2**20),
-        cost_estimate=pl.CostEstimate(
-            flops=9 * 2 * rows * width * hidden,
-            bytes_accessed=40 * 2**20,
-            transcendentals=rows * hidden,
-        ),
+        cost_estimate=pl.CostEstimate(flops=10**8, bytes_accessed=10**5, transcendentals=0),
     )(*operands)
     return results[0], results[1], results[2], results[3], results[4:]
 
@@ -595,19 +598,6 @@
 
     def swap(self, x):
         return lax.ppermute(x, "seq", self.core_pairs)
-
-    def gather(self, piece):
-        u = self.first(piece)
-        v = self.second(piece)
-        d = self.second(u)
-        return [piece, u, v, d], [self.swap(piece), self.swap(v), self.swap(u), self.swap(d)]
-
-    def merge(self, own, other):
-        swaps = [self.swap(term) for term in other]
-        from_d = self.second(added(own[3], swaps[3]))
-        from_v = self.second(added(own[2], swaps[1]))
-        from_u = self.first(added(own[1], swaps[2], from_d))
-        return added(own[0], swaps[0], from_v, from_u)
 
     def down_columns(self, x):
         return lax.psum_scatter(x, "fsdp", scatter_dimension=0, tiled=True)
@@ -819,131 +809,198 @@
     def by_parts(shard):
         return shard.reshape(ranks, part_rows, shard.shape[1])
 
-    gains = jnp.pad(jnp.stack([norm_gain, ffn_gain]), ((0, 14), (0, 0)))
-    early = plane.along(jnp.concatenate([my_rows(w_query), my_rows(w_kv)], axis=1))
-    other_gains = plane.along(gains)
+    def second_halves(slots):
+        return [plane.swap(slots[i]) for i in (0, 2, 1, 3)]
+
+
+    gains = jnp.concatenate([norm_gain, ffn_gain]).reshape(part_rows, -1)
+    gain_width = gains.shape[1]
+    early = plane.along(
+        jnp.concatenate(
+            [my_rows(w_query), my_rows(w_kv), jnp.pad(gains, ((0, 0), (0, 128 - gain_width)))],
+            axis=1,
+        )
+    )
     send_slot, send_place = places_of(arrival_order, ranks)
-    place_slots = to_slots(send_place, send_slot, ranks, -1)
-    token_slots = to_slots(tokens[0], send_slot, ranks)
-    cotangent_slots = to_slots(after(cotangent[0], token_slots), send_slot, ranks)
-    got_place = exchange(place_slots)
+    labels = jnp.stack([send_place // 2, send_place % 2, jnp.ones_like(send_place)], axis=1)
+    labels = jnp.pad(labels.astype(jnp.bfloat16), ((0, 0), (0, 125)))
+    token_slots = to_slots(jnp.concatenate([tokens[0], labels], axis=1), send_slot, ranks)
+    *early, token_slots, cotangent_rows, out_mine, down_mine, gate_up_mine = fence(
+        *early, token_slots, cotangent[0], my_rows(w_out), w_down, w_gate_up
+    )
     got_tokens = exchange(token_slots)
-    early = jnp.stack(after_all(early, cotangent_slots))
-    own, other = plane.gather(early)
-    got_cotangent = exchange(after(cotangent_slots, early))
-    down_piece = lax.dynamic_slice(
-        after(w_down, early), (plane.core * half_rows, plane.chip * column), (half_rows, column)
-    )
-    down_piece = lax.all_gather(down_piece, "fsdp", axis=0, tiled=False)
+    early = jnp.stack(early)
+    gain_rows = early[:, :, split : split + gain_width].reshape(depth - 1, 2, shard_rows)
+    early = early[:, :, :split]
+
+    def down_of(shard, chip):
+        piece = lax.dynamic_slice(
+            shard, (plane.core * half_rows, chip * column), (half_rows, column)
+        )
+        return lax.all_gather(piece, "fsdp", axis=0, tiled=False)
+
+    down_piece = down_of(down_mine, plane.chip)
     gate_up_piece = lax.dynamic_slice(
-        after(w_gate_up, early),
-        (0, plane.core * FF + plane.chip * quarter),
-        (shard_rows, quarter),
+        gate_up_mine, (0, plane.core * FF + plane.chip * quarter), (shard_rows, quarter)
     )
     gate_up_piece = lax.all_gather(gate_up_piece, "fsdp", axis=0, tiled=False)
-    out_piece = plane.along(after(my_rows(w_out), early))
-
-    recv_place = got_place.reshape(-1)
-    is_live = recv_place >= 0
-    landing = jnp.where(is_live, recv_place, row_count)
-    safe_place = jnp.where(is_live, recv_place, 0)
-    packed_f = widened(from_slots(got_tokens, landing))
-    gain_rows = jnp.concatenate([jnp.stack(other_gains), gains[None]], axis=0)[:, :2]
+
+    early_u, early_v, early_0 = plane.first(early), plane.second(early), plane.swap(early)
+    out = plane.along(out_mine)
+    docs, cosine, sine = positions_of(lengths, row_count)
+    tables = rows_first(tables_of(cosine, sine, 2, 0))
+    cotangent_slots = to_slots(cotangent_rows, send_slot, ranks)
+    early_u, early_v, early_0, got_tokens, out, cotangent_slots, tables = fence(
+        early_u, early_v, early_0, got_tokens, out, cotangent_slots, tables
+    )
+    got_cotangent = exchange(cotangent_slots)
+
+    out = jnp.stack(out)
+    early_d, early_2, early_1 = plane.second(early_u), plane.swap(early_u), plane.swap(early_v)
+    out_u, out_v, out_0 = plane.first(out), plane.second(out), plane.swap(out)
+    labels = got_tokens.reshape(-1, model_width + 128)[:, model_width:].astype(jnp.int32)
+    safe_place = labels[:, 0] * 2 + labels[:, 1]
+    is_live = labels[:, 2] == 1
+    landing = jnp.where(is_live, safe_place, row_count)
+    packed_f = widened(from_slots(got_tokens, landing)[:, :model_width])
+    gain_rows = jnp.concatenate([gain_rows, gains.reshape(1, 2, shard_rows)], axis=0)
     gain_rows = gain_rows[(jnp.arange(depth, dtype=jnp.int32) + depth - 1 - level) % depth]
     gain_attn = widened(gain_rows[:, 0].reshape(model_width))
     gain_ffn = widened(gain_rows[:, 1].reshape(model_width))
-    docs, cosine, sine = positions_of(lengths, row_count)
-    tables = tables_of(cosine, sine, 2, 0)
     normed = rounded(rms_scale(packed_f, gain_attn))
-
-    query_w, kv_w = put_pieces(own + other, at, [by_parts(w_query), by_parts(w_kv)])
+    early_d, early_2, early_1, out_u, out_v, out_0, normed = fence(
+        early_d, early_2, early_1, out_u, out_v, out_0, normed
+    )
+
+    early_3, out_d, out_2, out_1 = (
+        plane.swap(early_d),
+        plane.second(out_u),
+        plane.swap(out_u),
+        plane.swap(out_v),
+    )
+    down_piece = rest(after(down_piece, normed), level)
+    early_3, out_d, out_2, out_1, down_piece = fence(early_3, out_d, out_2, out_1, down_piece)
+
+    down_u, down_v, down_0 = (
+        plane.first(down_piece),
+        plane.second(down_piece),
+        plane.swap(down_piece),
+    )
+    out_3 = plane.swap(out_d)
+    query_w, kv_w = put_pieces(
+        [early, early_u, early_v, early_d, early_0, early_1, early_2, early_3],
+        after(at, down_piece),
+        [by_parts(w_query), by_parts(w_kv)],
+    )
     query_w = query_w.reshape(model_width, model_width)
     kv_w = kv_w.reshape(model_width, 2 * HD)
+    query_lin = dot(normed, query_w)
     pair = pair_of(dot(normed, kv_w), cosine, sine)
-    query_lin = dot(after(normed, pair), query_w)
-    out_own, out_other = plane.gather(jnp.stack(after_all(out_piece, own[3])))
-    packed_grad = from_slots(after(got_cotangent, pair), landing)
-    down_piece = rest(after(down_piece, pair), level)
-    down_own, down_other = plane.gather(down_piece)
-    down_pieces = down_own + down_other
+    down_u, down_v, down_0, out_3, query_lin, pair = fence(
+        down_u, down_v, down_0, out_3, query_lin, pair
+    )
+
     pair_rows = with_earlier(pair, reach)
+    down_2, down_1 = plane.swap(down_u), plane.swap(down_v)
+    (out_w,) = put_pieces(
+        [out, out_u, out_v, out_d, out_0, out_1, out_2, out_3],
+        after(at, pair),
+        [by_parts(w_out)],
+    )
+    out_w = out_w.reshape(model_width, model_width)
+    down_d = down_of(after(w_down, gate_up_piece), plane.chips[3])
+    gate_up_piece = rest(gate_up_piece, level)
+    gate_up_piece = gate_up_piece.reshape((depth - 1) * shard_rows, quarter)
+    packed_grad = from_slots(after(got_cotangent, gate_up_piece), landing)
+    pair_rows, down_2, down_1, out_w, gate_up_piece, packed_grad = fence(
+        pair_rows, down_2, down_1, out_w, gate_up_piece, packed_grad
+    )
+
+    gate_up_u, gate_up_v, gate_up_0 = (
+        plane.first(gate_up_piece),
+        plane.second(gate_up_piece),
+        plane.swap(gate_up_piece),
+    )
     pairs_across = pair_rows.T
-    queries, mixed, totals = attend(
-        after(query_lin, packed_grad, down_piece), tables, pair_rows, pairs_across, *docs
-    )
-    (out_w,) = put_pieces(out_own + out_other, after(at, mixed), [by_parts(w_out)])
-    out_w = out_w.reshape(model_width, model_width)
+    queries, mixed, totals = attend(query_lin, tables, pair_rows, pairs_across, *docs)
     hidden_state = packed_f + dot(mixed, out_w)
     ffn_in = rounded(rms_scale(hidden_state, gain_ffn))
-
-    gate_up_piece = rest(after(gate_up_piece, ffn_in), level)
-    first_ws, second_ws = plane.gather(gate_up_piece.reshape((depth - 1) * shard_rows, quarter))
-    block_sum, d_ffn_in, terms = hidden_state, None, None
-    firsts, swaps = [], []
-    chunk_in = ffn_in
-    for slot in range(4):
-        if slot >= 2:
-            chunk_in = after(chunk_in, swaps[slot - 2])
+    down_d = rest(after(down_d, ffn_in), level)
+    down_3 = plane.swap(down_d)
+
+    def chunk(slot, first_w, second_w, chunk_in, block_sum, back_sum, terms):
         facts = [plane.core, plane.chips[slot], plane.core, *plane.chips, level]
-        block_sum, d_ffn_in, first_grad, second_grad, terms = feed(
+        return feed(
             jnp.stack(facts).astype(jnp.int32),
             chunk_in,
             packed_grad,
-            first_ws[slot],
-            second_ws[slot],
+            first_w,
+            second_w,
             w_gate_up,
-            down_pieces,
+            [down_piece, down_u, down_v, down_d, down_0, down_1, down_2, down_3],
             w_down,
             block_sum,
-            d_ffn_in,
+            back_sum,
             terms,
         )
-        firsts.append(first_grad)
-        swaps.append(plane.swap(second_grad))
-        if slot == 2:
-            sum_v = added(firsts[2], swaps[1])
-            from_v = plane.second(sum_v)
-            chunk_in = after(chunk_in, sum_v)
-
+
+    block_sum, back_sum, own_0, other_0, terms = chunk(
+        0, gate_up_piece, gate_up_0, ffn_in, hidden_state, None, None
+    )
+    gate_up_u, gate_up_v, block_sum, back_sum, own_0, other_0 = fence(
+        gate_up_u, gate_up_v, block_sum, back_sum, own_0, other_0
+    )
+
+    gate_up_2, gate_up_1 = plane.swap(gate_up_u), plane.swap(gate_up_v)
+    gate_up_2, gate_up_1, gate_up_u, back_sum = fence(gate_up_2, gate_up_1, gate_up_u, back_sum)
+    gate_up_d, swap_0 = plane.second(gate_up_u), plane.swap(other_0)
+    block_sum, back_sum, own_u, other_u, terms = chunk(
+        1, gate_up_u, gate_up_1, ffn_in, block_sum, back_sum, terms
+    )
+    gate_up_d, swap_0, block_sum, back_sum, own_u, other_u = fence(
+        gate_up_d, swap_0, block_sum, back_sum, own_u, other_u
+    )
+    gate_up_3, swap_u = plane.swap(gate_up_d), plane.swap(other_u)
+    block_sum, back_sum, own_v, other_v, terms = chunk(
+        2, gate_up_v, gate_up_2, ffn_in, block_sum, back_sum, terms
+    )
+    gate_up_3, swap_u, block_sum, back_sum, own_v, other_v = fence(
+        gate_up_3, swap_u, block_sum, back_sum, own_v, other_v
+    )
+    sum_v, other_v, back_sum = fence(added(own_v, swap_u), other_v, back_sum)
+    from_v, swap_v = plane.second(sum_v), plane.swap(other_v)
+    block_sum, back_sum, own_d, other_d, terms = chunk(
+        3, gate_up_d, gate_up_3, ffn_in, block_sum, back_sum, terms
+    )
+    sum_u = added(own_u, swap_v)
+    from_v, sum_u, block_sum, back_sum, own_d, other_d, terms = fence(
+        from_v, sum_u, block_sum, back_sum, own_d, other_d, terms
+    )
+
+    from_u, swap_d = plane.first(sum_u), plane.swap(other_d)
     terms = [term.reshape(depth * half_rows, column) for term in terms]
     down_swaps = [plane.swap(term) for term in terms[4:]]
     unused_scaled, ffn_norm_pull = jax.vjp(rms_scale, hidden_state, gain_ffn)
-    d_hidden_norm, grad_gain_ffn = ffn_norm_pull(d_ffn_in)
+    d_hidden_norm, grad_gain_ffn = ffn_norm_pull(back_sum)
     d_hidden = widened(packed_grad) + d_hidden_norm
     d_branch = rounded(d_hidden)
     d_mixed = rounded(dot_across(d_branch, out_w))
-    sum_d = added(after(firsts[3], d_mixed), swaps[3])
-    from_d = plane.second(sum_d)
+    sum_d = added(after(own_d, d_mixed), swap_d)
+    part_d = plane.down_columns(sum_d)
     down_sums = [
         added(after(term, sum_d), down_swaps[match])
         for term, match in zip(terms[:4], (0, 2, 1, 3))
     ]
+    from_u, d_branch, d_mixed, down_sums = fence(from_u, d_branch, d_mixed, down_sums)
     from_down_d, from_down_v = plane.second(down_sums[3]), plane.second(down_sums[2])
+    total = added(own_0, swap_0, from_v, from_u)
+    part_0 = plane.down_columns(total)
     d_query_lin, d_pairs = attend_back(
-        queries, after(d_mixed, *down_sums), totals, tables, pair_rows, pairs_across, *docs
-    )
-    d_own = owners_sum(d_pairs, row_count, reach)
-    sum_u = added(after(firsts[1], d_pairs), swaps[2], from_d)
-    from_u = plane.first(sum_u)
-    grad_out = dot_rows(mixed, after(d_branch, sum_u))
-    grad_query = dot_rows(normed, after(d_query_lin, sum_u))
-    block_rows = rounded(after(block_sum, sum_u))
-    home_out = exchange(back_to_slots(block_rows, is_live, safe_place, ranks))
-    down_u = added(after(down_sums[1], grad_query), from_down_d)
-    from_down_u = plane.first(down_u)
-    d_kv_lin = rounded(
-        jnp.concatenate([unrotate(d_own[:, :HD], cosine, sine), d_own[:, HD:]], axis=1)
-    )
-    d_kv_lin = after(d_kv_lin, down_u)
-    grad_kv = dot_rows(normed, d_kv_lin)
-    d_normed = dot_across(d_query_lin, query_w) + dot_across(d_kv_lin, kv_w)
-    unused_normed, attn_norm_pull = jax.vjp(rms_scale, packed_f, gain_attn)
-    d_packed_norm, grad_gain_attn = attn_norm_pull(d_normed)
-    grad_rows = rounded(d_hidden + d_packed_norm)
-    home_grad = exchange(back_to_slots(grad_rows, is_live, safe_place, ranks))
-
-    total = added(after(firsts[0], grad_rows), swaps[0], from_v, from_u)
-    mine_gate_up = plane.down_columns(total)
+        queries, after(d_mixed, total), totals, tables, pair_rows, pairs_across, *docs
+    )
+    from_down_d, from_down_v, d_query_lin, d_pairs, block_sum = fence(
+        from_down_d, from_down_v, d_query_lin, d_pairs, block_sum
+    )
 
     def by_rows(grad):
         pieces = rounded(grad).reshape(depth, ranks, part_rows, grad.shape[1])
@@ -952,6 +1009,24 @@
             for i in range(8)
         ]
 
+    d_own = owners_sum(d_pairs, row_count, reach)
+    down_u = added(down_sums[1], from_down_d)
+    block_slots = back_to_slots(rounded(block_sum), is_live, safe_place, ranks)
+    d_own, down_u, block_slots, part_d = fence(d_own, down_u, block_slots, part_d)
+    home_out = exchange(block_slots)
+    from_down_u, part_d_u = plane.first(down_u), plane.first(part_d)
+    grad_out = dot_rows(mixed, after(d_branch, block_slots))
+    out_terms = [p.reshape(depth * part_rows, model_width) for p in by_rows(grad_out)]
+    out_swaps = [plane.swap(term) for term in out_terms[4:]]
+    d_kv_lin = rounded(
+        jnp.concatenate([unrotate(d_own[:, :HD], cosine, sine), d_own[:, HD:]], axis=1)
+    )
+    grad_query = dot_rows(normed, after(d_query_lin, *out_terms))
+    grad_kv = dot_rows(normed, d_kv_lin)
+    d_normed = dot_across(d_query_lin, query_w) + dot_across(d_kv_lin, kv_w)
+    unused_normed, attn_norm_pull = jax.vjp(rms_scale, packed_f, gain_attn)
+    d_packed_norm, grad_gain_attn = attn_norm_pull(d_normed)
+    grad_rows = rounded(d_hidden + d_packed_norm)
     gain_rows = jnp.concatenate(
         [
             rounded(grad_gain_attn).reshape(depth, 1, shard_rows),
@@ -960,32 +1035,99 @@
         axis=2,
     )
     gain_rows = jnp.pad(gain_rows, ((0, 0), (0, 15), (0, split - 2 * shard_rows)))
-    pieces = [
+    early_terms = [
         jnp.concatenate([jnp.concatenate([q, k], axis=2), gain_rows], axis=1).reshape(
             depth * (part_rows + 16), split
         )
         for q, k in zip(by_rows(grad_query), by_rows(grad_kv))
     ]
-    mine_early = plane.down_columns(plane.merge(pieces[:4], pieces[4:]))
-    total = added(down_sums[0], from_down_v, from_down_u)
+    grad_slots = back_to_slots(after(grad_rows, *early_terms), is_live, safe_place, ranks)
+    from_down_u, part_d_u, early_terms, out_swaps, grad_slots, home_out = fence(
+        from_down_u, part_d_u, early_terms, out_swaps, grad_slots, home_out
+    )
+
+    home_grad = exchange(grad_slots)
+    part_d = plane.second(part_d_u)
+    early_swaps = [plane.swap(term) for term in early_terms[4:]]
+    out_d, out_v = added(out_terms[3], out_swaps[3]), added(out_terms[2], out_swaps[1])
+    out_from_d, out_from_v = plane.second(out_d), plane.second(out_v)
+    total = added(after(down_sums[0], out_d, out_v), from_down_v, from_down_u)
     mine_down = plane.down_columns(total)
-    pieces = [p.reshape(depth * part_rows, model_width) for p in by_rows(grad_out)]
-    mine_out = plane.down_columns(plane.merge(pieces[:4], pieces[4:]))
-
-    def everywhere(mine, rows, width, place):
-        own, other = plane.gather(mine)
-        return spread(own + other, plane.sources, (rows, width), place)
-
-    total_gate_up = everywhere(
-        mine_gate_up, shard_rows, 2 * FF, lambda p: (0, (p % 2) * 4 + p // 2)
-    )
-    total_down = everywhere(
-        mine_down, 2 * half_rows, model_width, lambda p: (p % 2, p // 2)
-    )
-    total_out = everywhere(mine_out, shard_rows, model_width, lambda p: (p, 0))
-    total_early = everywhere(mine_early[:part_rows], shard_rows, split, lambda p: (p, 0))
+    early_d = added(early_terms[3], early_swaps[3])
+    early_v = added(early_terms[2], early_swaps[1])
     block_arrived = home_out.reshape(-1, model_width)[send_slot]
+    part_d, out_from_d, out_from_v, early_d, early_v, early_swaps, part_0, block_arrived = fence(
+        part_d, out_from_d, out_from_v, early_d, early_v, early_swaps, part_0, block_arrived
+    )
+
+    mine_gate_up = added(part_0, part_d)
+    early_from_d, early_from_v = plane.second(early_d), plane.second(early_v)
+    out_from_u = plane.first(added(out_terms[1], out_swaps[2], out_from_d))
+    gate_up_u, gate_up_v, gate_up_0 = (
+        plane.first(mine_gate_up),
+        plane.second(mine_gate_up),
+        plane.swap(mine_gate_up),
+    )
+    early_from_d, early_from_v, out_from_u, gate_up_u, gate_up_v, gate_up_0, home_grad = fence(
+        early_from_d, early_from_v, out_from_u, gate_up_u, gate_up_v, gate_up_0, home_grad
+    )
+
+    early_from_u = plane.first(added(early_terms[1], early_swaps[2], early_from_d))
+    total = added(out_terms[0], out_swaps[0], out_from_v, out_from_u)
+    mine_out = plane.down_columns(total)
+    gate_up_d, gate_up_2, gate_up_1 = (
+        plane.second(gate_up_u),
+        plane.swap(gate_up_u),
+        plane.swap(gate_up_v),
+    )
     grad_arrived = home_grad.reshape(-1, model_width)[send_slot]
+    early_from_u, gate_up_d, gate_up_2, gate_up_1, mine_down, total, grad_arrived = fence(
+        early_from_u, gate_up_d, gate_up_2, gate_up_1, mine_down, total, grad_arrived
+    )
+
+    total = added(early_terms[0], early_swaps[0], early_from_v, early_from_u)
+    mine_early = plane.down_columns(total)
+    gate_up_3 = plane.swap(gate_up_d)
+    down_own = [mine_down, plane.first(mine_down), plane.second(mine_down)]
+    total_gate_up = spread(
+        [mine_gate_up, gate_up_u, gate_up_v, gate_up_d]
+        + [gate_up_0, gate_up_1, gate_up_2, gate_up_3],
+        after(plane.sources, total),
+        (shard_rows, 2 * FF),
+        lambda p: (0, (p % 2) * 4 + p // 2),
+    )
+    down_own, total_gate_up, mine_out = fence(down_own, total_gate_up, mine_out)
+
+    down_own.append(plane.second(down_own[1]))
+    down_swaps = [plane.swap(piece) for piece in down_own[:3]]
+    out_own = [mine_out, plane.first(mine_out), plane.second(mine_out)]
+    down_own, down_swaps, out_own, mine_early = fence(down_own, down_swaps, out_own, mine_early)
+
+    down_swaps.append(plane.swap(down_own[3]))
+    out_own.append(plane.second(out_own[1]))
+    piece = mine_early[:part_rows]
+    early_own = [piece, plane.first(piece), plane.second(piece)]
+    total_down = spread(
+        down_own + [down_swaps[i] for i in (0, 2, 1, 3)],
+        plane.sources,
+        (2 * half_rows, model_width),
+        lambda p: (p % 2, p // 2),
+    )
+    early_own, out_own, total_down = fence(early_own, out_own, total_down)
+    early_own.append(plane.second(early_own[1]))
+    total_out = spread(
+        out_own + second_halves(out_own),
+        plane.sources,
+        (shard_rows, model_width),
+        lambda p: (p, 0),
+    )
+    early_own, total_out = fence(early_own, total_out)
+    total_early = spread(
+        early_own + second_halves(early_own),
+        plane.sources,
+        (shard_rows, split),
+        lambda p: (p, 0),
+    )
     return (
         block_arrived[None],
         grad_arrived[None],

time: 924 us -> 805 us (0.87)
  waiting for transfers between devices: 343 us -> 239 us
  other arithmetic: 80.4 us -> 109 us
  starting transfers between devices: 119 us -> 97.1 us
  local copies, waits for them, and re-layouts: 121 us -> 101 us
    ppermute x24 -> x23, waiting for transfers between devices: 178 us -> 63.5 us  [second(): return lax.ppermute(x, 'seq', self.second_pairs)]
    ppermute x12 -> x13, waiting for transfers between devices: 107 us -> 145 us  [first(): return lax.ppermute(x, 'seq', self.first_pairs)]
    all_to_all x5 -> x4, waiting for transfers between devices: 27.5 us -> 0.01 us  [exchange(): return lax.all_to_all(x, 'seq', split_axis=0, concat_axis=0, tiled=True)]
    unnamed x222 -> x168, local copies, waits for them, and re-layouts: 38.2 us -> 22.8 us
    convert_element_type x23 -> x24, other arithmetic: 55.1 us -> 68.9 us  [rounded(): return x.astype(jnp.bfloat16)]
    ppermute x48, starting transfers between devices: 23.5 us -> 10.5 us  [swap(): return lax.ppermute(x, 'seq', self.core_pairs)]
    ppermute x12 -> x13, starting transfers between devices: 18.8 us -> 15.8 us  [first(): return lax.ppermute(x, 'seq', self.first_pairs)]
    ppermute x24 -> x23, starting transfers between devices: 28.4 us -> 28.2 us  [second(): return lax.ppermute(x, 'seq', self.second_pairs)]
  transfers between devices with their start and end apart: 108 -> 106, of which waited for: 30 -> 28; matrix products, arithmetic and copies ran while one was open for 21% -> 25% of each run, Pallas kernels for 18% -> 26%
where the time goes in v3:
time: 805 us; the launch traced here: 794 us
  waiting for transfers between devices  239 us (30%)
  Pallas kernels  205 us (25%)
  other arithmetic  109 us (14%)
  local copies, waits for them, and re-layouts  101 us (13%)
  starting transfers between devices  97.1 us (12%)
  matrix products  27.4 us (3%)
  between operations  15.7 us (2%)
    ppermute x13, waiting for transfers between devices, first(): return lax.ppermute(x, 'seq', self.first_pairs)  145 us
    pallas_call x4, Pallas kernels, feed(): pl.pallas_call(kernel, in_specs=[pl.BlockSpec(memory_space=pltpu.SMEM), i...  115 us
    convert_element_type x24, other arithmetic, rounded(): return x.astype(jnp.bfloat16)  68.9 us
    ppermute x23, waiting for transfers between devices, second(): return lax.ppermute(x, 'seq', self.second_pairs)  63.5 us
    ppermute x23, starting transfers between devices, second(): return lax.ppermute(x, 'seq', self.second_pairs)  28.2 us
    pallas_call x1, Pallas kernels, attend_back(): pl.pallas_call(kernel, grid=(rows // block, couples), in_specs=[tile, til...  26 us
    unnamed x168, local copies, waits for them, and re-layouts  22.8 us
    all_to_all x4, starting transfers between devices, exchange(): return lax.all_to_all(x, 'seq', split_axis=0, concat_axis=0, tiled=True)  21.7 us
  transfers between devices with their start and end apart: 106, of which 28 were waited for; matrix products, arithmetic and copies ran while one was open for 25% of the time, Pallas kernels for 26%

profile of v3, /device:TPU:0, one launch (start us, length us, event | category | flops | bytes accessed | tf_op | source)
XLA Modules:
  0.0 794.0 jit_solution(2637346286019489661)
XLA Ops:
  21.3 6.3 scatter_custom_fusion
  70.4 11.5 %collective-permute-done.7 = bf16[48,1536]{1,0:T(8,128)(2,1)} collective-permute-done((bf16[48,1536]{1,0:T(8,128)(2,1)}, bf16[48,1536]{1,0:T(8,128)(2,1)}, u32[]{:S(2)}, u32[]{:S(2)}) %collective-permute-start.7) | collective-permute-done | bytes 147488 | tf_op jit(solution)/shard_map/ppermute | solution.py:595
  81.9 8.4 %collective-permute-done.3.refs_1_ = bf16[3,48,1920]{2,1,0:T(8,128)(2,1)S(1)} collective-permute-done((bf16[3,48,1920]{2,1,0:T(8,128)(2,1)S(1)}, bf16[3,48,1920]{2,1,0:T(8,128)(2,1)S(1)}, u32[]{:S(2)}, u32[]{:S(2)}) %collective-permute-start.3) | collective-permute-done | bytes 552992 | tf_op jit(solution)/shard_map/ppermute | solution.py:587
  98.8 7.9 scatter_custom_fusion.2
  142.2 41.9 %collective-permute-done.19.refs_6_ = bf16[3,576,384]{2,1,0:T(8,128)(2,1)} collective-permute-done((bf16[3,576,384]{2,1,0:T(8,128)(2,1)}, bf16[3,576,384]{2,1,0:T(8,128)(2,1)}, u32[]{:S(2)}, u32[]{:S(2)}) %collective-permute-start.19) | collective-permute-done | bytes 1327136 | tf_op jit(solution)/shard_map/ppermute | solution.py:587
  205.3 7.5 scatter_custom_fusion.3.g_ref
  219.4 21.0 %shard_map.183 = (bf16[512,1536]{1,0:T(8,128)(2,1)}, bf16[512,1536]{1,0:T(8,128)(2,1)}, f32[4,2,512]{2,1,0:T(2,128)S(1)}) custom-call(f32[512,1536]{1,0:T(8,128)} %fusion.78.q_ref, f32[512,384]{1,0:T(8,128)S(1)} %copy-done.1, f32[512,384]{1,0:T(8,128)S(1)} %copy-done.3, f32[512,384]{1,0:T(8,128)S(1)} %copy-done.5, bf16[1536,384]{1,0:T(8,128)(2,1)S(1)} %copy.124.pairs_ref, ...), custom_call_target="tpu_custom_call" | custom-call | flops 100000000 | bytes 100000 | tf_op jit(solution)/shard_map/pallas_call | solution.py:170
  255.3 28.4 %shard_map.185 = (f32[512,1536]{1,0:T(8,128)}, f32[512,1536]{1,0:T(8,128)}, bf16[1536,1152]{1,0:T(8,128)(2,1)}, bf16[1536,1152]{1,0:T(8,128)(2,1)}, bf16[4,576,3...) custom-call(s32[8]{0:T(128)} %stack.133.facts_ref, ...), custom_call_target="tpu_custom_call" | custom-call | flops 100000000 | bytes 100000 | tf_op jit(solution)/shard_map/pallas_call | solution.py:540
  295.6 28.8 %shard_map.186 = (f32[512,1536]{1,0:T(8,128)}, f32[512,1536]{1,0:T(8,128)}, bf16[1536,1152]{1,0:T(8,128)(2,1)}, bf16[1536,1152]{1,0:T(8,128)(2,1)}, bf16[4,576,3...) custom-call(s32[8]{0:T(128)} %stack.134.facts_ref, ...), custom_call_target="tpu_custom_call", output_to_operand_aliasing={{0}: (7, {}), {1}: (16, {}), {4}: (17, {}), {5}: (18, {}), ... | custom-call | flops 100000000 | bytes 100000 | tf_op jit(solution)/shard_map/pallas_call | solution.py:540
  326.4 28.6 %shard_map.187 = (f32[512,1536]{1,0:T(8,128)}, f32[512,1536]{1,0:T(8,128)}, bf16[1536,1152]{1,0:T(8,128)(2,1)}, bf16[1536,1152]{1,0:T(8,128)(2,1)}, bf16[4,576,3...) custom-call(s32[8]{0:T(128)} %stack.135.facts_ref, ...), custom_call_target="tpu_custom_call", output_to_operand_aliasing={{0}: (7, {}), {1}: (16, {}), {4}: (17, {}), {5}: (18, {}), ... | custom-call | flops 100000000 | bytes 100000 | tf_op jit(solution)/shard_map/pallas_call | solution.py:540
  363.4 29.0 %shard_map.188 = (f32[512,1536]{1,0:T(8,128)}, f32[512,1536]{1,0:T(8,128)}, bf16[1536,1152]{1,0:T(8,128)(2,1)}, bf16[1536,1152]{1,0:T(8,128)(2,1)}, bf16[4,576,3...) custom-call(s32[8]{0:T(128)} %stack.136.facts_ref, ...), custom_call_target="tpu_custom_call", output_to_operand_aliasing={{0}: (7, {}), {1}: (16, {}), {4}: (17, {}), {5}: (18, {}), ... | custom-call | flops 100000000 | bytes 100000 | tf_op jit(solution)/shard_map/pallas_call | solution.py:540
  429.4 25.8 %collective-permute-done.39 = bf16[1536,1152]{1,0:T(8,128)(2,1)} collective-permute-done((bf16[1536,1152]{1,0:T(8,128)(2,1)}, bf16[1536,1152]{1,0:T(8,128)(2,1)}, u32[]{:S(2)}, u32[]{:S(2)}) %collective-permute-start.39) | collective-permute-done | bytes 3538976 | tf_op jit(solution)/shard_map/ppermute | solution.py:587
  457.2 7.7 add_convert_fusion
  468.4 26.0 %shard_map.189 = (bf16[512,1536]{1,0:T(8,128)(2,1)}, f32[1536,384]{1,0:T(8,128)}) custom-call(bf16[512,1536]{1,0:T(8,128)(2,1)} %get-tuple-element.394.q_ref, bf16[512,1536]{1,0:T(8,128)(2,1)} %convolution_convert_fusion.2.do_ref, f32[4,2,512]{2,1,0:T(2,128)S(1)} %get-tuple-element.401.total_ref, f32[512,384]{1,0:T(8,128)S(1)} %copy-done.2, ...), custom_call_target="tpu_custom_call" | custom-call | flops 100000000 | bytes 100000 | tf_op jit(solution)/shard_map/pallas_call | solution.py:242
  519.7 8.3 %all-to-all-start.2 = ((bf16[8,128,1536]{2,1,0:T(8,128)(2,1)}), bf16[8,128,1536]{2,1,0:T(8,128)(2,1)}, u32[]{:S(2)}, u32[]{:S(2)}) async-start(bf16[8,128,1536]{2,1,0:T(8,128)(2,1)} %broadcast_select_fusion.1), calls=%async_computation.3 | async-start | bytes 6291456 | tf_op jit(solution)/shard_map/all_to_all | solution.py:634
  566.3 27.2 %collective-permute-done.50 = bf16[384,1152]{1,0:T(8,128)(2,1)} collective-permute-done((bf16[384,1152]{1,0:T(8,128)(2,1)}, bf16[384,1152]{1,0:T(8,128)(2,1)}, u32[]{:S(2)}, u32[]{:S(2)}) %collective-permute-start.50) | collective-permute-done | bytes 884768 | tf_op jit(solution)/shard_map/ppermute | solution.py:587
  602.8 7.0 gather_fusion.3
  621.7 33.1 %collective-permute-done.55 = bf16[384,1152]{1,0:T(8,128)(2,1)} collective-permute-done((bf16[384,1152]{1,0:T(8,128)(2,1)}, bf16[384,1152]{1,0:T(8,128)(2,1)}, u32[]{:S(2)}, u32[]{:S(2)}) %collective-permute-start.55) | collective-permute-done | bytes 884768 | tf_op jit(solution)/shard_map/ppermute | solution.py:590
  663.7 8.7 %collective-permute-done.64 = bf16[192,1536]{1,0:T(8,128)(2,1)S(1)} collective-permute-done((bf16[192,1536]{1,0:T(8,128)(2,1)S(1)}, bf16[192,1536]{1,0:T(8,128)(2,1)S(1)}, u32[]{:S(2)}, u32[]{:S(2)}) %collective-permute-start.64) | collective-permute-done | bytes 589856 | tf_op jit(solution)/shard_map/ppermute | solution.py:587
  672.4 19.0 %collective-permute-done.65.refs_1_ = bf16[384,1152]{1,0:T(8,128)(2,1)S(1)} collective-permute-done((bf16[384,1152]{1,0:T(8,128)(2,1)S(1)}, bf16[384,1152]{1,0:T(8,128)(2,1)S(1)}, u32[]{:S(2)}, u32[]{:S(2)}) %collective-permute-start.65) | collective-permute-done | bytes 884768 | tf_op jit(solution)/shard_map/ppermute | solution.py:587
  691.4 13.2 %collective-permute-done.66.refs_2_ = bf16[384,1152]{1,0:T(8,128)(2,1)S(1)} collective-permute-done((bf16[384,1152]{1,0:T(8,128)(2,1)S(1)}, bf16[384,1152]{1,0:T(8,128)(2,1)S(1)}, u32[]{:S(2)}, u32[]{:S(2)}) %collective-permute-start.66) | collective-permute-done | bytes 884768 | tf_op jit(solution)/shard_map/ppermute | solution.py:590
  713.4 6.7 gather_fusion.4
  735.2 8.5 %shard_map.190 = f32[384,9216]{1,0:T(8,128)} custom-call(s32[8]{0:T(128)S(1)} %stack.137.positions_ref, bf16[384,1152]{1,0:T(8,128)(2,1)S(1)} %add_convert_fusion.14.refs_0_, bf16[384,1152]{1,0:T(8,128)(2,1)S(1)} %collective-permute-done.65.refs_1_, bf16[384,1152]{1,0:T(8,128)(2,1)S(1)} %collective-permute-done.66.refs_2_, ...), custom_call_target="tpu_custom_call" | custom-call | tf_op jit(solution)/shard_map/pallas_call | solution.py:355
  748.3 6.3 collective-permute-done.79.refs_1_
  (522 shorter events, 361.4 us)
Async XLA Ops:
  7.2 111.6 %all-gather.7.cloned.1.call-start = ((), (), s32[]{:S(2)}) async-start(), calls=%async_computation.14 | async-start | bytes 2211840 | tf_op jit(solution)/shard_map/all_gather | solution.py:840
  34.3 56.9 %all-to-all-start = ((bf16[8,128,1664]{2,1,0:T(8,128)(2,1)}), bf16[8,128,1664]{2,1,0:T(8,128)(2,1)}, u32[]{:S(2)}, u32[]{:S(2)}) async-start(bf16[8,128,1664]{2,1,0:T(8,128)(2,1)} %bitcast.199), calls=%async_computation | async-start | bytes 6815744 | tf_op jit(solution)/shard_map/all_to_all | solution.py:634
  38.8 145.8 %all-gather.9.cloned.1.call-start = ((), (), s32[]{:S(2)}) async-start(), calls=%async_computation.15 | async-start | bytes 4423680 | tf_op jit(solution)/shard_map/all_gather | solution.py:846
  44.5 45.9 %collective-permute-start.3 = (bf16[3,48,1920]{2,1,0:T(8,128)(2,1)S(1)}, bf16[3,48,1920]{2,1,0:T(8,128)(2,1)S(1)}, u32[]{:S(2)}, u32[]{:S(2)}) collective-permute-start(bf16[3,48,1920]{2,1,0:T(8,128)(2,1)S(1)} %slice.123.refs_0_), channel_id=1, source_target_pairs={{0,8},{4,20},{8,0},{12,28},{16,24},{20,4},{24,16},{28,12},{1,9},{5... | collective-permute-start | bytes 1658888 | tf_op jit(solution)/shard_map/ppermute | solution.py:587
  46.4 44.0 %collective-permute-start.4 = (bf16[3,48,1920]{2,1,0:T(8,128)(2,1)S(1)}, bf16[3,48,1920]{2,1,0:T(8,128)(2,1)S(1)}, u32[]{:S(2)}, u32[]{:S(2)}) collective-permute-start(bf16[3,48,1920]{2,1,0:T(8,128)(2,1)S(1)} %slice.123.refs_0_), channel_id=1, source_target_pairs={{0,16},{4,12},{8,24},{12,4},{16,0},{20,28},{24,8},{28,20},{1,17},{... | collective-permute-start | bytes 1658888 | tf_op jit(solution)/shard_map/ppermute | solution.py:590
  114.2 91.2 %all-to-all-start.1 = ((bf16[8,128,1536]{2,1,0:T(8,128)(2,1)}), bf16[8,128,1536]{2,1,0:T(8,128)(2,1)}, u32[]{:S(2)}, u32[]{:S(2)}) async-start(bf16[8,128,1536]{2,1,0:T(8,128)(2,1)} %bitcast.200), calls=%async_computation.1 | async-start | bytes 6291456 | tf_op jit(solution)/shard_map/all_to_all | solution.py:634
  118.6 130.1 %all-gather.11.cloned.1.call-start = ((), (), s32[]{:S(2)}) async-start(), calls=%async_computation.16 | async-start | bytes 2211840 | tf_op jit(solution)/shard_map/all_gather | solution.py:840
  122.1 62.0 %collective-permute-start.19 = (bf16[3,576,384]{2,1,0:T(8,128)(2,1)}, bf16[3,576,384]{2,1,0:T(8,128)(2,1)}, u32[]{:S(2)}, u32[]{:S(2)}) collective-permute-start(bf16[3,576,384]{2,1,0:T(8,128)(2,1)} %shard_map.179.refs_5_), channel_id=1, source_target_pairs={{0,8},{4,20},{8,0},{12,28},{16,24},{20,4},{24,16},{28,12},{1,9},{5... | collective-permute-start | bytes 3981320 | tf_op jit(solution)/shard_map/ppermute | solution.py:587
  124.0 60.1 %collective-permute-start.20 = (bf16[3,576,384]{2,1,0:T(8,128)(2,1)}, bf16[3,576,384]{2,1,0:T(8,128)(2,1)}, u32[]{:S(2)}, u32[]{:S(2)}) collective-permute-start(bf16[3,576,384]{2,1,0:T(8,128)(2,1)} %shard_map.179.refs_5_), channel_id=1, source_target_pairs={{0,16},{4,12},{8,24},{12,4},{16,0},{20,28},{24,8},{28,20},{1,17},{... | collective-permute-start | bytes 3981320 | tf_op jit(solution)/shard_map/ppermute | solution.py:590
  125.4 58.6 %collective-permute-start.21 = (bf16[3,576,384]{2,1,0:T(8,128)(2,1)}, bf16[3,576,384]{2,1,0:T(8,128)(2,1)}, u32[]{:S(2)}, u32[]{:S(2)}) collective-permute-start(bf16[3,576,384]{2,1,0:T(8,128)(2,1)} %shard_map.179.refs_5_), channel_id=1, source_target_pairs={{0,4},{4,0},{8,12},{12,8},{16,20},{20,16},{24,28},{28,24},{1,5},{5... | collective-permute-start | bytes 3981320 | tf_op jit(solution)/shard_map/ppermute | solution.py:600
  186.4 331.7 %reduce-scatter.6.cloned.1.call-start = ((), (), s32[]{:S(2)}) async-start(), calls=%async_computation.9 | async-start | bytes 4423680 | tf_op jit(solution)/shard_map/reduce_scatter | solution.py:603
  214.6 69.2 %collective-permute-start.27 = (bf16[1152,1152]{1,0:T(8,128)(2,1)}, bf16[1152,1152]{1,0:T(8,128)(2,1)}, u32[]{:S(2)}, u32[]{:S(2)}) collective-permute-start(bf16[1152,1152]{1,0:T(8,128)(2,1)} %bitcast.204), channel_id=1, source_target_pairs={{0,8},{4,20},{8,0},{12,28},{16,24},{20,4},{24,16},{28,12},{1,9},{5... | collective-permute-start | bytes 7962632 | tf_op jit(solution)/shard_map/ppermute | solution.py:587
  215.2 68.6 %collective-permute-start.28 = (bf16[1152,1152]{1,0:T(8,128)(2,1)}, bf16[1152,1152]{1,0:T(8,128)(2,1)}, u32[]{:S(2)}, u32[]{:S(2)}) collective-permute-start(bf16[1152,1152]{1,0:T(8,128)(2,1)} %bitcast.205), channel_id=1, source_target_pairs={{0,16},{4,12},{8,24},{12,4},{16,0},{20,28},{24,8},{28,20},{1,17},{... | collective-permute-start | bytes 7962632 | tf_op jit(solution)/shard_map/ppermute | solution.py:590
  412.2 208.9 %reduce-scatter.8.cloned.1.call-start = ((), (), s32[]{:S(2)}) async-start(), calls=%async_computation.10 | async-start | bytes 4423680 | tf_op jit(solution)/shard_map/reduce_scatter | solution.py:603
  519.7 73.8 %all-to-all-start.2 = ((bf16[8,128,1536]{2,1,0:T(8,128)(2,1)}), bf16[8,128,1536]{2,1,0:T(8,128)(2,1)}, u32[]{:S(2)}, u32[]{:S(2)}) async-start(bf16[8,128,1536]{2,1,0:T(8,128)(2,1)} %broadcast_select_fusion.1), calls=%async_computation.3 | async-start | bytes 6291456 | tf_op jit(solution)/shard_map/all_to_all | solution.py:634
  540.8 52.7 %collective-permute-start.49 = (bf16[2304,384]{1,0:T(8,128)(2,1)}, bf16[2304,384]{1,0:T(8,128)(2,1)}, u32[]{:S(2)}, u32[]{:S(2)}) collective-permute-start(bf16[2304,384]{1,0:T(8,128)(2,1)} %add_convert_fusion.5), channel_id=1, source_target_pairs={{0,8},{4,20},{8,0},{12,28},{16,24},{20,4},{24,16},{28,12},{1,9},{5... | collective-permute-start | bytes 5308424 | tf_op jit(solution)/shard_map/ppermute | solution.py:587
  542.5 50.9 %collective-permute-start.50 = (bf16[384,1152]{1,0:T(8,128)(2,1)}, bf16[384,1152]{1,0:T(8,128)(2,1)}, u32[]{:S(2)}, u32[]{:S(2)}) collective-permute-start(bf16[384,1152]{1,0:T(8,128)(2,1)} %reduce-scatter.6.cloned.1.call-done), channel_id=1, source_target_pairs={{0,8},{4,20},{8,0},{12,28},{16,24},{20,4},{24,16},{28,12},{1,9},{5... | collective-permute-start | bytes 2654216 | tf_op jit(solution)/shard_map/ppermute | solution.py:587
  598.3 56.5 %collective-permute-start.60 = (bf16[256,1920]{1,0:T(8,128)(2,1)}, bf16[256,1920]{1,0:T(8,128)(2,1)}, u32[]{:S(2)}, u32[]{:S(2)}) collective-permute-start(bf16[256,1920]{1,0:T(8,128)(2,1)} %bitcast.222), channel_id=1, source_target_pairs={{0,4},{4,0},{8,12},{12,8},{16,20},{20,16},{24,28},{28,24},{1,5},{5... | collective-permute-start | bytes 2949128 | tf_op jit(solution)/shard_map/ppermute | solution.py:600
  598.3 106.4 %all-to-all-start.3 = ((bf16[8,128,1536]{2,1,0:T(8,128)(2,1)}), bf16[8,128,1536]{2,1,0:T(8,128)(2,1)}, u32[]{:S(2)}, u32[]{:S(2)}) async-start(bf16[8,128,1536]{2,1,0:T(8,128)(2,1)} %broadcast_select_fusion), calls=%async_computation.5 | async-start | bytes 6291456 | tf_op jit(solution)/shard_map/all_to_all | solution.py:634
  602.8 117.4 %reduce-scatter.10.cloned.1.call-start = ((), (), s32[]{:S(2)}) async-start(), calls=%async_computation.11 | async-start | bytes 2211840 | tf_op jit(solution)/shard_map/reduce_scatter | solution.py:603
  613.7 130.1 %reduce-scatter.12.cloned.1.call-start = ((), (), s32[]{:S(2)}) async-start(), calls=%async_computation.12 | async-start | bytes 737280 | tf_op jit(solution)/shard_map/reduce_scatter | solution.py:603
  657.1 47.5 %collective-permute-start.62 = (bf16[256,1920]{1,0:T(8,128)(2,1)}, bf16[256,1920]{1,0:T(8,128)(2,1)}, u32[]{:S(2)}, u32[]{:S(2)}) collective-permute-start(bf16[256,1920]{1,0:T(8,128)(2,1)} %add_convert_fusion.13), channel_id=1, source_target_pairs={{0,16},{4,12},{8,24},{12,4},{16,0},{20,28},{24,8},{28,20},{1,17},{... | collective-permute-start | bytes 2949128 | tf_op jit(solution)/shard_map/ppermute | solution.py:590
  658.3 46.3 %collective-permute-start.63 = (bf16[256,1920]{1,0:T(8,128)(2,1)}, bf16[256,1920]{1,0:T(8,128)(2,1)}, u32[]{:S(2)}, u32[]{:S(2)}) collective-permute-start(bf16[256,1920]{1,0:T(8,128)(2,1)} %add_convert_fusion.12), channel_id=1, source_target_pairs={{0,16},{4,12},{8,24},{12,4},{16,0},{20,28},{24,8},{28,20},{1,17},{... | collective-permute-start | bytes 2949128 | tf_op jit(solution)/shard_map/ppermute | solution.py:590
  713.4 48.6 %reduce-scatter.14.cloned.1.call-start = ((), (), s32[]{:S(2)}) async-start(), calls=%async_computation.13 | async-start | bytes 1228800 | tf_op jit(solution)/shard_map/reduce_scatter | solution.py:603
  (165 other events, 2461.4 us)
Sparse Core Ops, SparseCore 0:
  34.4 53.2 all-gather.6
  89.9 68.7 all-gather.8
  186.5 39.6 all-gather.10
  412.3 67.3 reduce-scatter.5
  481.8 66.6 reduce-scatter.7
  613.8 38.9 reduce-scatter.9
  713.5 20.9 reduce-scatter.11
  737.5 24.5 reduce-scatter.13

commit v4 on v3

--- a/solution.py
+++ b/solution.py
@@ -625,9 +625,8 @@
     return out.at[landing].set(flat, mode="drop")
 
 
-def back_to_slots(rows, is_live, safe_place, ranks):
-    chosen = jnp.where(is_live[:, None], rows[safe_place], jnp.zeros((), rows.dtype))
-    return chosen.reshape(ranks, -1, rows.shape[1])
+def back_to_slots(rows, safe_place, ranks):
+    return rows[safe_place].reshape(ranks, -1, rows.shape[1])
 
 
 def exchange(x):
@@ -752,7 +751,7 @@
     d_packed_norm, grad_gain_attn = attn_norm_pull(d_normed)
     grad_rows = rounded(d_hidden + d_packed_norm)
     block_arrived, grad_arrived = (
-        exchange(back_to_slots(rows, is_live, safe_place, ranks)).reshape(-1, rows.shape[1])[
+        exchange(back_to_slots(rows, safe_place, ranks)).reshape(-1, rows.shape[1])[
             send_slot
         ]
         for rows in (block_rows, grad_rows)
@@ -825,10 +824,10 @@
     labels = jnp.stack([send_place // 2, send_place % 2, jnp.ones_like(send_place)], axis=1)
     labels = jnp.pad(labels.astype(jnp.bfloat16), ((0, 0), (0, 125)))
     token_slots = to_slots(jnp.concatenate([tokens[0], labels], axis=1), send_slot, ranks)
-    *early, token_slots, cotangent_rows, out_mine, down_mine, gate_up_mine = fence(
-        *early, token_slots, cotangent[0], my_rows(w_out), w_down, w_gate_up
-    )
     got_tokens = exchange(token_slots)
+    *early, cotangent_rows, out_mine, down_mine, gate_up_mine = fence(
+        *early, after(cotangent[0], token_slots), my_rows(w_out), w_down, w_gate_up
+    )
     early = jnp.stack(early)
     gain_rows = early[:, :, split : split + gain_width].reshape(depth - 1, 2, shard_rows)
     early = early[:, :, :split]
@@ -896,24 +895,24 @@
     kv_w = kv_w.reshape(model_width, 2 * HD)
     query_lin = dot(normed, query_w)
     pair = pair_of(dot(normed, kv_w), cosine, sine)
-    down_u, down_v, down_0, out_3, query_lin, pair = fence(
-        down_u, down_v, down_0, out_3, query_lin, pair
-    )
-
-    pair_rows = with_earlier(pair, reach)
-    down_2, down_1 = plane.swap(down_u), plane.swap(down_v)
     (out_w,) = put_pieces(
         [out, out_u, out_v, out_d, out_0, out_1, out_2, out_3],
         after(at, pair),
         [by_parts(w_out)],
     )
     out_w = out_w.reshape(model_width, model_width)
+    down_u, down_v, down_0, out_w, query_lin, pair = fence(
+        down_u, down_v, down_0, out_w, query_lin, pair
+    )
+
+    pair_rows = with_earlier(pair, reach)
+    down_2, down_1 = plane.swap(down_u), plane.swap(down_v)
     down_d = down_of(after(w_down, gate_up_piece), plane.chips[3])
     gate_up_piece = rest(gate_up_piece, level)
     gate_up_piece = gate_up_piece.reshape((depth - 1) * shard_rows, quarter)
     packed_grad = from_slots(after(got_cotangent, gate_up_piece), landing)
-    pair_rows, down_2, down_1, out_w, gate_up_piece, packed_grad = fence(
-        pair_rows, down_2, down_1, out_w, gate_up_piece, packed_grad
+    pair_rows, down_2, down_1, gate_up_piece, packed_grad = fence(
+        pair_rows, down_2, down_1, gate_up_piece, packed_grad
     )
 
     gate_up_u, gate_up_v, gate_up_0 = (
@@ -998,9 +997,10 @@
     d_query_lin, d_pairs = attend_back(
         queries, after(d_mixed, total), totals, tables, pair_rows, pairs_across, *docs
     )
-    from_down_d, from_down_v, d_query_lin, d_pairs, block_sum = fence(
-        from_down_d, from_down_v, d_query_lin, d_pairs, block_sum
-    )
+    from_down_d, from_down_v, d_query_lin, d_pairs, block_sum, part_d = fence(
+        from_down_d, from_down_v, d_query_lin, d_pairs, block_sum, part_d
+    )
+    part_d_u = plane.first(part_d)
 
     def by_rows(grad):
         pieces = rounded(grad).reshape(depth, ranks, part_rows, grad.shape[1])
@@ -1011,10 +1011,10 @@
 
     d_own = owners_sum(d_pairs, row_count, reach)
     down_u = added(down_sums[1], from_down_d)
-    block_slots = back_to_slots(rounded(block_sum), is_live, safe_place, ranks)
-    d_own, down_u, block_slots, part_d = fence(d_own, down_u, block_slots, part_d)
+    block_slots = back_to_slots(rounded(block_sum), safe_place, ranks)
+    d_own, down_u, block_slots, part_d_u = fence(d_own, down_u, block_slots, part_d_u)
     home_out = exchange(block_slots)
-    from_down_u, part_d_u = plane.first(down_u), plane.first(part_d)
+    from_down_u, part_d = plane.first(down_u), plane.second(part_d_u)
     grad_out = dot_rows(mixed, after(d_branch, block_slots))
     out_terms = [p.reshape(depth * part_rows, model_width) for p in by_rows(grad_out)]
     out_swaps = [plane.swap(term) for term in out_terms[4:]]
@@ -1041,13 +1041,12 @@
         )
         for q, k in zip(by_rows(grad_query), by_rows(grad_kv))
     ]
-    grad_slots = back_to_slots(after(grad_rows, *early_terms), is_live, safe_place, ranks)
-    from_down_u, part_d_u, early_terms, out_swaps, grad_slots, home_out = fence(
-        from_down_u, part_d_u, early_terms, out_swaps, grad_slots, home_out
+    grad_slots = back_to_slots(after(grad_rows, *early_terms), safe_place, ranks)
+    from_down_u, part_d, early_terms, out_swaps, grad_slots, home_out = fence(
+        from_down_u, part_d, early_terms, out_swaps, grad_slots, home_out
     )
 
     home_grad = exchange(grad_slots)
-    part_d = plane.second(part_d_u)
     early_swaps = [plane.swap(term) for term in early_terms[4:]]
     out_d, out_v = added(out_terms[3], out_swaps[3]), added(out_terms[2], out_swaps[1])
     out_from_d, out_from_v = plane.second(out_d), plane.second(out_v)
@@ -1056,8 +1055,8 @@
     early_d = added(early_terms[3], early_swaps[3])
     early_v = added(early_terms[2], early_swaps[1])
     block_arrived = home_out.reshape(-1, model_width)[send_slot]
-    part_d, out_from_d, out_from_v, early_d, early_v, early_swaps, part_0, block_arrived = fence(
-        part_d, out_from_d, out_from_v, early_d, early_v, early_swaps, part_0, block_arrived
+    out_from_d, out_from_v, early_d, early_v, early_swaps, part_0, block_arrived = fence(
+        out_from_d, out_from_v, early_d, early_v, early_swaps, part_0, block_arrived
     )
 
     mine_gate_up = added(part_0, part_d)

time: 805 us -> 788 us (0.979)
  waiting for transfers between devices: 239 us -> 225 us
  other arithmetic: 109 us -> 100 us
    ppermute x23, waiting for transfers between devices: 63.5 us -> 53.6 us  [second(): return lax.ppermute(x, 'seq', self.second_pairs)]
    unnamed x168 -> x172, local copies, waits for them, and re-layouts: 22.8 us -> 24.6 us
  transfers between devices with their start and end apart: 106 -> 106, of which waited for: 28 -> 29; matrix products, arithmetic and copies ran while one was open for 25% -> 25% of each run, Pallas kernels for 26% -> 26%
where the time goes in v4:
time: 788 us; the launch traced here: 777 us
  waiting for transfers between devices  225 us (29%)
  Pallas kernels  205 us (26%)
  local copies, waits for them, and re-layouts  104 us (13%)
  other arithmetic  100 us (13%)
  starting transfers between devices  98.2 us (12%)
  matrix products  28.3 us (4%)
  between operations  15.8 us (2%)
    ppermute x13, waiting for transfers between devices, first(): return lax.ppermute(x, 'seq', self.first_pairs)  140 us
    pallas_call x4, Pallas kernels, feed(): pl.pallas_call(kernel, in_specs=[pl.BlockSpec(memory_space=pltpu.SMEM), i...  115 us
    convert_element_type x24, other arithmetic, rounded(): return x.astype(jnp.bfloat16)  70.5 us
    ppermute x23, waiting for transfers between devices, second(): return lax.ppermute(x, 'seq', self.second_pairs)  53.6 us
    ppermute x23, starting transfers between devices, second(): return lax.ppermute(x, 'seq', self.second_pairs)  27.1 us
    pallas_call x1, Pallas kernels, attend_back(): pl.pallas_call(kernel, grid=(rows // block, couples), in_specs=[tile, til...  25.8 us
    unnamed x172, local copies, waits for them, and re-layouts  24.6 us
    pallas_call x1, Pallas kernels, attend(): pl.pallas_call(kernel, grid=(rows // block, couples), in_specs=[tile, tab...  21.1 us
  transfers between devices with their start and end apart: 106, of which 29 were waited for; matrix products, arithmetic and copies ran while one was open for 25% of the time, Pallas kernels for 26%

profile of v4, /device:TPU:0, one launch (start us, length us, event | category | flops | bytes accessed | tf_op | source)
XLA Modules:
  0.0 776.8 jit_solution(1801688915853760917)
XLA Ops:
  21.3 6.3 scatter_custom_fusion
  69.0 12.7 %collective-permute-done.7 = bf16[48,1536]{1,0:T(8,128)(2,1)} collective-permute-done((bf16[48,1536]{1,0:T(8,128)(2,1)}, bf16[48,1536]{1,0:T(8,128)(2,1)}, u32[]{:S(2)}, u32[]{:S(2)}) %collective-permute-start.7) | collective-permute-done | bytes 147488 | tf_op jit(solution)/shard_map/ppermute | solution.py:595
  81.7 8.6 %collective-permute-done.3.refs_1_ = bf16[3,48,1920]{2,1,0:T(8,128)(2,1)S(1)} collective-permute-done((bf16[3,48,1920]{2,1,0:T(8,128)(2,1)S(1)}, bf16[3,48,1920]{2,1,0:T(8,128)(2,1)S(1)}, u32[]{:S(2)}, u32[]{:S(2)}) %collective-permute-start.3) | collective-permute-done | bytes 552992 | tf_op jit(solution)/shard_map/ppermute | solution.py:587
  97.2 8.1 %scatter_custom_fusion.2 = bf16[512,1664]{1,0:T(8,128)(2,1)} fusion(s32[1024]{0:T(1024)S(1)} %get-tuple-element.492, bf16[1024,1664]{1,0:T(8,128)(2,1)} %bitcast.21, bf16[]{:T(256)} %constant.192.clone.1), kind=kCustom, calls=%fused_computation.77 | custom fusion | bytes 1704448 | tf_op jit(solution)/shard_map/scatter | solution.py:625
  148.1 34.5 %collective-permute-done.19.refs_6_ = bf16[3,576,384]{2,1,0:T(8,128)(2,1)} collective-permute-done((bf16[3,576,384]{2,1,0:T(8,128)(2,1)}, bf16[3,576,384]{2,1,0:T(8,128)(2,1)}, u32[]{:S(2)}, u32[]{:S(2)}) %collective-permute-start.19) | collective-permute-done | bytes 1327136 | tf_op jit(solution)/shard_map/ppermute | solution.py:587
  195.8 7.5 scatter_custom_fusion.3.g_ref
  211.6 21.1 %shard_map.183 = (bf16[512,1536]{1,0:T(8,128)(2,1)}, bf16[512,1536]{1,0:T(8,128)(2,1)}, f32[4,2,512]{2,1,0:T(2,128)S(1)}) custom-call(f32[512,1536]{1,0:T(8,128)} %fusion.78.q_ref, f32[512,384]{1,0:T(8,128)S(1)} %copy-done.1, f32[512,384]{1,0:T(8,128)S(1)} %copy-done.3, f32[512,384]{1,0:T(8,128)S(1)} %copy-done.5, bf16[1536,384]{1,0:T(8,128)(2,1)S(1)} %copy.124.pairs_ref, ...), custom_call_target="tpu_custom_call" | custom-call | flops 100000000 | bytes 100000 | tf_op jit(solution)/shard_map/pallas_call | solution.py:170
  247.8 28.4 %shard_map.185 = (f32[512,1536]{1,0:T(8,128)}, f32[512,1536]{1,0:T(8,128)}, bf16[1536,1152]{1,0:T(8,128)(2,1)}, bf16[1536,1152]{1,0:T(8,128)(2,1)}, bf16[4,576,3...) custom-call(s32[8]{0:T(128)} %stack.133.facts_ref, ...), custom_call_target="tpu_custom_call" | custom-call | flops 100000000 | bytes 100000 | tf_op jit(solution)/shard_map/pallas_call | solution.py:540
  287.6 28.8 %shard_map.186 = (f32[512,1536]{1,0:T(8,128)}, f32[512,1536]{1,0:T(8,128)}, bf16[1536,1152]{1,0:T(8,128)(2,1)}, bf16[1536,1152]{1,0:T(8,128)(2,1)}, bf16[4,576,3...) custom-call(s32[8]{0:T(128)} %stack.134.facts_ref, ...), custom_call_target="tpu_custom_call", output_to_operand_aliasing={{0}: (7, {}), {1}: (16, {}), {4}: (17, {}), {5}: (18, {}), ... | custom-call | flops 100000000 | bytes 100000 | tf_op jit(solution)/shard_map/pallas_call | solution.py:540
  318.8 28.6 %shard_map.187 = (f32[512,1536]{1,0:T(8,128)}, f32[512,1536]{1,0:T(8,128)}, bf16[1536,1152]{1,0:T(8,128)(2,1)}, bf16[1536,1152]{1,0:T(8,128)(2,1)}, bf16[4,576,3...) custom-call(s32[8]{0:T(128)} %stack.135.facts_ref, ...), custom_call_target="tpu_custom_call", output_to_operand_aliasing={{0}: (7, {}), {1}: (16, {}), {4}: (17, {}), {5}: (18, {}), ... | custom-call | flops 100000000 | bytes 100000 | tf_op jit(solution)/shard_map/pallas_call | solution.py:540
  355.5 29.0 %shard_map.188 = (f32[512,1536]{1,0:T(8,128)}, f32[512,1536]{1,0:T(8,128)}, bf16[1536,1152]{1,0:T(8,128)(2,1)}, bf16[1536,1152]{1,0:T(8,128)(2,1)}, bf16[4,576,3...) custom-call(s32[8]{0:T(128)} %stack.136.facts_ref, ...), custom_call_target="tpu_custom_call", output_to_operand_aliasing={{0}: (7, {}), {1}: (16, {}), {4}: (17, {}), {5}: (18, {}), ... | custom-call | flops 100000000 | bytes 100000 | tf_op jit(solution)/shard_map/pallas_call | solution.py:540
  422.2 25.5 %collective-permute-done.39 = bf16[1536,1152]{1,0:T(8,128)(2,1)} collective-permute-done((bf16[1536,1152]{1,0:T(8,128)(2,1)}, bf16[1536,1152]{1,0:T(8,128)(2,1)}, u32[]{:S(2)}, u32[]{:S(2)}) %collective-permute-start.39) | collective-permute-done | bytes 3538976 | tf_op jit(solution)/shard_map/ppermute | solution.py:587
  449.8 7.7 add_convert_fusion
  460.9 25.8 %shard_map.189 = (bf16[512,1536]{1,0:T(8,128)(2,1)}, f32[1536,384]{1,0:T(8,128)}) custom-call(bf16[512,1536]{1,0:T(8,128)(2,1)} %get-tuple-element.393.q_ref, bf16[512,1536]{1,0:T(8,128)(2,1)} %convolution_convert_fusion.2.do_ref, f32[4,2,512]{2,1,0:T(2,128)S(1)} %get-tuple-element.400.total_ref, f32[512,384]{1,0:T(8,128)S(1)} %copy-done.2, ...), custom_call_target="tpu_custom_call" | custom-call | flops 100000000 | bytes 100000 | tf_op jit(solution)/shard_map/pallas_call | solution.py:242
  510.0 8.4 %collective-permute-done.49 = bf16[384,1152]{1,0:T(8,128)(2,1)} collective-permute-done((bf16[384,1152]{1,0:T(8,128)(2,1)}, bf16[384,1152]{1,0:T(8,128)(2,1)}, u32[]{:S(2)}, u32[]{:S(2)}) %collective-permute-start.49) | collective-permute-done | bytes 884768 | tf_op jit(solution)/shard_map/ppermute | solution.py:587
  562.8 16.6 %collective-permute-done.51 = bf16[384,1152]{1,0:T(8,128)(2,1)} collective-permute-done((bf16[384,1152]{1,0:T(8,128)(2,1)}, bf16[384,1152]{1,0:T(8,128)(2,1)}, u32[]{:S(2)}, u32[]{:S(2)}) %collective-permute-start.51) | collective-permute-done | bytes 884768 | tf_op jit(solution)/shard_map/ppermute | solution.py:590
  579.4 9.4 %collective-permute-done.50 = bf16[2304,384]{1,0:T(8,128)(2,1)} collective-permute-done((bf16[2304,384]{1,0:T(8,128)(2,1)}, bf16[2304,384]{1,0:T(8,128)(2,1)}, u32[]{:S(2)}, u32[]{:S(2)}) %collective-permute-start.50) | collective-permute-done | bytes 1769504 | tf_op jit(solution)/shard_map/ppermute | solution.py:587
  604.1 6.7 gather_fusion.3
  627.8 22.3 %collective-permute-done.64 = bf16[192,1536]{1,0:T(8,128)(2,1)S(1)} collective-permute-done((bf16[192,1536]{1,0:T(8,128)(2,1)S(1)}, bf16[192,1536]{1,0:T(8,128)(2,1)S(1)}, u32[]{:S(2)}, u32[]{:S(2)}) %collective-permute-start.64) | collective-permute-done | bytes 589856 | tf_op jit(solution)/shard_map/ppermute | solution.py:587
  650.2 19.0 %collective-permute-done.65.refs_1_ = bf16[384,1152]{1,0:T(8,128)(2,1)S(1)} collective-permute-done((bf16[384,1152]{1,0:T(8,128)(2,1)S(1)}, bf16[384,1152]{1,0:T(8,128)(2,1)S(1)}, u32[]{:S(2)}, u32[]{:S(2)}) %collective-permute-start.65) | collective-permute-done | bytes 884768 | tf_op jit(solution)/shard_map/ppermute | solution.py:587
  669.1 18.8 %collective-permute-done.66.refs_2_ = bf16[384,1152]{1,0:T(8,128)(2,1)S(1)} collective-permute-done((bf16[384,1152]{1,0:T(8,128)(2,1)S(1)}, bf16[384,1152]{1,0:T(8,128)(2,1)S(1)}, u32[]{:S(2)}, u32[]{:S(2)}) %collective-permute-start.66) | collective-permute-done | bytes 884768 | tf_op jit(solution)/shard_map/ppermute | solution.py:590
  695.8 6.7 gather_fusion.4
  717.9 8.5 %shard_map.190 = f32[384,9216]{1,0:T(8,128)} custom-call(s32[8]{0:T(128)S(1)} %stack.137.positions_ref, bf16[384,1152]{1,0:T(8,128)(2,1)S(1)} %add_convert_fusion.14.refs_0_, bf16[384,1152]{1,0:T(8,128)(2,1)S(1)} %collective-permute-done.65.refs_1_, bf16[384,1152]{1,0:T(8,128)(2,1)S(1)} %collective-permute-done.66.refs_2_, ...), custom_call_target="tpu_custom_call" | custom-call | tf_op jit(solution)/shard_map/pallas_call | solution.py:355
  731.1 6.2 collective-permute-done.79.refs_1_
  (523 shorter events, 365.9 us)
Async XLA Ops:
  7.2 110.2 %all-gather.7.cloned.1.call-start = ((), (), s32[]{:S(2)}) async-start(), calls=%async_computation.14 | async-start | bytes 2211840 | tf_op jit(solution)/shard_map/all_gather | solution.py:839
  34.2 56.1 %all-to-all-start = ((bf16[8,128,1664]{2,1,0:T(8,128)(2,1)}), bf16[8,128,1664]{2,1,0:T(8,128)(2,1)}, u32[]{:S(2)}, u32[]{:S(2)}) async-start(bf16[8,128,1664]{2,1,0:T(8,128)(2,1)} %bitcast.198), calls=%async_computation | async-start | bytes 6815744 | tf_op jit(solution)/shard_map/all_to_all | solution.py:633
  38.7 144.4 %all-gather.9.cloned.1.call-start = ((), (), s32[]{:S(2)}) async-start(), calls=%async_computation.15 | async-start | bytes 4423680 | tf_op jit(solution)/shard_map/all_gather | solution.py:845
  43.7 46.5 %collective-permute-start.3 = (bf16[3,48,1920]{2,1,0:T(8,128)(2,1)S(1)}, bf16[3,48,1920]{2,1,0:T(8,128)(2,1)S(1)}, u32[]{:S(2)}, u32[]{:S(2)}) collective-permute-start(bf16[3,48,1920]{2,1,0:T(8,128)(2,1)S(1)} %slice.123.refs_0_), channel_id=1, source_target_pairs={{0,8},{4,20},{8,0},{12,28},{16,24},{20,4},{24,16},{28,12},{1,9},{5... | collective-permute-start | bytes 1658888 | tf_op jit(solution)/shard_map/ppermute | solution.py:587
  45.7 44.6 %collective-permute-start.4 = (bf16[3,48,1920]{2,1,0:T(8,128)(2,1)S(1)}, bf16[3,48,1920]{2,1,0:T(8,128)(2,1)S(1)}, u32[]{:S(2)}, u32[]{:S(2)}) collective-permute-start(bf16[3,48,1920]{2,1,0:T(8,128)(2,1)S(1)} %slice.123.refs_0_), channel_id=1, source_target_pairs={{0,16},{4,12},{8,24},{12,4},{16,0},{20,28},{24,8},{28,20},{1,17},{... | collective-permute-start | bytes 1658888 | tf_op jit(solution)/shard_map/ppermute | solution.py:590
  112.7 83.1 %all-to-all-start.1 = ((bf16[8,128,1536]{2,1,0:T(8,128)(2,1)}), bf16[8,128,1536]{2,1,0:T(8,128)(2,1)}, u32[]{:S(2)}, u32[]{:S(2)}) async-start(bf16[8,128,1536]{2,1,0:T(8,128)(2,1)} %bitcast.199), calls=%async_computation.1 | async-start | bytes 6291456 | tf_op jit(solution)/shard_map/all_to_all | solution.py:633
  117.2 123.8 %all-gather.11.cloned.1.call-start = ((), (), s32[]{:S(2)}) async-start(), calls=%async_computation.16 | async-start | bytes 2211840 | tf_op jit(solution)/shard_map/all_gather | solution.py:839
  120.8 61.9 %collective-permute-start.19 = (bf16[3,576,384]{2,1,0:T(8,128)(2,1)}, bf16[3,576,384]{2,1,0:T(8,128)(2,1)}, u32[]{:S(2)}, u32[]{:S(2)}) collective-permute-start(bf16[3,576,384]{2,1,0:T(8,128)(2,1)} %shard_map.179.refs_5_), channel_id=1, source_target_pairs={{0,8},{4,20},{8,0},{12,28},{16,24},{20,4},{24,16},{28,12},{1,9},{5... | collective-permute-start | bytes 3981320 | tf_op jit(solution)/shard_map/ppermute | solution.py:587
  122.6 60.0 %collective-permute-start.20 = (bf16[3,576,384]{2,1,0:T(8,128)(2,1)}, bf16[3,576,384]{2,1,0:T(8,128)(2,1)}, u32[]{:S(2)}, u32[]{:S(2)}) collective-permute-start(bf16[3,576,384]{2,1,0:T(8,128)(2,1)} %shard_map.179.refs_5_), channel_id=1, source_target_pairs={{0,16},{4,12},{8,24},{12,4},{16,0},{20,28},{24,8},{28,20},{1,17},{... | collective-permute-start | bytes 3981320 | tf_op jit(solution)/shard_map/ppermute | solution.py:590
  124.1 58.6 %collective-permute-start.21 = (bf16[3,576,384]{2,1,0:T(8,128)(2,1)}, bf16[3,576,384]{2,1,0:T(8,128)(2,1)}, u32[]{:S(2)}, u32[]{:S(2)}) collective-permute-start(bf16[3,576,384]{2,1,0:T(8,128)(2,1)} %shard_map.179.refs_5_), channel_id=1, source_target_pairs={{0,4},{4,0},{8,12},{12,8},{16,20},{20,16},{24,28},{28,24},{1,5},{5... | collective-permute-start | bytes 3981320 | tf_op jit(solution)/shard_map/ppermute | solution.py:600
  185.0 304.6 %reduce-scatter.6.cloned.1.call-start = ((), (), s32[]{:S(2)}) async-start(), calls=%async_computation.9 | async-start | bytes 4423680 | tf_op jit(solution)/shard_map/reduce_scatter | solution.py:603
  206.7 69.5 %collective-permute-start.27 = (bf16[1152,1152]{1,0:T(8,128)(2,1)}, bf16[1152,1152]{1,0:T(8,128)(2,1)}, u32[]{:S(2)}, u32[]{:S(2)}) collective-permute-start(bf16[1152,1152]{1,0:T(8,128)(2,1)} %bitcast.202), channel_id=1, source_target_pairs={{0,8},{4,20},{8,0},{12,28},{16,24},{20,4},{24,16},{28,12},{1,9},{5... | collective-permute-start | bytes 7962632 | tf_op jit(solution)/shard_map/ppermute | solution.py:587
  207.2 69.0 %collective-permute-start.28 = (bf16[1152,1152]{1,0:T(8,128)(2,1)}, bf16[1152,1152]{1,0:T(8,128)(2,1)}, u32[]{:S(2)}, u32[]{:S(2)}) collective-permute-start(bf16[1152,1152]{1,0:T(8,128)(2,1)} %bitcast.203), channel_id=1, source_target_pairs={{0,16},{4,12},{8,24},{12,4},{16,0},{20,28},{24,8},{28,20},{1,17},{... | collective-permute-start | bytes 7962632 | tf_op jit(solution)/shard_map/ppermute | solution.py:590
  404.7 212.2 %reduce-scatter.8.cloned.1.call-start = ((), (), s32[]{:S(2)}) async-start(), calls=%async_computation.10 | async-start | bytes 4423680 | tf_op jit(solution)/shard_map/reduce_scatter | solution.py:603
  518.4 70.4 %all-to-all-start.2 = ((bf16[8,128,1536]{2,1,0:T(8,128)(2,1)}), bf16[8,128,1536]{2,1,0:T(8,128)(2,1)}, u32[]{:S(2)}, u32[]{:S(2)}) async-start(bf16[8,128,1536]{2,1,0:T(8,128)(2,1)} %bitcast.200), calls=%async_computation.3 | async-start | bytes 6291456 | tf_op jit(solution)/shard_map/all_to_all | solution.py:633
  530.5 58.3 %collective-permute-start.50 = (bf16[2304,384]{1,0:T(8,128)(2,1)}, bf16[2304,384]{1,0:T(8,128)(2,1)}, u32[]{:S(2)}, u32[]{:S(2)}) collective-permute-start(bf16[2304,384]{1,0:T(8,128)(2,1)} %add_convert_fusion.5), channel_id=1, source_target_pairs={{0,8},{4,20},{8,0},{12,28},{16,24},{20,4},{24,16},{28,12},{1,9},{5... | collective-permute-start | bytes 5308424 | tf_op jit(solution)/shard_map/ppermute | solution.py:587
  532.5 46.9 %collective-permute-start.51 = (bf16[384,1152]{1,0:T(8,128)(2,1)}, bf16[384,1152]{1,0:T(8,128)(2,1)}, u32[]{:S(2)}, u32[]{:S(2)}) collective-permute-start(bf16[384,1152]{1,0:T(8,128)(2,1)} %collective-permute-done.49), channel_id=1, source_target_pairs={{0,16},{4,12},{8,24},{12,4},{16,0},{20,28},{24,8},{28,20},{1,17},{... | collective-permute-start | bytes 2654216 | tf_op jit(solution)/shard_map/ppermute | solution.py:590
  595.5 92.4 %all-to-all-start.3 = ((bf16[8,128,1536]{2,1,0:T(8,128)(2,1)}), bf16[8,128,1536]{2,1,0:T(8,128)(2,1)}, u32[]{:S(2)}, u32[]{:S(2)}) async-start(bf16[8,128,1536]{2,1,0:T(8,128)(2,1)} %bitcast.94), calls=%async_computation.5 | async-start | bytes 6291456 | tf_op jit(solution)/shard_map/all_to_all | solution.py:633
  600.0 102.5 %reduce-scatter.10.cloned.1.call-start = ((), (), s32[]{:S(2)}) async-start(), calls=%async_computation.11 | async-start | bytes 2211840 | tf_op jit(solution)/shard_map/reduce_scatter | solution.py:603
  610.8 115.6 %reduce-scatter.12.cloned.1.call-start = ((), (), s32[]{:S(2)}) async-start(), calls=%async_computation.12 | async-start | bytes 737280 | tf_op jit(solution)/shard_map/reduce_scatter | solution.py:603
  621.7 66.2 %collective-permute-start.62 = (bf16[256,1920]{1,0:T(8,128)(2,1)}, bf16[256,1920]{1,0:T(8,128)(2,1)}, u32[]{:S(2)}, u32[]{:S(2)}) collective-permute-start(bf16[256,1920]{1,0:T(8,128)(2,1)} %add_convert_fusion.13), channel_id=1, source_target_pairs={{0,16},{4,12},{8,24},{12,4},{16,0},{20,28},{24,8},{28,20},{1,17},{... | collective-permute-start | bytes 2949128 | tf_op jit(solution)/shard_map/ppermute | solution.py:590
  624.3 63.7 %collective-permute-start.63 = (bf16[256,1920]{1,0:T(8,128)(2,1)}, bf16[256,1920]{1,0:T(8,128)(2,1)}, u32[]{:S(2)}, u32[]{:S(2)}) collective-permute-start(bf16[256,1920]{1,0:T(8,128)(2,1)} %add_convert_fusion.12), channel_id=1, source_target_pairs={{0,16},{4,12},{8,24},{12,4},{16,0},{20,28},{24,8},{28,20},{1,17},{... | collective-permute-start | bytes 2949128 | tf_op jit(solution)/shard_map/ppermute | solution.py:590
  625.9 62.1 %collective-permute-start.66 = (bf16[384,1152]{1,0:T(8,128)(2,1)S(1)}, bf16[384,1152]{1,0:T(8,128)(2,1)S(1)}, u32[]{:S(2)}, u32[]{:S(2)}) collective-permute-start(bf16[384,1152]{1,0:T(8,128)(2,1)S(1)} %add_convert_fusion.14.refs_0_), channel_id=1, source_target_pairs={{0,16},{4,12},{8,24},{12,4},{16,0},{20,28},{24,8},{28,20},{1,17},{... | collective-permute-start | bytes 2654216 | tf_op jit(solution)/shard_map/ppermute | solution.py:590
  695.8 49.0 %reduce-scatter.14.cloned.1.call-start = ((), (), s32[]{:S(2)}) async-start(), calls=%async_computation.13 | async-start | bytes 1228800 | tf_op jit(solution)/shard_map/reduce_scatter | solution.py:603
  (167 other events, 2258.5 us)
Sparse Core Ops, SparseCore 0:
  34.3 53.3 all-gather.6
  89.8 68.7 all-gather.8
  185.1 39.7 all-gather.10
  404.8 67.0 reduce-scatter.5
  474.0 66.6 reduce-scatter.7
  611.0 39.1 reduce-scatter.9
  695.9 21.3 reduce-scatter.11
  720.3 24.4 reduce-scatter.13

commit v5 on v4

--- a/solution.py
+++ b/solution.py
@@ -80,6 +80,25 @@
 
 def added(*terms):
     return rounded(sum(widened(term) for term in terms))
+
+
+def added_apart(*terms):
+    rows, width = terms[0].shape
+    steps = 4
+
+    def kernel(*refs):
+        refs[-1][...] = rounded(sum(widened(ref[...]) for ref in refs[:-1]))
+
+    block = pl.BlockSpec((rows // steps, width), lambda i: (i, 0))
+    return pl.pallas_call(
+        kernel,
+        grid=(steps,),
+        in_specs=[block] * len(terms),
+        out_specs=block,
+        out_shape=jax.ShapeDtypeStruct((rows, width), jnp.bfloat16),
+        compiler_params=pltpu.CompilerParams(vmem_limit_bytes=32 * 2**20),
+        cost_estimate=pl.CostEstimate(flops=10**6, bytes_accessed=10**5, transcendentals=0),
+    )(*terms)
 
 
 def dot(a, b):
@@ -922,10 +941,10 @@
     )
     pairs_across = pair_rows.T
     queries, mixed, totals = attend(query_lin, tables, pair_rows, pairs_across, *docs)
-    hidden_state = packed_f + dot(mixed, out_w)
+    down_d = rest(after(down_d, mixed), level)
+    down_3 = plane.swap(down_d)
+    hidden_state = packed_f + dot(after(mixed, down_d), out_w)
     ffn_in = rounded(rms_scale(hidden_state, gain_ffn))
-    down_d = rest(after(down_d, ffn_in), level)
-    down_3 = plane.swap(down_d)
 
     def chunk(slot, first_w, second_w, chunk_in, block_sum, back_sum, terms):
         facts = [plane.core, plane.chips[slot], plane.core, *plane.chips, level]
@@ -984,10 +1003,10 @@
     d_hidden = widened(packed_grad) + d_hidden_norm
     d_branch = rounded(d_hidden)
     d_mixed = rounded(dot_across(d_branch, out_w))
-    sum_d = added(after(own_d, d_mixed), swap_d)
+    sum_d = added_apart(after(own_d, d_mixed), swap_d)
     part_d = plane.down_columns(sum_d)
     down_sums = [
-        added(after(term, sum_d), down_swaps[match])
+        added_apart(after(term, sum_d), down_swaps[match])
         for term, match in zip(terms[:4], (0, 2, 1, 3))
     ]
     from_u, d_branch, d_mixed, down_sums = fence(from_u, d_branch, d_mixed, down_sums)

time: 788 us -> 782 us (level)
  other arithmetic: 100 us -> 83.8 us
  Pallas kernels: 205 us -> 220 us
    ppermute x13, waiting for transfers between devices: 140 us -> 115 us  [first(): return lax.ppermute(x, 'seq', self.first_pairs)]
    all_gather x1, waiting for transfers between devices: 0.01 us -> 19.7 us  [square_body(): gate_up_piece = lax.all_gather(gate_up_piece, 'fsdp', axis=0, tiled=False)]
    convert_element_type x24 -> x19, other arithmetic: 70.5 us -> 54.2 us  [rounded(): return x.astype(jnp.bfloat16)]
    pallas_call x0 -> x5, Pallas kernels: none -> 14.7 us  [added_apart(): pl.pallas_call(kernel, grid=(steps,), in_specs=[block] * len(terms), out_...]
    unnamed x172 -> x188, local copies, waits for them, and re-layouts: 24.6 us -> 28.6 us
  transfers between devices with their start and end apart: 106 -> 106, of which waited for: 29 -> 30; matrix products, arithmetic and copies ran while one was open for 25% -> 23% of each run, Pallas kernels for 26% -> 28%
where the time goes in v5:
time: 782 us; the launch traced here: 771 us
  Pallas kernels  220 us (28%)
  waiting for transfers between devices  218 us (28%)
  local copies, waits for them, and re-layouts  107 us (14%)
  starting transfers between devices  97.4 us (12%)
  other arithmetic  83.8 us (11%)
  matrix products  28.2 us (4%)
  between operations  16.2 us (2%)
    pallas_call x4, Pallas kernels, feed(): pl.pallas_call(kernel, in_specs=[pl.BlockSpec(memory_space=pltpu.SMEM), i...  115 us
    ppermute x13, waiting for transfers between devices, first(): return lax.ppermute(x, 'seq', self.first_pairs)  115 us
    convert_element_type x19, other arithmetic, rounded(): return x.astype(jnp.bfloat16)  54.2 us
    ppermute x23, waiting for transfers between devices, second(): return lax.ppermute(x, 'seq', self.second_pairs)  52.3 us
    unnamed x188, local copies, waits for them, and re-layouts  28.6 us
    ppermute x23, starting transfers between devices, second(): return lax.ppermute(x, 'seq', self.second_pairs)  26.4 us
    pallas_call x1, Pallas kernels, attend_back(): pl.pallas_call(kernel, grid=(rows // block, couples), in_specs=[tile, til...  25.9 us
    pallas_call x1, Pallas kernels, attend(): pl.pallas_call(kernel, grid=(rows // block, couples), in_specs=[tile, tab...  20.9 us
  transfers between devices with their start and end apart: 106, of which 30 were waited for; matrix products, arithmetic and copies ran while one was open for 23% of the time, Pallas kernels for 28%

profile of v5, /device:TPU:0, one launch (start us, length us, event | category | flops | bytes accessed | tf_op | source)
XLA Modules:
  0.0 770.9 jit_solution(14871748822211816340)
XLA Ops:
  69.0 12.7 %collective-permute-done.7 = bf16[48,1536]{1,0:T(8,128)(2,1)} collective-permute-done((bf16[48,1536]{1,0:T(8,128)(2,1)}, bf16[48,1536]{1,0:T(8,128)(2,1)}, u32[]{:S(2)}, u32[]{:S(2)}) %collective-permute-start.7) | collective-permute-done | bytes 147488 | tf_op jit(solution)/shard_map/ppermute | solution.py:614
  81.7 8.5 %collective-permute-done.3.refs_1_ = bf16[3,48,1920]{2,1,0:T(8,128)(2,1)S(1)} collective-permute-done((bf16[3,48,1920]{2,1,0:T(8,128)(2,1)S(1)}, bf16[3,48,1920]{2,1,0:T(8,128)(2,1)S(1)}, u32[]{:S(2)}, u32[]{:S(2)}) %collective-permute-start.3) | collective-permute-done | bytes 552992 | tf_op jit(solution)/shard_map/ppermute | solution.py:606
  97.1 8.0 %scatter_custom_fusion.2 = bf16[512,1664]{1,0:T(8,128)(2,1)} fusion(s32[1024]{0:T(1024)S(1)} %get-tuple-element.494, bf16[1024,1664]{1,0:T(8,128)(2,1)} %bitcast.21, bf16[]{:T(256)} %constant.192.clone.1), kind=kCustom, calls=%fused_computation.72 | custom fusion | bytes 1704448 | tf_op jit(solution)/shard_map/scatter | solution.py:644
  138.9 19.7 %all-gather.9.cloned.1.call-done = bf16[1536,1152]{1,0:T(8,128)(2,1)} async-done(((bf16[384,1152]{1,0:T(8,128)(2,1)}), bf16[1536,1152]{1,0:T(8,128)(2,1)}) %all-gather.9.cloned.1.call-update) | async-done | bytes 3538960 | tf_op jit(solution)/shard_map/all_gather | solution.py:864
  169.5 13.0 %collective-permute-done.19.refs_6_ = bf16[3,576,384]{2,1,0:T(8,128)(2,1)} collective-permute-done((bf16[3,576,384]{2,1,0:T(8,128)(2,1)}, bf16[3,576,384]{2,1,0:T(8,128)(2,1)}, u32[]{:S(2)}, u32[]{:S(2)}) %collective-permute-start.19) | collective-permute-done | bytes 1327136 | tf_op jit(solution)/shard_map/ppermute | solution.py:606
  192.7 7.5 scatter_custom_fusion.3.g_ref
  209.8 20.9 %shard_map.183 = (bf16[512,1536]{1,0:T(8,128)(2,1)}, bf16[512,1536]{1,0:T(8,128)(2,1)}, f32[4,2,512]{2,1,0:T(2,128)S(1)}) custom-call(f32[512,1536]{1,0:T(8,128)} %fusion.78.q_ref, f32[512,384]{1,0:T(8,128)S(1)} %copy-done.15, f32[512,384]{1,0:T(8,128)S(1)} %copy-done.17, f32[512,384]{1,0:T(8,128)S(1)} %copy-done.19, bf16[1536,384]{1,0:T(8,128)(2,1)S(1)} %copy.124.pairs_ref, ...), custom_call_target="tpu_custom_call" | custom-call | flops 100000000 | bytes 100000 | tf_op jit(solution)/shard_map/pallas_call | solution.py:189
  242.7 28.4 %shard_map.185 = (f32[512,1536]{1,0:T(8,128)}, f32[512,1536]{1,0:T(8,128)}, bf16[1536,1152]{1,0:T(8,128)(2,1)}, bf16[1536,1152]{1,0:T(8,128)(2,1)}, bf16[4,576,3...) custom-call(s32[8]{0:T(128)} %stack.133.facts_ref, ...), custom_call_target="tpu_custom_call" | custom-call | flops 100000000 | bytes 100000 | tf_op jit(solution)/shard_map/pallas_call | solution.py:559
  282.6 28.8 %shard_map.186 = (f32[512,1536]{1,0:T(8,128)}, f32[512,1536]{1,0:T(8,128)}, bf16[1536,1152]{1,0:T(8,128)(2,1)}, bf16[1536,1152]{1,0:T(8,128)(2,1)}, bf16[4,576,3...) custom-call(s32[8]{0:T(128)} %stack.134.facts_ref, ...), custom_call_target="tpu_custom_call", output_to_operand_aliasing={{0}: (7, {}), {1}: (16, {}), {4}: (17, {}), {5}: (18, {}), ... | custom-call | flops 100000000 | bytes 100000 | tf_op jit(solution)/shard_map/pallas_call | solution.py:559
  313.8 28.6 %shard_map.187 = (f32[512,1536]{1,0:T(8,128)}, f32[512,1536]{1,0:T(8,128)}, bf16[1536,1152]{1,0:T(8,128)(2,1)}, bf16[1536,1152]{1,0:T(8,128)(2,1)}, bf16[4,576,3...) custom-call(s32[8]{0:T(128)} %stack.135.facts_ref, ...), custom_call_target="tpu_custom_call", output_to_operand_aliasing={{0}: (7, {}), {1}: (16, {}), {4}: (17, {}), {5}: (18, {}), ... | custom-call | flops 100000000 | bytes 100000 | tf_op jit(solution)/shard_map/pallas_call | solution.py:559
  350.4 29.0 %shard_map.188 = (f32[512,1536]{1,0:T(8,128)}, f32[512,1536]{1,0:T(8,128)}, bf16[1536,1152]{1,0:T(8,128)(2,1)}, bf16[1536,1152]{1,0:T(8,128)(2,1)}, bf16[4,576,3...) custom-call(s32[8]{0:T(128)} %stack.136.facts_ref, ...), custom_call_target="tpu_custom_call", output_to_operand_aliasing={{0}: (7, {}), {1}: (16, {}), {4}: (17, {}), {5}: (18, {}), ... | custom-call | flops 100000000 | bytes 100000 | tf_op jit(solution)/shard_map/pallas_call | solution.py:559
  420.6 20.7 %collective-permute-done.39 = bf16[1536,1152]{1,0:T(8,128)(2,1)} collective-permute-done((bf16[1536,1152]{1,0:T(8,128)(2,1)}, bf16[1536,1152]{1,0:T(8,128)(2,1)}, u32[]{:S(2)}, u32[]{:S(2)}) %collective-permute-start.39) | collective-permute-done | bytes 3538976 | tf_op jit(solution)/shard_map/ppermute | solution.py:606
  443.4 7.7 %add_convert_fusion = bf16[1536,1152]{1,0:T(8,128)(2,1)} fusion(bf16[1536,1152]{1,0:T(8,128)(2,1)} %collective-permute-done.39, bf16[1536,1152]{1,0:T(8,128)(2,1)} %collective-permute-done.37, bf16[1536,1152]{1,0:T(8,128)(2,1)} %collective-permute-done.34, bf16[1536,1152]{1,0:T(8,128)(2,1)S(1)} %copy-done.50), kind=kLoop, calls=%fused_computation.11 | loop fusion | flops 14155776 | bytes 17694720 | tf_op jit(solution)/shard_map/convert_element_type | solution.py:74
  456.1 25.9 %shard_map.194 = (bf16[512,1536]{1,0:T(8,128)(2,1)}, f32[1536,384]{1,0:T(8,128)}) custom-call(bf16[512,1536]{1,0:T(8,128)(2,1)} %get-tuple-element.395.q_ref, bf16[512,1536]{1,0:T(8,128)(2,1)} %convolution_convert_fusion.2.do_ref, f32[4,2,512]{2,1,0:T(2,128)S(1)} %get-tuple-element.402.total_ref, f32[512,384]{1,0:T(8,128)S(1)} %copy-done.16, ...), custom_call_target="tpu_custom_call" | custom-call | flops 100000000 | bytes 100000 | tf_op jit(solution)/shard_map/pallas_call | solution.py:261
  503.1 8.8 %collective-permute-done.49 = bf16[384,1152]{1,0:T(8,128)(2,1)} collective-permute-done((bf16[384,1152]{1,0:T(8,128)(2,1)}, bf16[384,1152]{1,0:T(8,128)(2,1)}, u32[]{:S(2)}, u32[]{:S(2)}) %collective-permute-start.49) | collective-permute-done | bytes 884768 | tf_op jit(solution)/shard_map/ppermute | solution.py:606
  556.6 16.5 %collective-permute-done.51 = bf16[384,1152]{1,0:T(8,128)(2,1)} collective-permute-done((bf16[384,1152]{1,0:T(8,128)(2,1)}, bf16[384,1152]{1,0:T(8,128)(2,1)}, u32[]{:S(2)}, u32[]{:S(2)}) %collective-permute-start.51) | collective-permute-done | bytes 884768 | tf_op jit(solution)/shard_map/ppermute | solution.py:609
  573.1 9.6 %collective-permute-done.50 = bf16[2304,384]{1,0:T(8,128)(2,1)} collective-permute-done((bf16[2304,384]{1,0:T(8,128)(2,1)}, bf16[2304,384]{1,0:T(8,128)(2,1)}, u32[]{:S(2)}, u32[]{:S(2)}) %collective-permute-start.50) | collective-permute-done | bytes 1769504 | tf_op jit(solution)/shard_map/ppermute | solution.py:606
  598.0 6.7 gather_fusion.3
  620.9 23.1 %collective-permute-done.64 = bf16[192,1536]{1,0:T(8,128)(2,1)S(1)} collective-permute-done((bf16[192,1536]{1,0:T(8,128)(2,1)S(1)}, bf16[192,1536]{1,0:T(8,128)(2,1)S(1)}, u32[]{:S(2)}, u32[]{:S(2)}) %collective-permute-start.64) | collective-permute-done | bytes 589856 | tf_op jit(solution)/shard_map/ppermute | solution.py:606
  644.0 19.0 %collective-permute-done.65.refs_1_ = bf16[384,1152]{1,0:T(8,128)(2,1)S(1)} collective-permute-done((bf16[384,1152]{1,0:T(8,128)(2,1)S(1)}, bf16[384,1152]{1,0:T(8,128)(2,1)S(1)}, u32[]{:S(2)}, u32[]{:S(2)}) %collective-permute-start.65) | collective-permute-done | bytes 884768 | tf_op jit(solution)/shard_map/ppermute | solution.py:606
  663.0 18.9 %collective-permute-done.66.refs_2_ = bf16[384,1152]{1,0:T(8,128)(2,1)S(1)} collective-permute-done((bf16[384,1152]{1,0:T(8,128)(2,1)S(1)}, bf16[384,1152]{1,0:T(8,128)(2,1)S(1)}, u32[]{:S(2)}, u32[]{:S(2)}) %collective-permute-start.66) | collective-permute-done | bytes 884768 | tf_op jit(solution)/shard_map/ppermute | solution.py:609
  689.7 6.7 gather_fusion.4
  711.8 8.5 %shard_map.195 = f32[384,9216]{1,0:T(8,128)} custom-call(s32[8]{0:T(128)S(1)} %stack.137.positions_ref, bf16[384,1152]{1,0:T(8,128)(2,1)S(1)} %add_convert_fusion.9.refs_0_, bf16[384,1152]{1,0:T(8,128)(2,1)S(1)} %collective-permute-done.65.refs_1_, bf16[384,1152]{1,0:T(8,128)(2,1)S(1)} %collective-permute-done.66.refs_2_, ...), custom_call_target="tpu_custom_call" | custom-call | tf_op jit(solution)/shard_map/pallas_call | solution.py:374
  724.7 6.4 collective-permute-done.79.refs_1_
  (539 shorter events, 371.2 us)
Async XLA Ops:
  7.2 110.1 %all-gather.7.cloned.1.call-start = ((), (), s32[]{:S(2)}) async-start(), calls=%async_computation.14 | async-start | bytes 2211840 | tf_op jit(solution)/shard_map/all_gather | solution.py:858
  34.2 56.1 %all-to-all-start = ((bf16[8,128,1664]{2,1,0:T(8,128)(2,1)}), bf16[8,128,1664]{2,1,0:T(8,128)(2,1)}, u32[]{:S(2)}, u32[]{:S(2)}) async-start(bf16[8,128,1664]{2,1,0:T(8,128)(2,1)} %bitcast.199), calls=%async_computation | async-start | bytes 6815744 | tf_op jit(solution)/shard_map/all_to_all | solution.py:652
  38.7 120.0 %all-gather.9.cloned.1.call-start = ((), (), s32[]{:S(2)}) async-start(), calls=%async_computation.15 | async-start | bytes 4423680 | tf_op jit(solution)/shard_map/all_gather | solution.py:864
  43.7 46.5 %collective-permute-start.3 = (bf16[3,48,1920]{2,1,0:T(8,128)(2,1)S(1)}, bf16[3,48,1920]{2,1,0:T(8,128)(2,1)S(1)}, u32[]{:S(2)}, u32[]{:S(2)}) collective-permute-start(bf16[3,48,1920]{2,1,0:T(8,128)(2,1)S(1)} %slice.123.refs_0_), channel_id=1, source_target_pairs={{0,8},{4,20},{8,0},{12,28},{16,24},{20,4},{24,16},{28,12},{1,9},{5... | collective-permute-start | bytes 1658888 | tf_op jit(solution)/shard_map/ppermute | solution.py:606
  45.6 44.6 %collective-permute-start.4 = (bf16[3,48,1920]{2,1,0:T(8,128)(2,1)S(1)}, bf16[3,48,1920]{2,1,0:T(8,128)(2,1)S(1)}, u32[]{:S(2)}, u32[]{:S(2)}) collective-permute-start(bf16[3,48,1920]{2,1,0:T(8,128)(2,1)S(1)} %slice.123.refs_0_), channel_id=1, source_target_pairs={{0,16},{4,12},{8,24},{12,4},{16,0},{20,28},{24,8},{28,20},{1,17},{... | collective-permute-start | bytes 1658888 | tf_op jit(solution)/shard_map/ppermute | solution.py:609
  112.6 80.0 %all-to-all-start.1 = ((bf16[8,128,1536]{2,1,0:T(8,128)(2,1)}), bf16[8,128,1536]{2,1,0:T(8,128)(2,1)}, u32[]{:S(2)}, u32[]{:S(2)}) async-start(bf16[8,128,1536]{2,1,0:T(8,128)(2,1)} %bitcast.200), calls=%async_computation.1 | async-start | bytes 6291456 | tf_op jit(solution)/shard_map/all_to_all | solution.py:652
  117.1 113.7 %all-gather.11.cloned.1.call-start = ((), (), s32[]{:S(2)}) async-start(), calls=%async_computation.16 | async-start | bytes 2211840 | tf_op jit(solution)/shard_map/all_gather | solution.py:858
  120.7 61.8 %collective-permute-start.19 = (bf16[3,576,384]{2,1,0:T(8,128)(2,1)}, bf16[3,576,384]{2,1,0:T(8,128)(2,1)}, u32[]{:S(2)}, u32[]{:S(2)}) collective-permute-start(bf16[3,576,384]{2,1,0:T(8,128)(2,1)} %shard_map.179.refs_5_), channel_id=1, source_target_pairs={{0,8},{4,20},{8,0},{12,28},{16,24},{20,4},{24,16},{28,12},{1,9},{5... | collective-permute-start | bytes 3981320 | tf_op jit(solution)/shard_map/ppermute | solution.py:606
  122.5 60.0 %collective-permute-start.20 = (bf16[3,576,384]{2,1,0:T(8,128)(2,1)}, bf16[3,576,384]{2,1,0:T(8,128)(2,1)}, u32[]{:S(2)}, u32[]{:S(2)}) collective-permute-start(bf16[3,576,384]{2,1,0:T(8,128)(2,1)} %shard_map.179.refs_5_), channel_id=1, source_target_pairs={{0,16},{4,12},{8,24},{12,4},{16,0},{20,28},{24,8},{28,20},{1,17},{... | collective-permute-start | bytes 3981320 | tf_op jit(solution)/shard_map/ppermute | solution.py:609
  124.0 58.5 %collective-permute-start.21 = (bf16[3,576,384]{2,1,0:T(8,128)(2,1)}, bf16[3,576,384]{2,1,0:T(8,128)(2,1)}, u32[]{:S(2)}, u32[]{:S(2)}) collective-permute-start(bf16[3,576,384]{2,1,0:T(8,128)(2,1)} %shard_map.179.refs_5_), channel_id=1, source_target_pairs={{0,4},{4,0},{8,12},{12,8},{16,20},{20,16},{24,28},{28,24},{1,5},{5... | collective-permute-start | bytes 3981320 | tf_op jit(solution)/shard_map/ppermute | solution.py:619
  160.5 322.7 %reduce-scatter.6.cloned.1.call-start = ((), (), s32[]{:S(2)}) async-start(), calls=%async_computation.9 | async-start | bytes 4423680 | tf_op jit(solution)/shard_map/reduce_scatter | solution.py:622
  203.2 67.9 %collective-permute-start.27 = (bf16[1152,1152]{1,0:T(8,128)(2,1)}, bf16[1152,1152]{1,0:T(8,128)(2,1)}, u32[]{:S(2)}, u32[]{:S(2)}) collective-permute-start(bf16[1152,1152]{1,0:T(8,128)(2,1)} %bitcast.204), channel_id=1, source_target_pairs={{0,8},{4,20},{8,0},{12,28},{16,24},{20,4},{24,16},{28,12},{1,9},{5... | collective-permute-start | bytes 7962632 | tf_op jit(solution)/shard_map/ppermute | solution.py:606
  203.8 67.4 %collective-permute-start.28 = (bf16[1152,1152]{1,0:T(8,128)(2,1)}, bf16[1152,1152]{1,0:T(8,128)(2,1)}, u32[]{:S(2)}, u32[]{:S(2)}) collective-permute-start(bf16[1152,1152]{1,0:T(8,128)(2,1)} %bitcast.205), channel_id=1, source_target_pairs={{0,16},{4,12},{8,24},{12,4},{16,0},{20,28},{24,8},{28,20},{1,17},{... | collective-permute-start | bytes 7962632 | tf_op jit(solution)/shard_map/ppermute | solution.py:609
  399.5 211.3 %reduce-scatter.8.cloned.1.call-start = ((), (), s32[]{:S(2)}) async-start(), calls=%async_computation.10 | async-start | bytes 4423680 | tf_op jit(solution)/shard_map/reduce_scatter | solution.py:622
  511.9 70.8 %all-to-all-start.2 = ((bf16[8,128,1536]{2,1,0:T(8,128)(2,1)}), bf16[8,128,1536]{2,1,0:T(8,128)(2,1)}, u32[]{:S(2)}, u32[]{:S(2)}) async-start(bf16[8,128,1536]{2,1,0:T(8,128)(2,1)} %bitcast.201), calls=%async_computation.3 | async-start | bytes 6291456 | tf_op jit(solution)/shard_map/all_to_all | solution.py:652
  524.2 58.5 %collective-permute-start.50 = (bf16[2304,384]{1,0:T(8,128)(2,1)}, bf16[2304,384]{1,0:T(8,128)(2,1)}, u32[]{:S(2)}, u32[]{:S(2)}) collective-permute-start(bf16[2304,384]{1,0:T(8,128)(2,1)} %add_convert_fusion.4), channel_id=1, source_target_pairs={{0,8},{4,20},{8,0},{12,28},{16,24},{20,4},{24,16},{28,12},{1,9},{5... | collective-permute-start | bytes 5308424 | tf_op jit(solution)/shard_map/ppermute | solution.py:606
  526.4 46.6 %collective-permute-start.51 = (bf16[384,1152]{1,0:T(8,128)(2,1)}, bf16[384,1152]{1,0:T(8,128)(2,1)}, u32[]{:S(2)}, u32[]{:S(2)}) collective-permute-start(bf16[384,1152]{1,0:T(8,128)(2,1)} %collective-permute-done.49), channel_id=1, source_target_pairs={{0,16},{4,12},{8,24},{12,4},{16,0},{20,28},{24,8},{28,20},{1,17},{... | collective-permute-start | bytes 2654216 | tf_op jit(solution)/shard_map/ppermute | solution.py:609
  589.4 92.4 %all-to-all-start.3 = ((bf16[8,128,1536]{2,1,0:T(8,128)(2,1)}), bf16[8,128,1536]{2,1,0:T(8,128)(2,1)}, u32[]{:S(2)}, u32[]{:S(2)}) async-start(bf16[8,128,1536]{2,1,0:T(8,128)(2,1)} %bitcast.202), calls=%async_computation.5 | async-start | bytes 6291456 | tf_op jit(solution)/shard_map/all_to_all | solution.py:652
  593.9 102.5 %reduce-scatter.10.cloned.1.call-start = ((), (), s32[]{:S(2)}) async-start(), calls=%async_computation.11 | async-start | bytes 2211840 | tf_op jit(solution)/shard_map/reduce_scatter | solution.py:622
  604.8 115.5 %reduce-scatter.12.cloned.1.call-start = ((), (), s32[]{:S(2)}) async-start(), calls=%async_computation.12 | async-start | bytes 737280 | tf_op jit(solution)/shard_map/reduce_scatter | solution.py:622
  615.2 66.6 %collective-permute-start.62 = (bf16[256,1920]{1,0:T(8,128)(2,1)}, bf16[256,1920]{1,0:T(8,128)(2,1)}, u32[]{:S(2)}, u32[]{:S(2)}) collective-permute-start(bf16[256,1920]{1,0:T(8,128)(2,1)} %add_convert_fusion.8), channel_id=1, source_target_pairs={{0,16},{4,12},{8,24},{12,4},{16,0},{20,28},{24,8},{28,20},{1,17},{... | collective-permute-start | bytes 2949128 | tf_op jit(solution)/shard_map/ppermute | solution.py:609
  617.3 64.5 %collective-permute-start.63 = (bf16[256,1920]{1,0:T(8,128)(2,1)}, bf16[256,1920]{1,0:T(8,128)(2,1)}, u32[]{:S(2)}, u32[]{:S(2)}) collective-permute-start(bf16[256,1920]{1,0:T(8,128)(2,1)} %add_convert_fusion.7), channel_id=1, source_target_pairs={{0,16},{4,12},{8,24},{12,4},{16,0},{20,28},{24,8},{28,20},{1,17},{... | collective-permute-start | bytes 2949128 | tf_op jit(solution)/shard_map/ppermute | solution.py:609
  619.0 62.9 %collective-permute-start.66 = (bf16[384,1152]{1,0:T(8,128)(2,1)S(1)}, bf16[384,1152]{1,0:T(8,128)(2,1)S(1)}, u32[]{:S(2)}, u32[]{:S(2)}) collective-permute-start(bf16[384,1152]{1,0:T(8,128)(2,1)S(1)} %add_convert_fusion.9.refs_0_), channel_id=1, source_target_pairs={{0,16},{4,12},{8,24},{12,4},{16,0},{20,28},{24,8},{28,20},{1,17},{... | collective-permute-start | bytes 2654216 | tf_op jit(solution)/shard_map/ppermute | solution.py:609
  689.7 49.0 %reduce-scatter.14.cloned.1.call-start = ((), (), s32[]{:S(2)}) async-start(), calls=%async_computation.13 | async-start | bytes 1228800 | tf_op jit(solution)/shard_map/reduce_scatter | solution.py:622
  (175 other events, 2382.2 us)
Sparse Core Ops, SparseCore 0:
  34.3 53.3 all-gather.6
  89.8 68.7 all-gather.8
  160.8 38.9 all-gather.10
  399.6 66.8 reduce-scatter.5
  468.7 66.6 reduce-scatter.7
  604.9 39.1 reduce-scatter.9
  689.8 21.3 reduce-scatter.11
  714.2 24.4 reduce-scatter.13

commit v6 on v5

--- a/solution.py
+++ b/solution.py
@@ -1086,21 +1086,21 @@
         plane.second(mine_gate_up),
         plane.swap(mine_gate_up),
     )
-    early_from_d, early_from_v, out_from_u, gate_up_u, gate_up_v, gate_up_0, home_grad = fence(
-        early_from_d, early_from_v, out_from_u, gate_up_u, gate_up_v, gate_up_0, home_grad
-    )
-
-    early_from_u = plane.first(added(early_terms[1], early_swaps[2], early_from_d))
     total = added(out_terms[0], out_swaps[0], out_from_v, out_from_u)
     mine_out = plane.down_columns(total)
+    early_from_d, early_from_v, total, gate_up_u, gate_up_v, gate_up_0, home_grad = fence(
+        early_from_d, early_from_v, total, gate_up_u, gate_up_v, gate_up_0, home_grad
+    )
+
+    early_from_u = plane.first(added(early_terms[1], early_swaps[2], early_from_d))
     gate_up_d, gate_up_2, gate_up_1 = (
         plane.second(gate_up_u),
         plane.swap(gate_up_u),
         plane.swap(gate_up_v),
     )
     grad_arrived = home_grad.reshape(-1, model_width)[send_slot]
-    early_from_u, gate_up_d, gate_up_2, gate_up_1, mine_down, total, grad_arrived = fence(
-        early_from_u, gate_up_d, gate_up_2, gate_up_1, mine_down, total, grad_arrived
+    early_from_u, gate_up_d, gate_up_2, gate_up_1, mine_down, mine_out, grad_arrived = fence(
+        early_from_u, gate_up_d, gate_up_2, gate_up_1, mine_down, mine_out, grad_arrived
     )
 
     total = added(early_terms[0], early_swaps[0], early_from_v, early_from_u)
@@ -1114,15 +1114,15 @@
         (shard_rows, 2 * FF),
         lambda p: (0, (p % 2) * 4 + p // 2),
     )
-    down_own, total_gate_up, mine_out = fence(down_own, total_gate_up, mine_out)
+    out_own = [mine_out, plane.first(mine_out), plane.second(mine_out)]
+    down_own, out_own, total_gate_up = fence(down_own, out_own, total_gate_up)
 
     down_own.append(plane.second(down_own[1]))
     down_swaps = [plane.swap(piece) for piece in down_own[:3]]
-    out_own = [mine_out, plane.first(mine_out), plane.second(mine_out)]
+    out_own.append(plane.second(out_own[1]))
     down_own, down_swaps, out_own, mine_early = fence(down_own, down_swaps, out_own, mine_early)
 
     down_swaps.append(plane.swap(down_own[3]))
-    out_own.append(plane.second(out_own[1]))
     piece = mine_early[:part_rows]
     early_own = [piece, plane.first(piece), plane.second(piece)]
     total_down = spread(
@@ -1131,7 +1131,7 @@
         (2 * half_rows, model_width),
         lambda p: (p % 2, p // 2),
     )
-    early_own, out_own, total_down = fence(early_own, out_own, total_down)
+    early_own, total_down = fence(early_own, total_down)
     early_own.append(plane.second(early_own[1]))
     total_out = spread(
         out_own + second_halves(out_own),

time: 782 us -> 796 us (1.018)
  waiting for transfers between devices: 218 us -> 238 us
    ppermute x23, waiting for transfers between devices: 52.3 us -> 68.4 us  [second(): return lax.ppermute(x, 'seq', self.second_pairs)]
    unnamed x188 -> x186, local copies, waits for them, and re-layouts: 28.6 us -> 28 us
  transfers between devices with their start and end apart: 106 -> 106, of which waited for: 30 -> 27; matrix products, arithmetic and copies ran while one was open for 23% -> 21% of each run, Pallas kernels for 28% -> 28%
where the time goes in v6:
time: 796 us; the launch traced here: 785 us
  waiting for transfers between devices  238 us (30%)
  Pallas kernels  221 us (28%)
  local copies, waits for them, and re-layouts  107 us (13%)
  starting transfers between devices  93.7 us (12%)
  other arithmetic  81.6 us (10%)
  matrix products  28.4 us (4%)
  between operations  16.2 us (2%)
    ppermute x13, waiting for transfers between devices, first(): return lax.ppermute(x, 'seq', self.first_pairs)  121 us
    pallas_call x4, Pallas kernels, feed(): pl.pallas_call(kernel, in_specs=[pl.BlockSpec(memory_space=pltpu.SMEM), i...  115 us
    ppermute x23, waiting for transfers between devices, second(): return lax.ppermute(x, 'seq', self.second_pairs)  68.4 us
    convert_element_type x19, other arithmetic, rounded(): return x.astype(jnp.bfloat16)  53 us
    unnamed x186, local copies, waits for them, and re-layouts  28 us
    pallas_call x1, Pallas kernels, attend_back(): pl.pallas_call(kernel, grid=(rows // block, couples), in_specs=[tile, til...  25.6 us
    ppermute x23, starting transfers between devices, second(): return lax.ppermute(x, 'seq', self.second_pairs)  24.6 us
    pallas_call x1, Pallas kernels, attend(): pl.pallas_call(kernel, grid=(rows // block, couples), in_specs=[tile, tab...  20.9 us
  transfers between devices with their start and end apart: 106, of which 27 were waited for; matrix products, arithmetic and copies ran while one was open for 21% of the time, Pallas kernels for 28%

profile of v6, /device:TPU:0, one launch (start us, length us, event | category | flops | bytes accessed | tf_op | source)
XLA Modules:
  0.0 785.2 jit_solution(14238312982800792826)
XLA Ops:
  69.1 12.7 %collective-permute-done.7 = bf16[48,1536]{1,0:T(8,128)(2,1)} collective-permute-done((bf16[48,1536]{1,0:T(8,128)(2,1)}, bf16[48,1536]{1,0:T(8,128)(2,1)}, u32[]{:S(2)}, u32[]{:S(2)}) %collective-permute-start.7) | collective-permute-done | bytes 147488 | tf_op jit(solution)/shard_map/ppermute | solution.py:614
  81.7 8.5 %collective-permute-done.3.refs_1_ = bf16[3,48,1920]{2,1,0:T(8,128)(2,1)S(1)} collective-permute-done((bf16[3,48,1920]{2,1,0:T(8,128)(2,1)S(1)}, bf16[3,48,1920]{2,1,0:T(8,128)(2,1)S(1)}, u32[]{:S(2)}, u32[]{:S(2)}) %collective-permute-start.3) | collective-permute-done | bytes 552992 | tf_op jit(solution)/shard_map/ppermute | solution.py:606
  97.1 8.0 %scatter_custom_fusion.2 = bf16[512,1664]{1,0:T(8,128)(2,1)} fusion(s32[1024]{0:T(1024)S(1)} %get-tuple-element.492, bf16[1024,1664]{1,0:T(8,128)(2,1)} %bitcast.21, bf16[]{:T(256)} %constant.192.clone.1), kind=kCustom, calls=%fused_computation.72 | custom fusion | bytes 1704448 | tf_op jit(solution)/shard_map/scatter | solution.py:644
  138.9 19.7 %all-gather.9.cloned.1.call-done = bf16[1536,1152]{1,0:T(8,128)(2,1)} async-done(((bf16[384,1152]{1,0:T(8,128)(2,1)}), bf16[1536,1152]{1,0:T(8,128)(2,1)}) %all-gather.9.cloned.1.call-update) | async-done | bytes 3538960 | tf_op jit(solution)/shard_map/all_gather | solution.py:864
  168.8 13.8 %collective-permute-done.19.refs_6_ = bf16[3,576,384]{2,1,0:T(8,128)(2,1)} collective-permute-done((bf16[3,576,384]{2,1,0:T(8,128)(2,1)}, bf16[3,576,384]{2,1,0:T(8,128)(2,1)}, u32[]{:S(2)}, u32[]{:S(2)}) %collective-permute-start.19) | collective-permute-done | bytes 1327136 | tf_op jit(solution)/shard_map/ppermute | solution.py:606
  193.4 7.5 scatter_custom_fusion.3.g_ref
  209.8 20.9 %shard_map.183 = (bf16[512,1536]{1,0:T(8,128)(2,1)}, bf16[512,1536]{1,0:T(8,128)(2,1)}, f32[4,2,512]{2,1,0:T(2,128)S(1)}) custom-call(f32[512,1536]{1,0:T(8,128)} %fusion.78.q_ref, f32[512,384]{1,0:T(8,128)S(1)} %copy-done.15, f32[512,384]{1,0:T(8,128)S(1)} %copy-done.17, f32[512,384]{1,0:T(8,128)S(1)} %copy-done.19, bf16[1536,384]{1,0:T(8,128)(2,1)S(1)} %copy.124.pairs_ref, ...), custom_call_target="tpu_custom_call" | custom-call | flops 100000000 | bytes 100000 | tf_op jit(solution)/shard_map/pallas_call | solution.py:189
  242.6 28.4 %shard_map.185 = (f32[512,1536]{1,0:T(8,128)}, f32[512,1536]{1,0:T(8,128)}, bf16[1536,1152]{1,0:T(8,128)(2,1)}, bf16[1536,1152]{1,0:T(8,128)(2,1)}, bf16[4,576,3...) custom-call(s32[8]{0:T(128)} %stack.133.facts_ref, ...), custom_call_target="tpu_custom_call" | custom-call | flops 100000000 | bytes 100000 | tf_op jit(solution)/shard_map/pallas_call | solution.py:559
  282.6 28.8 %shard_map.186 = (f32[512,1536]{1,0:T(8,128)}, f32[512,1536]{1,0:T(8,128)}, bf16[1536,1152]{1,0:T(8,128)(2,1)}, bf16[1536,1152]{1,0:T(8,128)(2,1)}, bf16[4,576,3...) custom-call(s32[8]{0:T(128)} %stack.134.facts_ref, ...), custom_call_target="tpu_custom_call", output_to_operand_aliasing={{0}: (7, {}), {1}: (16, {}), {4}: (17, {}), {5}: (18, {}), ... | custom-call | flops 100000000 | bytes 100000 | tf_op jit(solution)/shard_map/pallas_call | solution.py:559
  313.7 28.6 %shard_map.187 = (f32[512,1536]{1,0:T(8,128)}, f32[512,1536]{1,0:T(8,128)}, bf16[1536,1152]{1,0:T(8,128)(2,1)}, bf16[1536,1152]{1,0:T(8,128)(2,1)}, bf16[4,576,3...) custom-call(s32[8]{0:T(128)} %stack.135.facts_ref, ...), custom_call_target="tpu_custom_call", output_to_operand_aliasing={{0}: (7, {}), {1}: (16, {}), {4}: (17, {}), {5}: (18, {}), ... | custom-call | flops 100000000 | bytes 100000 | tf_op jit(solution)/shard_map/pallas_call | solution.py:559
  350.4 29.0 %shard_map.188 = (f32[512,1536]{1,0:T(8,128)}, f32[512,1536]{1,0:T(8,128)}, bf16[1536,1152]{1,0:T(8,128)(2,1)}, bf16[1536,1152]{1,0:T(8,128)(2,1)}, bf16[4,576,3...) custom-call(s32[8]{0:T(128)} %stack.136.facts_ref, ...), custom_call_target="tpu_custom_call", output_to_operand_aliasing={{0}: (7, {}), {1}: (16, {}), {4}: (17, {}), {5}: (18, {}), ... | custom-call | flops 100000000 | bytes 100000 | tf_op jit(solution)/shard_map/pallas_call | solution.py:559
  420.6 20.7 %collective-permute-done.39 = bf16[1536,1152]{1,0:T(8,128)(2,1)} collective-permute-done((bf16[1536,1152]{1,0:T(8,128)(2,1)}, bf16[1536,1152]{1,0:T(8,128)(2,1)}, u32[]{:S(2)}, u32[]{:S(2)}) %collective-permute-start.39) | collective-permute-done | bytes 3538976 | tf_op jit(solution)/shard_map/ppermute | solution.py:606
  443.4 7.7 add_convert_fusion
  456.0 25.6 %shard_map.194 = (bf16[512,1536]{1,0:T(8,128)(2,1)}, f32[1536,384]{1,0:T(8,128)}) custom-call(bf16[512,1536]{1,0:T(8,128)(2,1)} %get-tuple-element.394.q_ref, bf16[512,1536]{1,0:T(8,128)(2,1)} %convolution_convert_fusion.2.do_ref, f32[4,2,512]{2,1,0:T(2,128)S(1)} %get-tuple-element.401.total_ref, f32[512,384]{1,0:T(8,128)S(1)} %copy-done.16, ...), custom_call_target="tpu_custom_call" | custom-call | flops 100000000 | bytes 100000 | tf_op jit(solution)/shard_map/pallas_call | solution.py:261
  503.0 8.7 %collective-permute-done.49 = bf16[384,1152]{1,0:T(8,128)(2,1)} collective-permute-done((bf16[384,1152]{1,0:T(8,128)(2,1)}, bf16[384,1152]{1,0:T(8,128)(2,1)}, u32[]{:S(2)}, u32[]{:S(2)}) %collective-permute-start.49) | collective-permute-done | bytes 884768 | tf_op jit(solution)/shard_map/ppermute | solution.py:606
  556.2 16.6 %collective-permute-done.51 = bf16[384,1152]{1,0:T(8,128)(2,1)} collective-permute-done((bf16[384,1152]{1,0:T(8,128)(2,1)}, bf16[384,1152]{1,0:T(8,128)(2,1)}, u32[]{:S(2)}, u32[]{:S(2)}) %collective-permute-start.51) | collective-permute-done | bytes 884768 | tf_op jit(solution)/shard_map/ppermute | solution.py:609
  572.8 9.6 %collective-permute-done.50 = bf16[2304,384]{1,0:T(8,128)(2,1)} collective-permute-done((bf16[2304,384]{1,0:T(8,128)(2,1)}, bf16[2304,384]{1,0:T(8,128)(2,1)}, u32[]{:S(2)}, u32[]{:S(2)}) %collective-permute-start.50) | collective-permute-done | bytes 1769504 | tf_op jit(solution)/shard_map/ppermute | solution.py:606
  589.2 6.9 gather_fusion.3
  603.4 9.7 %collective-permute-done.64 = bf16[192,1536]{1,0:T(8,128)(2,1)S(1)} collective-permute-done((bf16[192,1536]{1,0:T(8,128)(2,1)S(1)}, bf16[192,1536]{1,0:T(8,128)(2,1)S(1)}, u32[]{:S(2)}, u32[]{:S(2)}) %collective-permute-start.64) | collective-permute-done | bytes 589856 | tf_op jit(solution)/shard_map/ppermute | solution.py:606
  631.0 45.4 %collective-permute-done.65.refs_1_ = bf16[384,1152]{1,0:T(8,128)(2,1)S(1)} collective-permute-done((bf16[384,1152]{1,0:T(8,128)(2,1)S(1)}, bf16[384,1152]{1,0:T(8,128)(2,1)S(1)}, u32[]{:S(2)}, u32[]{:S(2)}) %collective-permute-start.65) | collective-permute-done | bytes 884768 | tf_op jit(solution)/shard_map/ppermute | solution.py:606
  676.4 20.5 %collective-permute-done.66.refs_2_ = bf16[384,1152]{1,0:T(8,128)(2,1)S(1)} collective-permute-done((bf16[384,1152]{1,0:T(8,128)(2,1)S(1)}, bf16[384,1152]{1,0:T(8,128)(2,1)S(1)}, u32[]{:S(2)}, u32[]{:S(2)}) %collective-permute-start.66) | collective-permute-done | bytes 884768 | tf_op jit(solution)/shard_map/ppermute | solution.py:609
  709.1 14.0 %collective-permute-done.69.refs_3_ = bf16[384,1152]{1,0:T(8,128)(2,1)} collective-permute-done((bf16[384,1152]{1,0:T(8,128)(2,1)S(1)}, bf16[384,1152]{1,0:T(8,128)(2,1)}, u32[]{:S(2)}, u32[]{:S(2)}) %collective-permute-start.69) | collective-permute-done | bytes 884768 | tf_op jit(solution)/shard_map/ppermute | solution.py:609
  731.7 8.5 %shard_map.195 = f32[384,9216]{1,0:T(8,128)} custom-call(s32[8]{0:T(128)S(1)} %stack.137.positions_ref, bf16[384,1152]{1,0:T(8,128)(2,1)S(1)} %add_convert_fusion.9.refs_0_, bf16[384,1152]{1,0:T(8,128)(2,1)S(1)} %collective-permute-done.65.refs_1_, bf16[384,1152]{1,0:T(8,128)(2,1)S(1)} %collective-permute-done.66.refs_2_, ...), custom_call_target="tpu_custom_call" | custom-call | tf_op jit(solution)/shard_map/pallas_call | solution.py:374
  746.4 7.5 collective-permute-done.81.refs_3_
  (537 shorter events, 361.4 us)
Async XLA Ops:
  7.2 110.1 %all-gather.7.cloned.1.call-start = ((), (), s32[]{:S(2)}) async-start(), calls=%async_computation.14 | async-start | bytes 2211840 | tf_op jit(solution)/shard_map/all_gather | solution.py:858
  34.2 56.1 %all-to-all-start = ((bf16[8,128,1664]{2,1,0:T(8,128)(2,1)}), bf16[8,128,1664]{2,1,0:T(8,128)(2,1)}, u32[]{:S(2)}, u32[]{:S(2)}) async-start(bf16[8,128,1664]{2,1,0:T(8,128)(2,1)} %bitcast.199), calls=%async_computation | async-start | bytes 6815744 | tf_op jit(solution)/shard_map/all_to_all | solution.py:652
  38.7 120.0 %all-gather.9.cloned.1.call-start = ((), (), s32[]{:S(2)}) async-start(), calls=%async_computation.15 | async-start | bytes 4423680 | tf_op jit(solution)/shard_map/all_gather | solution.py:864
  43.7 46.5 %collective-permute-start.3 = (bf16[3,48,1920]{2,1,0:T(8,128)(2,1)S(1)}, bf16[3,48,1920]{2,1,0:T(8,128)(2,1)S(1)}, u32[]{:S(2)}, u32[]{:S(2)}) collective-permute-start(bf16[3,48,1920]{2,1,0:T(8,128)(2,1)S(1)} %slice.123.refs_0_), channel_id=1, source_target_pairs={{0,8},{4,20},{8,0},{12,28},{16,24},{20,4},{24,16},{28,12},{1,9},{5... | collective-permute-start | bytes 1658888 | tf_op jit(solution)/shard_map/ppermute | solution.py:606
  112.6 80.8 %all-to-all-start.1 = ((bf16[8,128,1536]{2,1,0:T(8,128)(2,1)}), bf16[8,128,1536]{2,1,0:T(8,128)(2,1)}, u32[]{:S(2)}, u32[]{:S(2)}) async-start(bf16[8,128,1536]{2,1,0:T(8,128)(2,1)} %bitcast.200), calls=%async_computation.1 | async-start | bytes 6291456 | tf_op jit(solution)/shard_map/all_to_all | solution.py:652
  117.1 113.6 %all-gather.11.cloned.1.call-start = ((), (), s32[]{:S(2)}) async-start(), calls=%async_computation.16 | async-start | bytes 2211840 | tf_op jit(solution)/shard_map/all_gather | solution.py:858
  120.7 61.9 %collective-permute-start.19 = (bf16[3,576,384]{2,1,0:T(8,128)(2,1)}, bf16[3,576,384]{2,1,0:T(8,128)(2,1)}, u32[]{:S(2)}, u32[]{:S(2)}) collective-permute-start(bf16[3,576,384]{2,1,0:T(8,128)(2,1)} %shard_map.179.refs_5_), channel_id=1, source_target_pairs={{0,8},{4,20},{8,0},{12,28},{16,24},{20,4},{24,16},{28,12},{1,9},{5... | collective-permute-start | bytes 3981320 | tf_op jit(solution)/shard_map/ppermute | solution.py:606
  122.5 60.0 %collective-permute-start.20 = (bf16[3,576,384]{2,1,0:T(8,128)(2,1)}, bf16[3,576,384]{2,1,0:T(8,128)(2,1)}, u32[]{:S(2)}, u32[]{:S(2)}) collective-permute-start(bf16[3,576,384]{2,1,0:T(8,128)(2,1)} %shard_map.179.refs_5_), channel_id=1, source_target_pairs={{0,16},{4,12},{8,24},{12,4},{16,0},{20,28},{24,8},{28,20},{1,17},{... | collective-permute-start | bytes 3981320 | tf_op jit(solution)/shard_map/ppermute | solution.py:609
  124.0 58.5 %collective-permute-start.21 = (bf16[3,576,384]{2,1,0:T(8,128)(2,1)}, bf16[3,576,384]{2,1,0:T(8,128)(2,1)}, u32[]{:S(2)}, u32[]{:S(2)}) collective-permute-start(bf16[3,576,384]{2,1,0:T(8,128)(2,1)} %shard_map.179.refs_5_), channel_id=1, source_target_pairs={{0,4},{4,0},{8,12},{12,8},{16,20},{20,16},{24,28},{28,24},{1,5},{5... | collective-permute-start | bytes 3981320 | tf_op jit(solution)/shard_map/ppermute | solution.py:619
  160.5 322.6 %reduce-scatter.6.cloned.1.call-start = ((), (), s32[]{:S(2)}) async-start(), calls=%async_computation.9 | async-start | bytes 4423680 | tf_op jit(solution)/shard_map/reduce_scatter | solution.py:622
  203.2 67.8 %collective-permute-start.27 = (bf16[1152,1152]{1,0:T(8,128)(2,1)}, bf16[1152,1152]{1,0:T(8,128)(2,1)}, u32[]{:S(2)}, u32[]{:S(2)}) collective-permute-start(bf16[1152,1152]{1,0:T(8,128)(2,1)} %bitcast.204), channel_id=1, source_target_pairs={{0,8},{4,20},{8,0},{12,28},{16,24},{20,4},{24,16},{28,12},{1,9},{5... | collective-permute-start | bytes 7962632 | tf_op jit(solution)/shard_map/ppermute | solution.py:606
  203.8 67.2 %collective-permute-start.28 = (bf16[1152,1152]{1,0:T(8,128)(2,1)}, bf16[1152,1152]{1,0:T(8,128)(2,1)}, u32[]{:S(2)}, u32[]{:S(2)}) collective-permute-start(bf16[1152,1152]{1,0:T(8,128)(2,1)} %bitcast.205), channel_id=1, source_target_pairs={{0,16},{4,12},{8,24},{12,4},{16,0},{20,28},{24,8},{28,20},{1,17},{... | collective-permute-start | bytes 7962632 | tf_op jit(solution)/shard_map/ppermute | solution.py:609
  399.4 200.9 %reduce-scatter.8.cloned.1.call-start = ((), (), s32[]{:S(2)}) async-start(), calls=%async_computation.10 | async-start | bytes 4423680 | tf_op jit(solution)/shard_map/reduce_scatter | solution.py:622
  511.8 70.6 %all-to-all-start.2 = ((bf16[8,128,1536]{2,1,0:T(8,128)(2,1)}), bf16[8,128,1536]{2,1,0:T(8,128)(2,1)}, u32[]{:S(2)}, u32[]{:S(2)}) async-start(bf16[8,128,1536]{2,1,0:T(8,128)(2,1)} %bitcast.201), calls=%async_computation.3 | async-start | bytes 6291456 | tf_op jit(solution)/shard_map/all_to_all | solution.py:652
  516.5 192.6 %reduce-scatter.12.cloned.1.call-start = ((), (), s32[]{:S(2)}) async-start(), calls=%async_computation.12 | async-start | bytes 737280 | tf_op jit(solution)/shard_map/reduce_scatter | solution.py:622
  524.1 58.4 %collective-permute-start.50 = (bf16[2304,384]{1,0:T(8,128)(2,1)}, bf16[2304,384]{1,0:T(8,128)(2,1)}, u32[]{:S(2)}, u32[]{:S(2)}) collective-permute-start(bf16[2304,384]{1,0:T(8,128)(2,1)} %add_convert_fusion.4), channel_id=1, source_target_pairs={{0,8},{4,20},{8,0},{12,28},{16,24},{20,4},{24,16},{28,12},{1,9},{5... | collective-permute-start | bytes 5308424 | tf_op jit(solution)/shard_map/ppermute | solution.py:606
  615.5 81.5 %all-to-all-start.3 = ((bf16[8,128,1536]{2,1,0:T(8,128)(2,1)}), bf16[8,128,1536]{2,1,0:T(8,128)(2,1)}, u32[]{:S(2)}, u32[]{:S(2)}) async-start(bf16[8,128,1536]{2,1,0:T(8,128)(2,1)} %bitcast.202), calls=%async_computation.5 | async-start | bytes 6291456 | tf_op jit(solution)/shard_map/all_to_all | solution.py:652
  620.1 89.0 %reduce-scatter.10.cloned.1.call-start = ((), (), s32[]{:S(2)}) async-start(), calls=%async_computation.11 | async-start | bytes 2211840 | tf_op jit(solution)/shard_map/reduce_scatter | solution.py:622
  624.1 129.9 %reduce-scatter.14.cloned.1.call-start = ((), (), s32[]{:S(2)}) async-start(), calls=%async_computation.13 | async-start | bytes 1228800 | tf_op jit(solution)/shard_map/reduce_scatter | solution.py:622
  624.1 72.8 %collective-permute-start.62 = (bf16[256,1920]{1,0:T(8,128)(2,1)}, bf16[256,1920]{1,0:T(8,128)(2,1)}, u32[]{:S(2)}, u32[]{:S(2)}) collective-permute-start(bf16[256,1920]{1,0:T(8,128)(2,1)} %add_convert_fusion.8), channel_id=1, source_target_pairs={{0,16},{4,12},{8,24},{12,4},{16,0},{20,28},{24,8},{28,20},{1,17},{... | collective-permute-start | bytes 2949128 | tf_op jit(solution)/shard_map/ppermute | solution.py:609
  626.0 70.9 %collective-permute-start.63 = (bf16[256,1920]{1,0:T(8,128)(2,1)}, bf16[256,1920]{1,0:T(8,128)(2,1)}, u32[]{:S(2)}, u32[]{:S(2)}) collective-permute-start(bf16[256,1920]{1,0:T(8,128)(2,1)} %add_convert_fusion.7), channel_id=1, source_target_pairs={{0,16},{4,12},{8,24},{12,4},{16,0},{20,28},{24,8},{28,20},{1,17},{... | collective-permute-start | bytes 2949128 | tf_op jit(solution)/shard_map/ppermute | solution.py:609
  627.6 48.8 %collective-permute-start.65 = (bf16[384,1152]{1,0:T(8,128)(2,1)S(1)}, bf16[384,1152]{1,0:T(8,128)(2,1)S(1)}, u32[]{:S(2)}, u32[]{:S(2)}) collective-permute-start(bf16[384,1152]{1,0:T(8,128)(2,1)S(1)} %add_convert_fusion.9.refs_0_), channel_id=1, source_target_pairs={{0,8},{4,20},{8,0},{12,28},{16,24},{20,4},{24,16},{28,12},{1,9},{5... | collective-permute-start | bytes 2654216 | tf_op jit(solution)/shard_map/ppermute | solution.py:606
  629.5 67.4 %collective-permute-start.66 = (bf16[384,1152]{1,0:T(8,128)(2,1)S(1)}, bf16[384,1152]{1,0:T(8,128)(2,1)S(1)}, u32[]{:S(2)}, u32[]{:S(2)}) collective-permute-start(bf16[384,1152]{1,0:T(8,128)(2,1)S(1)} %add_convert_fusion.9.refs_0_), channel_id=1, source_target_pairs={{0,16},{4,12},{8,24},{12,4},{16,0},{20,28},{24,8},{28,20},{1,17},{... | collective-permute-start | bytes 2654216 | tf_op jit(solution)/shard_map/ppermute | solution.py:609
  631.0 66.0 %collective-permute-start.67 = (bf16[384,1152]{1,0:T(8,128)(2,1)S(1)}, bf16[384,1152]{1,0:T(8,128)(2,1)S(1)}, u32[]{:S(2)}, u32[]{:S(2)}) collective-permute-start(bf16[384,1152]{1,0:T(8,128)(2,1)S(1)} %add_convert_fusion.9.refs_0_), channel_id=1, source_target_pairs={{0,4},{4,0},{8,12},{12,8},{16,20},{20,16},{24,28},{28,24},{1,5},{5... | collective-permute-start | bytes 2654216 | tf_op jit(solution)/shard_map/ppermute | solution.py:619
  (174 other events, 2377.1 us)
Sparse Core Ops, SparseCore 0:
  34.3 53.3 all-gather.6
  89.8 68.7 all-gather.8
  160.8 38.8 all-gather.10
  399.5 66.9 reduce-scatter.5
  468.7 66.6 reduce-scatter.7
  615.6 20.8 reduce-scatter.11
  639.4 36.7 reduce-scatter.9
  727.6 24.7 reduce-scatter.13

commit v7 on v6

--- a/solution.py
+++ b/solution.py
@@ -1099,8 +1099,8 @@
         plane.swap(gate_up_v),
     )
     grad_arrived = home_grad.reshape(-1, model_width)[send_slot]
-    early_from_u, gate_up_d, gate_up_2, gate_up_1, mine_down, mine_out, grad_arrived = fence(
-        early_from_u, gate_up_d, gate_up_2, gate_up_1, mine_down, mine_out, grad_arrived
+    early_from_u, gate_up_d, gate_up_2, gate_up_1, mine_down, grad_arrived = fence(
+        early_from_u, gate_up_d, gate_up_2, gate_up_1, mine_down, grad_arrived
     )
 
     total = added(early_terms[0], early_swaps[0], early_from_v, early_from_u)
@@ -1114,15 +1114,15 @@
         (shard_rows, 2 * FF),
         lambda p: (0, (p % 2) * 4 + p // 2),
     )
-    out_own = [mine_out, plane.first(mine_out), plane.second(mine_out)]
-    down_own, out_own, total_gate_up = fence(down_own, out_own, total_gate_up)
+    down_own, total_gate_up, mine_out = fence(down_own, total_gate_up, mine_out)
 
     down_own.append(plane.second(down_own[1]))
     down_swaps = [plane.swap(piece) for piece in down_own[:3]]
+    out_own = [mine_out, plane.first(mine_out), plane.second(mine_out)]
+    down_own, down_swaps, out_own, mine_early = fence(down_own, down_swaps, out_own, mine_early)
+
+    down_swaps.append(plane.swap(down_own[3]))
     out_own.append(plane.second(out_own[1]))
-    down_own, down_swaps, out_own, mine_early = fence(down_own, down_swaps, out_own, mine_early)
-
-    down_swaps.append(plane.swap(down_own[3]))
     piece = mine_early[:part_rows]
     early_own = [piece, plane.first(piece), plane.second(piece)]
     total_down = spread(
@@ -1131,7 +1131,7 @@
         (2 * half_rows, model_width),
         lambda p: (p % 2, p // 2),
     )
-    early_own, total_down = fence(early_own, total_down)
+    early_own, out_own, total_down = fence(early_own, out_own, total_down)
     early_own.append(plane.second(early_own[1]))
     total_out = spread(
         out_own + second_halves(out_own),

time: 796 us -> 781 us (0.981)
  waiting for transfers between devices: 238 us -> 221 us
    ppermute x13, waiting for transfers between devices: 121 us -> 110 us  [first(): return lax.ppermute(x, 'seq', self.first_pairs)]
    unnamed x186 -> x184, local copies, waits for them, and re-layouts: 28 us -> 28 us
  transfers between devices with their start and end apart: 106 -> 106, of which waited for: 27 -> 29; matrix products, arithmetic and copies ran while one was open for 21% -> 23% of each run, Pallas kernels for 28% -> 28%
where the time goes in v7:
time: 781 us; the launch traced here: 770 us
  waiting for transfers between devices  221 us (28%)
  Pallas kernels  220 us (28%)
  local copies, waits for them, and re-layouts  107 us (14%)
  starting transfers between devices  94.3 us (12%)
  other arithmetic  83.7 us (11%)
  matrix products  28.3 us (4%)
  between operations  16.2 us (2%)
    pallas_call x4, Pallas kernels, feed(): pl.pallas_call(kernel, in_specs=[pl.BlockSpec(memory_space=pltpu.SMEM), i...  115 us
    ppermute x13, waiting for transfers between devices, first(): return lax.ppermute(x, 'seq', self.first_pairs)  110 us
    ppermute x23, waiting for transfers between devices, second(): return lax.ppermute(x, 'seq', self.second_pairs)  61.4 us
    convert_element_type x19, other arithmetic, rounded(): return x.astype(jnp.bfloat16)  54.1 us
    unnamed x184, local copies, waits for them, and re-layouts  28 us
    pallas_call x1, Pallas kernels, attend_back(): pl.pallas_call(kernel, grid=(rows // block, couples), in_specs=[tile, til...  25.9 us
    ppermute x23, starting transfers between devices, second(): return lax.ppermute(x, 'seq', self.second_pairs)  24.2 us
    pallas_call x1, Pallas kernels, attend(): pl.pallas_call(kernel, grid=(rows // block, couples), in_specs=[tile, tab...  20.9 us
  transfers between devices with their start and end apart: 106, of which 29 were waited for; matrix products, arithmetic and copies ran while one was open for 23% of the time, Pallas kernels for 28%

profile of v7, /device:TPU:0, one launch (start us, length us, event | category | flops | bytes accessed | tf_op | source)
XLA Modules:
  0.0 770.0 jit_solution(6703270146595525086)
XLA Ops:
  69.1 12.7 %collective-permute-done.7 = bf16[48,1536]{1,0:T(8,128)(2,1)} collective-permute-done((bf16[48,1536]{1,0:T(8,128)(2,1)}, bf16[48,1536]{1,0:T(8,128)(2,1)}, u32[]{:S(2)}, u32[]{:S(2)}) %collective-permute-start.7) | collective-permute-done | bytes 147488 | tf_op jit(solution)/shard_map/ppermute | solution.py:614
  81.7 8.5 %collective-permute-done.3.refs_1_ = bf16[3,48,1920]{2,1,0:T(8,128)(2,1)S(1)} collective-permute-done((bf16[3,48,1920]{2,1,0:T(8,128)(2,1)S(1)}, bf16[3,48,1920]{2,1,0:T(8,128)(2,1)S(1)}, u32[]{:S(2)}, u32[]{:S(2)}) %collective-permute-start.3) | collective-permute-done | bytes 552992 | tf_op jit(solution)/shard_map/ppermute | solution.py:606
  97.1 8.0 %scatter_custom_fusion.2 = bf16[512,1664]{1,0:T(8,128)(2,1)} fusion(s32[1024]{0:T(1024)S(1)} %get-tuple-element.492, bf16[1024,1664]{1,0:T(8,128)(2,1)} %bitcast.21, bf16[]{:T(256)} %constant.192.clone.1), kind=kCustom, calls=%fused_computation.72 | custom fusion | bytes 1704448 | tf_op jit(solution)/shard_map/scatter | solution.py:644
  138.9 19.7 %all-gather.9.cloned.1.call-done = bf16[1536,1152]{1,0:T(8,128)(2,1)} async-done(((bf16[384,1152]{1,0:T(8,128)(2,1)}), bf16[1536,1152]{1,0:T(8,128)(2,1)}) %all-gather.9.cloned.1.call-update) | async-done | bytes 3538960 | tf_op jit(solution)/shard_map/all_gather | solution.py:864
  169.5 13.0 %collective-permute-done.19.refs_6_ = bf16[3,576,384]{2,1,0:T(8,128)(2,1)} collective-permute-done((bf16[3,576,384]{2,1,0:T(8,128)(2,1)}, bf16[3,576,384]{2,1,0:T(8,128)(2,1)}, u32[]{:S(2)}, u32[]{:S(2)}) %collective-permute-start.19) | collective-permute-done | bytes 1327136 | tf_op jit(solution)/shard_map/ppermute | solution.py:606
  192.7 7.5 scatter_custom_fusion.3.g_ref
  209.9 20.9 %shard_map.183 = (bf16[512,1536]{1,0:T(8,128)(2,1)}, bf16[512,1536]{1,0:T(8,128)(2,1)}, f32[4,2,512]{2,1,0:T(2,128)S(1)}) custom-call(f32[512,1536]{1,0:T(8,128)} %fusion.78.q_ref, f32[512,384]{1,0:T(8,128)S(1)} %copy-done.15, f32[512,384]{1,0:T(8,128)S(1)} %copy-done.17, f32[512,384]{1,0:T(8,128)S(1)} %copy-done.19, bf16[1536,384]{1,0:T(8,128)(2,1)S(1)} %copy.124.pairs_ref, ...), custom_call_target="tpu_custom_call" | custom-call | flops 100000000 | bytes 100000 | tf_op jit(solution)/shard_map/pallas_call | solution.py:189
  242.8 28.4 %shard_map.185 = (f32[512,1536]{1,0:T(8,128)}, f32[512,1536]{1,0:T(8,128)}, bf16[1536,1152]{1,0:T(8,128)(2,1)}, bf16[1536,1152]{1,0:T(8,128)(2,1)}, bf16[4,576,3...) custom-call(s32[8]{0:T(128)} %stack.133.facts_ref, ...), custom_call_target="tpu_custom_call" | custom-call | flops 100000000 | bytes 100000 | tf_op jit(solution)/shard_map/pallas_call | solution.py:559
  282.7 28.8 %shard_map.186 = (f32[512,1536]{1,0:T(8,128)}, f32[512,1536]{1,0:T(8,128)}, bf16[1536,1152]{1,0:T(8,128)(2,1)}, bf16[1536,1152]{1,0:T(8,128)(2,1)}, bf16[4,576,3...) custom-call(s32[8]{0:T(128)} %stack.134.facts_ref, ...), custom_call_target="tpu_custom_call", output_to_operand_aliasing={{0}: (7, {}), {1}: (16, {}), {4}: (17, {}), {5}: (18, {}), ... | custom-call | flops 100000000 | bytes 100000 | tf_op jit(solution)/shard_map/pallas_call | solution.py:559
  313.9 28.6 %shard_map.187 = (f32[512,1536]{1,0:T(8,128)}, f32[512,1536]{1,0:T(8,128)}, bf16[1536,1152]{1,0:T(8,128)(2,1)}, bf16[1536,1152]{1,0:T(8,128)(2,1)}, bf16[4,576,3...) custom-call(s32[8]{0:T(128)} %stack.135.facts_ref, ...), custom_call_target="tpu_custom_call", output_to_operand_aliasing={{0}: (7, {}), {1}: (16, {}), {4}: (17, {}), {5}: (18, {}), ... | custom-call | flops 100000000 | bytes 100000 | tf_op jit(solution)/shard_map/pallas_call | solution.py:559
  350.5 29.0 %shard_map.188 = (f32[512,1536]{1,0:T(8,128)}, f32[512,1536]{1,0:T(8,128)}, bf16[1536,1152]{1,0:T(8,128)(2,1)}, bf16[1536,1152]{1,0:T(8,128)(2,1)}, bf16[4,576,3...) custom-call(s32[8]{0:T(128)} %stack.136.facts_ref, ...), custom_call_target="tpu_custom_call", output_to_operand_aliasing={{0}: (7, {}), {1}: (16, {}), {4}: (17, {}), {5}: (18, {}), ... | custom-call | flops 100000000 | bytes 100000 | tf_op jit(solution)/shard_map/pallas_call | solution.py:559
  420.8 20.7 %collective-permute-done.39 = bf16[1536,1152]{1,0:T(8,128)(2,1)} collective-permute-done((bf16[1536,1152]{1,0:T(8,128)(2,1)}, bf16[1536,1152]{1,0:T(8,128)(2,1)}, u32[]{:S(2)}, u32[]{:S(2)}) %collective-permute-start.39) | collective-permute-done | bytes 3538976 | tf_op jit(solution)/shard_map/ppermute | solution.py:606
  443.6 7.7 %add_convert_fusion = bf16[1536,1152]{1,0:T(8,128)(2,1)} fusion(bf16[1536,1152]{1,0:T(8,128)(2,1)} %collective-permute-done.39, bf16[1536,1152]{1,0:T(8,128)(2,1)} %collective-permute-done.37, bf16[1536,1152]{1,0:T(8,128)(2,1)} %collective-permute-done.34, bf16[1536,1152]{1,0:T(8,128)(2,1)S(1)} %copy-done.50), kind=kLoop, calls=%fused_computation.11 | loop fusion | flops 14155776 | bytes 17694720 | tf_op jit(solution)/shard_map/convert_element_type | solution.py:74
  456.3 25.9 %shard_map.194 = (bf16[512,1536]{1,0:T(8,128)(2,1)}, f32[1536,384]{1,0:T(8,128)}) custom-call(bf16[512,1536]{1,0:T(8,128)(2,1)} %get-tuple-element.394.q_ref, bf16[512,1536]{1,0:T(8,128)(2,1)} %convolution_convert_fusion.2.do_ref, f32[4,2,512]{2,1,0:T(2,128)S(1)} %get-tuple-element.401.total_ref, f32[512,384]{1,0:T(8,128)S(1)} %copy-done.16, ...), custom_call_target="tpu_custom_call" | custom-call | flops 100000000 | bytes 100000 | tf_op jit(solution)/shard_map/pallas_call | solution.py:261
  503.3 8.7 %collective-permute-done.49 = bf16[384,1152]{1,0:T(8,128)(2,1)} collective-permute-done((bf16[384,1152]{1,0:T(8,128)(2,1)}, bf16[384,1152]{1,0:T(8,128)(2,1)}, u32[]{:S(2)}, u32[]{:S(2)}) %collective-permute-start.49) | collective-permute-done | bytes 884768 | tf_op jit(solution)/shard_map/ppermute | solution.py:606
  556.8 16.5 %collective-permute-done.51 = bf16[384,1152]{1,0:T(8,128)(2,1)} collective-permute-done((bf16[384,1152]{1,0:T(8,128)(2,1)}, bf16[384,1152]{1,0:T(8,128)(2,1)}, u32[]{:S(2)}, u32[]{:S(2)}) %collective-permute-start.51) | collective-permute-done | bytes 884768 | tf_op jit(solution)/shard_map/ppermute | solution.py:609
  573.3 9.6 %collective-permute-done.50 = bf16[2304,384]{1,0:T(8,128)(2,1)} collective-permute-done((bf16[2304,384]{1,0:T(8,128)(2,1)}, bf16[2304,384]{1,0:T(8,128)(2,1)}, u32[]{:S(2)}, u32[]{:S(2)}) %collective-permute-start.50) | collective-permute-done | bytes 1769504 | tf_op jit(solution)/shard_map/ppermute | solution.py:606
  598.3 6.8 gather_fusion.3
  620.1 24.1 %collective-permute-done.64 = bf16[192,1536]{1,0:T(8,128)(2,1)S(1)} collective-permute-done((bf16[192,1536]{1,0:T(8,128)(2,1)S(1)}, bf16[192,1536]{1,0:T(8,128)(2,1)S(1)}, u32[]{:S(2)}, u32[]{:S(2)}) %collective-permute-start.64) | collective-permute-done | bytes 589856 | tf_op jit(solution)/shard_map/ppermute | solution.py:606
  646.6 16.6 %collective-permute-done.65.refs_1_ = bf16[384,1152]{1,0:T(8,128)(2,1)S(1)} collective-permute-done((bf16[384,1152]{1,0:T(8,128)(2,1)S(1)}, bf16[384,1152]{1,0:T(8,128)(2,1)S(1)}, u32[]{:S(2)}, u32[]{:S(2)}) %collective-permute-start.65) | collective-permute-done | bytes 884768 | tf_op jit(solution)/shard_map/ppermute | solution.py:606
  663.2 18.3 %collective-permute-done.66.refs_2_ = bf16[384,1152]{1,0:T(8,128)(2,1)S(1)} collective-permute-done((bf16[384,1152]{1,0:T(8,128)(2,1)S(1)}, bf16[384,1152]{1,0:T(8,128)(2,1)S(1)}, u32[]{:S(2)}, u32[]{:S(2)}) %collective-permute-start.66) | collective-permute-done | bytes 884768 | tf_op jit(solution)/shard_map/ppermute | solution.py:609
  686.7 6.7 gather_fusion.4
  693.4 13.9 %collective-permute-done.69.refs_3_ = bf16[384,1152]{1,0:T(8,128)(2,1)} collective-permute-done((bf16[384,1152]{1,0:T(8,128)(2,1)S(1)}, bf16[384,1152]{1,0:T(8,128)(2,1)}, u32[]{:S(2)}, u32[]{:S(2)}) %collective-permute-start.69) | collective-permute-done | bytes 884768 | tf_op jit(solution)/shard_map/ppermute | solution.py:609
  714.2 8.7 %shard_map.195 = f32[384,9216]{1,0:T(8,128)} custom-call(s32[8]{0:T(128)S(1)} %stack.137.positions_ref, bf16[384,1152]{1,0:T(8,128)(2,1)S(1)} %add_convert_fusion.9.refs_0_, bf16[384,1152]{1,0:T(8,128)(2,1)S(1)} %collective-permute-done.65.refs_1_, bf16[384,1152]{1,0:T(8,128)(2,1)S(1)} %collective-permute-done.66.refs_2_, ...), custom_call_target="tpu_custom_call" | custom-call | tf_op jit(solution)/shard_map/pallas_call | solution.py:374
  (535 shorter events, 364.5 us)
Async XLA Ops:
  7.2 110.1 %all-gather.7.cloned.1.call-start = ((), (), s32[]{:S(2)}) async-start(), calls=%async_computation.14 | async-start | bytes 2211840 | tf_op jit(solution)/shard_map/all_gather | solution.py:858
  34.2 56.1 %all-to-all-start = ((bf16[8,128,1664]{2,1,0:T(8,128)(2,1)}), bf16[8,128,1664]{2,1,0:T(8,128)(2,1)}, u32[]{:S(2)}, u32[]{:S(2)}) async-start(bf16[8,128,1664]{2,1,0:T(8,128)(2,1)} %bitcast.199), calls=%async_computation | async-start | bytes 6815744 | tf_op jit(solution)/shard_map/all_to_all | solution.py:652
  38.7 120.0 %all-gather.9.cloned.1.call-start = ((), (), s32[]{:S(2)}) async-start(), calls=%async_computation.15 | async-start | bytes 4423680 | tf_op jit(solution)/shard_map/all_gather | solution.py:864
  43.7 46.5 %collective-permute-start.3 = (bf16[3,48,1920]{2,1,0:T(8,128)(2,1)S(1)}, bf16[3,48,1920]{2,1,0:T(8,128)(2,1)S(1)}, u32[]{:S(2)}, u32[]{:S(2)}) collective-permute-start(bf16[3,48,1920]{2,1,0:T(8,128)(2,1)S(1)} %slice.123.refs_0_), channel_id=1, source_target_pairs={{0,8},{4,20},{8,0},{12,28},{16,24},{20,4},{24,16},{28,12},{1,9},{5... | collective-permute-start | bytes 1658888 | tf_op jit(solution)/shard_map/ppermute | solution.py:606
  45.6 44.6 %collective-permute-start.4 = (bf16[3,48,1920]{2,1,0:T(8,128)(2,1)S(1)}, bf16[3,48,1920]{2,1,0:T(8,128)(2,1)S(1)}, u32[]{:S(2)}, u32[]{:S(2)}) collective-permute-start(bf16[3,48,1920]{2,1,0:T(8,128)(2,1)S(1)} %slice.123.refs_0_), channel_id=1, source_target_pairs={{0,16},{4,12},{8,24},{12,4},{16,0},{20,28},{24,8},{28,20},{1,17},{... | collective-permute-start | bytes 1658888 | tf_op jit(solution)/shard_map/ppermute | solution.py:609
  112.6 80.1 %all-to-all-start.1 = ((bf16[8,128,1536]{2,1,0:T(8,128)(2,1)}), bf16[8,128,1536]{2,1,0:T(8,128)(2,1)}, u32[]{:S(2)}, u32[]{:S(2)}) async-start(bf16[8,128,1536]{2,1,0:T(8,128)(2,1)} %bitcast.200), calls=%async_computation.1 | async-start | bytes 6291456 | tf_op jit(solution)/shard_map/all_to_all | solution.py:652
  117.1 113.8 %all-gather.11.cloned.1.call-start = ((), (), s32[]{:S(2)}) async-start(), calls=%async_computation.16 | async-start | bytes 2211840 | tf_op jit(solution)/shard_map/all_gather | solution.py:858
  120.7 61.9 %collective-permute-start.19 = (bf16[3,576,384]{2,1,0:T(8,128)(2,1)}, bf16[3,576,384]{2,1,0:T(8,128)(2,1)}, u32[]{:S(2)}, u32[]{:S(2)}) collective-permute-start(bf16[3,576,384]{2,1,0:T(8,128)(2,1)} %shard_map.179.refs_5_), channel_id=1, source_target_pairs={{0,8},{4,20},{8,0},{12,28},{16,24},{20,4},{24,16},{28,12},{1,9},{5... | collective-permute-start | bytes 3981320 | tf_op jit(solution)/shard_map/ppermute | solution.py:606
  122.5 60.0 %collective-permute-start.20 = (bf16[3,576,384]{2,1,0:T(8,128)(2,1)}, bf16[3,576,384]{2,1,0:T(8,128)(2,1)}, u32[]{:S(2)}, u32[]{:S(2)}) collective-permute-start(bf16[3,576,384]{2,1,0:T(8,128)(2,1)} %shard_map.179.refs_5_), channel_id=1, source_target_pairs={{0,16},{4,12},{8,24},{12,4},{16,0},{20,28},{24,8},{28,20},{1,17},{... | collective-permute-start | bytes 3981320 | tf_op jit(solution)/shard_map/ppermute | solution.py:609
  124.0 58.5 %collective-permute-start.21 = (bf16[3,576,384]{2,1,0:T(8,128)(2,1)}, bf16[3,576,384]{2,1,0:T(8,128)(2,1)}, u32[]{:S(2)}, u32[]{:S(2)}) collective-permute-start(bf16[3,576,384]{2,1,0:T(8,128)(2,1)} %shard_map.179.refs_5_), channel_id=1, source_target_pairs={{0,4},{4,0},{8,12},{12,8},{16,20},{20,16},{24,28},{28,24},{1,5},{5... | collective-permute-start | bytes 3981320 | tf_op jit(solution)/shard_map/ppermute | solution.py:619
  160.5 322.9 %reduce-scatter.6.cloned.1.call-start = ((), (), s32[]{:S(2)}) async-start(), calls=%async_computation.9 | async-start | bytes 4423680 | tf_op jit(solution)/shard_map/reduce_scatter | solution.py:622
  203.2 68.0 %collective-permute-start.27 = (bf16[1152,1152]{1,0:T(8,128)(2,1)}, bf16[1152,1152]{1,0:T(8,128)(2,1)}, u32[]{:S(2)}, u32[]{:S(2)}) collective-permute-start(bf16[1152,1152]{1,0:T(8,128)(2,1)} %bitcast.204), channel_id=1, source_target_pairs={{0,8},{4,20},{8,0},{12,28},{16,24},{20,4},{24,16},{28,12},{1,9},{5... | collective-permute-start | bytes 7962632 | tf_op jit(solution)/shard_map/ppermute | solution.py:606
  203.8 67.4 %collective-permute-start.28 = (bf16[1152,1152]{1,0:T(8,128)(2,1)}, bf16[1152,1152]{1,0:T(8,128)(2,1)}, u32[]{:S(2)}, u32[]{:S(2)}) collective-permute-start(bf16[1152,1152]{1,0:T(8,128)(2,1)} %bitcast.205), channel_id=1, source_target_pairs={{0,16},{4,12},{8,24},{12,4},{16,0},{20,28},{24,8},{28,20},{1,17},{... | collective-permute-start | bytes 7962632 | tf_op jit(solution)/shard_map/ppermute | solution.py:609
  399.7 210.6 %reduce-scatter.8.cloned.1.call-start = ((), (), s32[]{:S(2)}) async-start(), calls=%async_computation.10 | async-start | bytes 4423680 | tf_op jit(solution)/shard_map/reduce_scatter | solution.py:622
  512.0 70.8 %all-to-all-start.2 = ((bf16[8,128,1536]{2,1,0:T(8,128)(2,1)}), bf16[8,128,1536]{2,1,0:T(8,128)(2,1)}, u32[]{:S(2)}, u32[]{:S(2)}) async-start(bf16[8,128,1536]{2,1,0:T(8,128)(2,1)} %bitcast.201), calls=%async_computation.3 | async-start | bytes 6291456 | tf_op jit(solution)/shard_map/all_to_all | solution.py:652
  524.4 58.5 %collective-permute-start.50 = (bf16[2304,384]{1,0:T(8,128)(2,1)}, bf16[2304,384]{1,0:T(8,128)(2,1)}, u32[]{:S(2)}, u32[]{:S(2)}) collective-permute-start(bf16[2304,384]{1,0:T(8,128)(2,1)} %add_convert_fusion.4), channel_id=1, source_target_pairs={{0,8},{4,20},{8,0},{12,28},{16,24},{20,4},{24,16},{28,12},{1,9},{5... | collective-permute-start | bytes 5308424 | tf_op jit(solution)/shard_map/ppermute | solution.py:606
  526.6 46.7 %collective-permute-start.51 = (bf16[384,1152]{1,0:T(8,128)(2,1)}, bf16[384,1152]{1,0:T(8,128)(2,1)}, u32[]{:S(2)}, u32[]{:S(2)}) collective-permute-start(bf16[384,1152]{1,0:T(8,128)(2,1)} %collective-permute-done.49), channel_id=1, source_target_pairs={{0,16},{4,12},{8,24},{12,4},{16,0},{20,28},{24,8},{28,20},{1,17},{... | collective-permute-start | bytes 2654216 | tf_op jit(solution)/shard_map/ppermute | solution.py:609
  589.6 91.9 %all-to-all-start.3 = ((bf16[8,128,1536]{2,1,0:T(8,128)(2,1)}), bf16[8,128,1536]{2,1,0:T(8,128)(2,1)}, u32[]{:S(2)}, u32[]{:S(2)}) async-start(bf16[8,128,1536]{2,1,0:T(8,128)(2,1)} %bitcast.202), calls=%async_computation.5 | async-start | bytes 6291456 | tf_op jit(solution)/shard_map/all_to_all | solution.py:652
  594.1 99.3 %reduce-scatter.10.cloned.1.call-start = ((), (), s32[]{:S(2)}) async-start(), calls=%async_computation.11 | async-start | bytes 2211840 | tf_op jit(solution)/shard_map/reduce_scatter | solution.py:622
  598.3 124.6 %reduce-scatter.12.cloned.1.call-start = ((), (), s32[]{:S(2)}) async-start(), calls=%async_computation.12 | async-start | bytes 737280 | tf_op jit(solution)/shard_map/reduce_scatter | solution.py:622
  615.4 66.1 %collective-permute-start.62 = (bf16[256,1920]{1,0:T(8,128)(2,1)}, bf16[256,1920]{1,0:T(8,128)(2,1)}, u32[]{:S(2)}, u32[]{:S(2)}) collective-permute-start(bf16[256,1920]{1,0:T(8,128)(2,1)} %add_convert_fusion.8), channel_id=1, source_target_pairs={{0,16},{4,12},{8,24},{12,4},{16,0},{20,28},{24,8},{28,20},{1,17},{... | collective-permute-start | bytes 2949128 | tf_op jit(solution)/shard_map/ppermute | solution.py:609
  616.5 65.0 %collective-permute-start.63 = (bf16[256,1920]{1,0:T(8,128)(2,1)}, bf16[256,1920]{1,0:T(8,128)(2,1)}, u32[]{:S(2)}, u32[]{:S(2)}) collective-permute-start(bf16[256,1920]{1,0:T(8,128)(2,1)} %add_convert_fusion.7), channel_id=1, source_target_pairs={{0,16},{4,12},{8,24},{12,4},{16,0},{20,28},{24,8},{28,20},{1,17},{... | collective-permute-start | bytes 2949128 | tf_op jit(solution)/shard_map/ppermute | solution.py:609
  619.0 62.5 %collective-permute-start.66 = (bf16[384,1152]{1,0:T(8,128)(2,1)S(1)}, bf16[384,1152]{1,0:T(8,128)(2,1)S(1)}, u32[]{:S(2)}, u32[]{:S(2)}) collective-permute-start(bf16[384,1152]{1,0:T(8,128)(2,1)S(1)} %add_convert_fusion.9.refs_0_), channel_id=1, source_target_pairs={{0,16},{4,12},{8,24},{12,4},{16,0},{20,28},{24,8},{28,20},{1,17},{... | collective-permute-start | bytes 2654216 | tf_op jit(solution)/shard_map/ppermute | solution.py:609
  686.7 52.0 %reduce-scatter.14.cloned.1.call-start = ((), (), s32[]{:S(2)}) async-start(), calls=%async_computation.13 | async-start | bytes 1228800 | tf_op jit(solution)/shard_map/reduce_scatter | solution.py:622
  (173 other events, 2382.4 us)
Sparse Core Ops, SparseCore 0:
  34.3 53.3 all-gather.6
  89.8 68.7 all-gather.8
  160.8 38.9 all-gather.10
  399.8 66.8 reduce-scatter.5
  468.8 66.6 reduce-scatter.7
  598.4 39.1 reduce-scatter.9
  686.8 21.9 reduce-scatter.11
  711.8 24.7 reduce-scatter.13
